TPU v7x, 512 devices: a whole 4x4x16 slice. The times are simulated.
512 devices in a mesh: outer: 16 (over z_lo, x), inner: 32 (over y, z_hi, core).
Axes of the slice: x: 4, y: 4, z: 16 (z_hi: 4, z_lo: 4; z = z_hi * 4 + z_lo), core: 2. Of those that a mesh axis runs over, the one named last changes fastest.
Arguments:
- image_proj: bfloat16 [65536, 1024], P(('outer', 'inner')), may hold values from -10 to 10
- report_proj: bfloat16 [65536, 1024], P(('outer', 'inner')), may hold values from -10 to 10
- report_feats: bfloat16 [65536, 4096], P(('outer', 'inner')), may hold values from -24 to 24
- pair_index: int32 [65536], P(('outer', 'inner')), may hold values from 0 to 65535, as said below
- natural_log_factor: float32 [1], replicated, may hold values from 1 to 2.3
- logit_bias: float32 [1], replicated, may hold values from -4 to -1
Outputs:
- picture_embedding_grad: bfloat16 [65536, 1024], P(('outer', 'inner'))
- caption_embedding_grad: bfloat16 [65536, 1024], P(('outer', 'inner'))
- head_grad: float32 [4096, 1024], P(('outer', 'inner'))
Inputs may be any that keep to these rules, and one draw needn't show every extreme that they name: Within each block of 128 rows, pair_index is a permutation of that block's own global row indices.
All inputs are finite; a program needn't handle non-finite values.
Results may differ from a plain program's by a relative error of at most 0.0058.
Values may be sent and summed in bfloat16 or wider, within the bound.
No kernel may reach another device: no remote copies, remote signals or barrier semaphores. Data moves between devices by JAX's collectives and lax.ppermute only.
A program may use at most 64 MiB of HBM per device.

v0:
```python
import jax
import jax.numpy as jnp
from jax import lax
from jax.sharding import PartitionSpec as P

STEPS = 8


EPSILON = 1e-06


def shifted(value, axis, steps):
    count = lax.axis_size(axis)
    pairs = [(source, (source + steps) % count) for source in range(count)]
    return lax.ppermute(value, axis, pairs)


def unit_rows(values):
    wide = values.astype(jnp.float32)
    length = jnp.sqrt(jnp.sum(wide * wide, axis=-1, keepdims=True) + EPSILON)
    return (wide / length, length)


def euclid_norm_derivative(grad_unit, unit, length):
    return (grad_unit - unit * jnp.sum(unit * grad_unit, axis=-1, keepdims=True)) / length


def contract_rows(first_tile_entries, second_tile_entries):
    return lax.dot_general(
        first_tile_entries,
        second_tile_entries,
        (((0,), (0,)), ((), ())),
        preferred_element_type=jnp.float32,
    )


def pairwise_slope_values(
    first_tile_entries, second_tile_entries, sharpness_factor, cyclic_offset, matching_indicator
):
    similarity_scores = (
        sharpness_factor
        * lax.dot_general(
            first_tile_entries,
            second_tile_entries,
            (((1,), (1,)), ((), ())),
            preferred_element_type=jnp.float32,
        )
        + cyclic_offset
    )
    if matching_indicator is None:
        slope = jax.nn.sigmoid(similarity_scores)
    else:
        target = jnp.where(matching_indicator, 1.0, -1.0).astype(jnp.float32)
        slope = -target * jax.nn.sigmoid(-target * similarity_scores)
    return slope.astype(jnp.bfloat16)


def on_device(image_proj, report_proj, report_feats, pair_index, natural_log_factor, logit_bias):
    picture_directions, picture_norms = unit_rows(image_proj)
    caption_directions, caption_norms = unit_rows(report_proj)
    slide_lower_index = picture_directions.astype(jnp.bfloat16)
    report_low = caption_directions.astype(jnp.bfloat16)
    sharpness_factor = jnp.exp(natural_log_factor[0])
    cyclic_offset = logit_bias[0]
    count = image_proj.shape[0]
    width = image_proj.shape[1]
    columns = lax.broadcasted_iota(jnp.int32, (count, count), 1)
    matching_indicator = columns == (pair_index % count)[:, None]
    empty = jnp.zeros((count, width), jnp.float32)
    rotating_rows = report_low
    partial_value = empty
    picture_energy = empty
    for rotation_step in range(STEPS):
        slopes = pairwise_slope_values(
            slide_lower_index,
            rotating_rows,
            sharpness_factor,
            cyclic_offset,
            matching_indicator if rotation_step == 0 else None,
        )
        picture_energy = picture_energy + jnp.dot(
            slopes, rotating_rows, preferred_element_type=jnp.float32
        )
        partial_value = partial_value + contract_rows(slopes, slide_lower_index)
        if rotation_step < STEPS - 1:
            rotating_rows = shifted(rotating_rows, ("outer", "inner"), 1)
            partial_value = shifted(partial_value, ("outer", "inner"), 1)
    caption_energy = shifted(partial_value, ("outer", "inner"), -(STEPS - 1))
    picture_embedding_grad = euclid_norm_derivative(
        sharpness_factor * picture_energy, picture_directions, picture_norms
    ).astype(jnp.bfloat16)
    caption_embedding_grad = euclid_norm_derivative(
        sharpness_factor * caption_energy, caption_directions, caption_norms
    ).astype(jnp.bfloat16)
    feats_width = report_feats.shape[1]
    outer_count = lax.axis_size("outer")
    inner_count = lax.axis_size("inner")
    narrow = feats_width // (outer_count * inner_count)
    ordered = report_feats.reshape(count, outer_count, inner_count, narrow)
    ordered = ordered.transpose(0, 2, 1, 3).reshape(count, feats_width)
    column_rows = lax.all_to_all(ordered, "inner", split_axis=1, concat_axis=0, tiled=True)
    weight_part = contract_rows(
        column_rows, lax.all_gather(caption_embedding_grad, "inner", axis=0, tiled=True)
    )
    head_grad = lax.psum_scatter(weight_part, "outer", scatter_dimension=0, tiled=True)
    return (picture_embedding_grad, caption_embedding_grad, head_grad)


def solution(mesh):
    placed = (
        P(("outer", "inner"), None),
        P(("outer", "inner"), None),
        P(("outer", "inner"), None),
        P(("outer", "inner")),
        P(),
        P(),
    )
    return jax.shard_map(
        on_device,
        mesh=mesh,
        in_specs=placed,
        out_specs=(
            P(("outer", "inner"), None),
            P(("outer", "inner"), None),
            P(("outer", "inner"), None),
        ),
        check_vma=False,
    )
```

profile of v0, /device:TPU:8, one launch (start us, length us, event | category | flops | bytes accessed | tf_op | source)
XLA Modules:
  0.0 603.8 jit_solution(804877244910292549)
XLA Ops:
  8.5 0.7 and_select_fusion
  9.2 1.1 fusion.51
  10.3 1.1 fusion.52
  11.4 1.1 fusion.54
  12.5 1.1 fusion.55
  14.1 1.9 collective-permute-start.7
  16.0 9.2 %collective-permute-start = (bf16[128,1024]{1,0:T(8,128)(2,1)S(1)}, bf16[128,1024]{1,0:T(8,128)(2,1)S(1)}, u32[]{:S(2)}, u32[]{:S(2)}) collective-permute-start(bf16[128,1024]{1,0:T(8,128)(2,1)S(1)} %fusion.55), channel_id=1, source_target_pairs={{0,1},{1,2},{2,3},{3,4},{4,5},{5,6},{6,7},{7,8},{8,9},{9,10},{10,1... | collective-permute-start | bytes 786440 | tf_op jit(solution)/shard_map/ppermute | solution.py:15
  25.2 15.5 %collective-permute-done = bf16[128,1024]{1,0:T(8,128)(2,1)S(1)} collective-permute-done((bf16[128,1024]{1,0:T(8,128)(2,1)S(1)}, bf16[128,1024]{1,0:T(8,128)(2,1)S(1)}, u32[]{:S(2)}, u32[]{:S(2)}) %collective-permute-start) | collective-permute-done | bytes 262176 | tf_op jit(solution)/shard_map/ppermute | solution.py:15
  40.7 1.9 collective-permute-start.1
  43.2 6.4 %collective-permute-start.8 = (f32[128,1024]{1,0:T(8,128)S(1)}, f32[128,1024]{1,0:T(8,128)S(1)}, u32[]{:S(2)}, u32[]{:S(2)}) collective-permute-start(f32[128,1024]{1,0:T(8,128)S(1)} %convolution_add_fusion), channel_id=1, source_target_pairs={{0,1},{1,2},{2,3},{3,4},{4,5},{5,6},{6,7},{7,8},{8,9},{9,10},{10,1... | collective-permute-start | bytes 1572872 | tf_op jit(solution)/shard_map/ppermute | solution.py:15
  49.6 18.8 %collective-permute-done.1 = bf16[128,1024]{1,0:T(8,128)(2,1)S(1)} collective-permute-done((bf16[128,1024]{1,0:T(8,128)(2,1)S(1)}, bf16[128,1024]{1,0:T(8,128)(2,1)S(1)}, u32[]{:S(2)}, u32[]{:S(2)}) %collective-permute-start.1) | collective-permute-done | bytes 262176 | tf_op jit(solution)/shard_map/ppermute | solution.py:15
  68.4 2.7 collective-permute-start.2
  71.6 48.5 %collective-permute-done.8 = f32[128,1024]{1,0:T(8,128)S(1)} collective-permute-done((f32[128,1024]{1,0:T(8,128)S(1)}, f32[128,1024]{1,0:T(8,128)S(1)}, u32[]{:S(2)}, u32[]{:S(2)}) %collective-permute-start.8) | collective-permute-done | bytes 524320 | tf_op jit(solution)/shard_map/ppermute | solution.py:15
  120.2 1.9 collective-permute-start.9
  122.2 6.1 %collective-permute-done.2 = bf16[128,1024]{1,0:T(8,128)(2,1)S(1)} collective-permute-done((bf16[128,1024]{1,0:T(8,128)(2,1)S(1)}, bf16[128,1024]{1,0:T(8,128)(2,1)S(1)}, u32[]{:S(2)}, u32[]{:S(2)}) %collective-permute-start.2) | collective-permute-done | bytes 262176 | tf_op jit(solution)/shard_map/ppermute | solution.py:15
  128.3 3.4 collective-permute-start.3
  132.2 25.9 %collective-permute-done.9 = f32[128,1024]{1,0:T(8,128)S(1)} collective-permute-done((f32[128,1024]{1,0:T(8,128)S(1)}, f32[128,1024]{1,0:T(8,128)S(1)}, u32[]{:S(2)}, u32[]{:S(2)}) %collective-permute-start.9) | collective-permute-done | bytes 524320 | tf_op jit(solution)/shard_map/ppermute | solution.py:15
  158.2 1.9 collective-permute-start.10
  160.2 16.0 %collective-permute-done.3 = bf16[128,1024]{1,0:T(8,128)(2,1)S(1)} collective-permute-done((bf16[128,1024]{1,0:T(8,128)(2,1)S(1)}, bf16[128,1024]{1,0:T(8,128)(2,1)S(1)}, u32[]{:S(2)}, u32[]{:S(2)}) %collective-permute-start.3) | collective-permute-done | bytes 262176 | tf_op jit(solution)/shard_map/ppermute | solution.py:15
  176.2 1.9 collective-permute-start.4
  178.6 18.6 %collective-permute-done.10 = f32[128,1024]{1,0:T(8,128)S(1)} collective-permute-done((f32[128,1024]{1,0:T(8,128)S(1)}, f32[128,1024]{1,0:T(8,128)S(1)}, u32[]{:S(2)}, u32[]{:S(2)}) %collective-permute-start.10) | collective-permute-done | bytes 524320 | tf_op jit(solution)/shard_map/ppermute | solution.py:15
  197.3 1.9 collective-permute-start.11
  199.2 7.5 %collective-permute-done.4 = bf16[128,1024]{1,0:T(8,128)(2,1)S(1)} collective-permute-done((bf16[128,1024]{1,0:T(8,128)(2,1)S(1)}, bf16[128,1024]{1,0:T(8,128)(2,1)S(1)}, u32[]{:S(2)}, u32[]{:S(2)}) %collective-permute-start.4) | collective-permute-done | bytes 262176 | tf_op jit(solution)/shard_map/ppermute | solution.py:15
  206.7 1.9 collective-permute-start.5
  209.1 0.4 copy-done.7
  209.5 11.9 %collective-permute-done.11 = f32[128,1024]{1,0:T(8,128)S(1)} collective-permute-done((f32[128,1024]{1,0:T(8,128)S(1)}, f32[128,1024]{1,0:T(8,128)S(1)}, u32[]{:S(2)}, u32[]{:S(2)}) %collective-permute-start.11) | collective-permute-done | bytes 524320 | tf_op jit(solution)/shard_map/ppermute | solution.py:15
  221.5 1.9 collective-permute-start.12
  223.4 7.0 %collective-permute-done.5 = bf16[128,1024]{1,0:T(8,128)(2,1)S(1)} collective-permute-done((bf16[128,1024]{1,0:T(8,128)(2,1)S(1)}, bf16[128,1024]{1,0:T(8,128)(2,1)S(1)}, u32[]{:S(2)}, u32[]{:S(2)}) %collective-permute-start.5) | collective-permute-done | bytes 262176 | tf_op jit(solution)/shard_map/ppermute | solution.py:15
  230.4 1.9 collective-permute-start.6
  233.2 18.7 %collective-permute-done.12 = f32[128,1024]{1,0:T(8,128)S(1)} collective-permute-done((f32[128,1024]{1,0:T(8,128)S(1)}, f32[128,1024]{1,0:T(8,128)S(1)}, u32[]{:S(2)}, u32[]{:S(2)}) %collective-permute-start.12) | collective-permute-done | bytes 524320 | tf_op jit(solution)/shard_map/ppermute | solution.py:15
  251.9 3.0 collective-permute-start.13
  255.0 7.8 %collective-permute-done.6 = bf16[128,1024]{1,0:T(8,128)(2,1)S(1)} collective-permute-done((bf16[128,1024]{1,0:T(8,128)(2,1)S(1)}, bf16[128,1024]{1,0:T(8,128)(2,1)S(1)}, u32[]{:S(2)}, u32[]{:S(2)}) %collective-permute-start.6) | collective-permute-done | bytes 262176 | tf_op jit(solution)/shard_map/ppermute | solution.py:15
  263.6 6.8 %collective-permute-done.13 = f32[128,1024]{1,0:T(8,128)S(1)} collective-permute-done((f32[128,1024]{1,0:T(8,128)S(1)}, f32[128,1024]{1,0:T(8,128)S(1)}, u32[]{:S(2)}, u32[]{:S(2)}) %collective-permute-start.13) | collective-permute-done | bytes 524320 | tf_op jit(solution)/shard_map/ppermute | solution.py:15
  270.4 1.9 collective-permute-start.14
  272.4 29.4 %collective-permute-done.14 = f32[128,1024]{1,0:T(8,128)S(1)} collective-permute-done((f32[128,1024]{1,0:T(8,128)S(1)}, f32[128,1024]{1,0:T(8,128)S(1)}, u32[]{:S(2)}, u32[]{:S(2)}) %collective-permute-start.14) | collective-permute-done | bytes 524320 | tf_op jit(solution)/shard_map/ppermute | solution.py:15
  302.1 0.9 divide_convert_fusion
  303.0 0.7 copy.14
  303.7 1.3 copy.21
  305.0 13.1 %all-to-all-start = ((bf16[128,32,128]{0,2,1:T(8,128)(2,1)}), bf16[128,32,128]{0,2,1:T(8,128)(2,1)S(1)}, u32[]{:S(2)}, u32[]{:S(2)}) async-start(bf16[128,32,128]{0,2,1:T(8,128)(2,1)} %bitcast.62), calls=%async_computation | async-start | bytes 2097152 | tf_op jit(solution)/shard_map/all_to_all | solution.py:101
  318.4 1.0 convolution_add_fusion.7
  319.8 39.1 %all-to-all-done = bf16[128,32,128]{0,2,1:T(8,128)(2,1)S(1)} async-done(((bf16[128,32,128]{0,2,1:T(8,128)(2,1)}), bf16[128,32,128]{0,2,1:T(8,128)(2,1)S(1)}, u32[]{:S(2)}, u32[]{:S(2)}) %all-to-all-start) | async-done | bytes 1048608 | tf_op jit(solution)/shard_map/all_to_all | solution.py:101
  359.0 0.7 copy.16
  359.6 145.5 %all-gather.2.cloned.1.call-done = bf16[4096,1024]{1,0:T(8,128)(2,1)} async-done(((bf16[128,1024]{1,0:T(8,128)(2,1)}), bf16[4096,1024]{1,0:T(8,128)(2,1)}) %all-gather.2.cloned.1.call-update) | async-done | bytes 8388624 | tf_op jit(solution)/shard_map/all_gather | solution.py:103
  505.1 5.7 convolution_bitcast_fusion
  510.8 1.0 copy.18
  512.6 1.3 multiply_reduce_fusion.1
  513.9 0.9 divide_convert_fusion.1
  514.8 82.2 %reduce-scatter.4.cloned.1.call-done = f32[8,1024]{1,0:T(8,128)} async-done(((f32[128,1024]{1,0:T(8,128)}), f32[8,1024]{1,0:T(8,128)}) %reduce-scatter.4.cloned.1.call-update) | async-done | bytes 32784
  (65 shorter events, 6.7 us)
Async XLA Ops:
  7.2 497.9 %all-gather.2.cloned.1.call-start = ((), (), s32[]{:S(2)}) async-start(), calls=%async_computation.2 | async-start | bytes 8650752 | tf_op jit(solution)/shard_map/all_gather | solution.py:103
  14.1 28.8 %collective-permute-start.7 = (f32[128,1024]{1,0:T(8,128)S(1)}, f32[128,1024]{1,0:T(8,128)S(1)}, u32[]{:S(2)}, u32[]{:S(2)}) collective-permute-start(f32[128,1024]{1,0:T(8,128)S(1)} %fusion.57), channel_id=1, source_target_pairs={{0,1},{1,2},{2,3},{3,4},{4,5},{5,6},{6,7},{7,8},{8,9},{9,10},{10,1... | collective-permute-start | bytes 1572872 | tf_op jit(solution)/shard_map/ppermute | solution.py:15
  16.0 24.7 %collective-permute-start = (bf16[128,1024]{1,0:T(8,128)(2,1)S(1)}, bf16[128,1024]{1,0:T(8,128)(2,1)S(1)}, u32[]{:S(2)}, u32[]{:S(2)}) collective-permute-start(bf16[128,1024]{1,0:T(8,128)(2,1)S(1)} %fusion.55), channel_id=1, source_target_pairs={{0,1},{1,2},{2,3},{3,4},{4,5},{5,6},{6,7},{7,8},{8,9},{9,10},{10,1... | collective-permute-start | bytes 786440 | tf_op jit(solution)/shard_map/ppermute | solution.py:15
  40.7 27.7 %collective-permute-start.1 = (bf16[128,1024]{1,0:T(8,128)(2,1)S(1)}, bf16[128,1024]{1,0:T(8,128)(2,1)S(1)}, u32[]{:S(2)}, u32[]{:S(2)}) collective-permute-start(bf16[128,1024]{1,0:T(8,128)(2,1)S(1)} %collective-permute-done), channel_id=1, source_target_pairs={{0,1},{1,2},{2,3},{3,4},{4,5},{5,6},{6,7},{7,8},{8,9},{9,10},{10,1... | collective-permute-start | bytes 786440 | tf_op jit(solution)/shard_map/ppermute | solution.py:15
  42.9 79.3 %copy-start.11 = (bf16[128,128]{1,0:T(8,128)(2,1)}, bf16[128,128]{1,0:T(8,128)(2,1)S(1)}, u32[]{:S(2)}) copy-start(bf16[128,128]{1,0:T(8,128)(2,1)S(1)} %fusion.49) | copy-start | bytes 98308
  43.2 77.0 %collective-permute-start.8 = (f32[128,1024]{1,0:T(8,128)S(1)}, f32[128,1024]{1,0:T(8,128)S(1)}, u32[]{:S(2)}, u32[]{:S(2)}) collective-permute-start(f32[128,1024]{1,0:T(8,128)S(1)} %convolution_add_fusion), channel_id=1, source_target_pairs={{0,1},{1,2},{2,3},{3,4},{4,5},{5,6},{6,7},{7,8},{8,9},{9,10},{10,1... | collective-permute-start | bytes 1572872 | tf_op jit(solution)/shard_map/ppermute | solution.py:15
  68.4 59.9 %collective-permute-start.2 = (bf16[128,1024]{1,0:T(8,128)(2,1)S(1)}, bf16[128,1024]{1,0:T(8,128)(2,1)S(1)}, u32[]{:S(2)}, u32[]{:S(2)}) collective-permute-start(bf16[128,1024]{1,0:T(8,128)(2,1)S(1)} %collective-permute-done.1), channel_id=1, source_target_pairs={{0,1},{1,2},{2,3},{3,4},{4,5},{5,6},{6,7},{7,8},{8,9},{9,10},{10,1... | collective-permute-start | bytes 786440 | tf_op jit(solution)/shard_map/ppermute | solution.py:15
  71.6 230.2 %copy-start = (bf16[128,1024]{1,0:T(8,128)(2,1)S(1)}, bf16[128,1024]{1,0:T(8,128)(2,1)}, u32[]{:S(2)}) copy-start(bf16[128,1024]{1,0:T(8,128)(2,1)} %param.7) | copy-start | bytes 786436
  120.2 37.9 %collective-permute-start.9 = (f32[128,1024]{1,0:T(8,128)S(1)}, f32[128,1024]{1,0:T(8,128)S(1)}, u32[]{:S(2)}, u32[]{:S(2)}) collective-permute-start(f32[128,1024]{1,0:T(8,128)S(1)} %add.152), channel_id=1, source_target_pairs={{0,1},{1,2},{2,3},{3,4},{4,5},{5,6},{6,7},{7,8},{8,9},{9,10},{10,1... | collective-permute-start | bytes 1572872 | tf_op jit(solution)/shard_map/ppermute | solution.py:15
  128.3 47.9 %collective-permute-start.3 = (bf16[128,1024]{1,0:T(8,128)(2,1)S(1)}, bf16[128,1024]{1,0:T(8,128)(2,1)S(1)}, u32[]{:S(2)}, u32[]{:S(2)}) collective-permute-start(bf16[128,1024]{1,0:T(8,128)(2,1)S(1)} %collective-permute-done.2), channel_id=1, source_target_pairs={{0,1},{1,2},{2,3},{3,4},{4,5},{5,6},{6,7},{7,8},{8,9},{9,10},{10,1... | collective-permute-start | bytes 786440 | tf_op jit(solution)/shard_map/ppermute | solution.py:15
  132.0 171.0 %copy-start.2 = (bf16[128,4096]{1,0:T(8,128)(2,1)S(1)}, bf16[128,4096]{1,0:T(8,128)(2,1)}, u32[]{:S(2)}) copy-start(bf16[128,4096]{1,0:T(8,128)(2,1)} %param.8) | copy-start | bytes 3145732
  158.2 39.0 %collective-permute-start.10 = (f32[128,1024]{1,0:T(8,128)S(1)}, f32[128,1024]{1,0:T(8,128)S(1)}, u32[]{:S(2)}, u32[]{:S(2)}) collective-permute-start(f32[128,1024]{1,0:T(8,128)S(1)} %add.153), channel_id=1, source_target_pairs={{0,1},{1,2},{2,3},{3,4},{4,5},{5,6},{6,7},{7,8},{8,9},{9,10},{10,1... | collective-permute-start | bytes 1572872 | tf_op jit(solution)/shard_map/ppermute | solution.py:15
  176.2 30.5 %collective-permute-start.4 = (bf16[128,1024]{1,0:T(8,128)(2,1)S(1)}, bf16[128,1024]{1,0:T(8,128)(2,1)S(1)}, u32[]{:S(2)}, u32[]{:S(2)}) collective-permute-start(bf16[128,1024]{1,0:T(8,128)(2,1)S(1)} %collective-permute-done.3), channel_id=1, source_target_pairs={{0,1},{1,2},{2,3},{3,4},{4,5},{5,6},{6,7},{7,8},{8,9},{9,10},{10,1... | collective-permute-start | bytes 786440 | tf_op jit(solution)/shard_map/ppermute | solution.py:15
  197.3 24.1 %collective-permute-start.11 = (f32[128,1024]{1,0:T(8,128)S(1)}, f32[128,1024]{1,0:T(8,128)S(1)}, u32[]{:S(2)}, u32[]{:S(2)}) collective-permute-start(f32[128,1024]{1,0:T(8,128)S(1)} %add.154), channel_id=1, source_target_pairs={{0,1},{1,2},{2,3},{3,4},{4,5},{5,6},{6,7},{7,8},{8,9},{9,10},{10,1... | collective-permute-start | bytes 1572872 | tf_op jit(solution)/shard_map/ppermute | solution.py:15
  206.7 95.1 %copy-start.3 = (bf16[128,1024]{1,0:T(8,128)(2,1)}, bf16[128,1024]{1,0:T(8,128)(2,1)S(1)}, u32[]{:S(2)}) copy-start(bf16[128,1024]{1,0:T(8,128)(2,1)S(1)} %collective-permute-done.4) | copy-start | bytes 786436
  206.7 23.7 %collective-permute-start.5 = (bf16[128,1024]{1,0:T(8,128)(2,1)S(1)}, bf16[128,1024]{1,0:T(8,128)(2,1)S(1)}, u32[]{:S(2)}, u32[]{:S(2)}) collective-permute-start(bf16[128,1024]{1,0:T(8,128)(2,1)S(1)} %collective-permute-done.4), channel_id=1, source_target_pairs={{0,1},{1,2},{2,3},{3,4},{4,5},{5,6},{6,7},{7,8},{8,9},{9,10},{10,1... | collective-permute-start | bytes 786440 | tf_op jit(solution)/shard_map/ppermute | solution.py:15
  208.9 0.6 copy-start.7
  221.5 30.4 %collective-permute-start.12 = (f32[128,1024]{1,0:T(8,128)S(1)}, f32[128,1024]{1,0:T(8,128)S(1)}, u32[]{:S(2)}, u32[]{:S(2)}) collective-permute-start(f32[128,1024]{1,0:T(8,128)S(1)} %add.155), channel_id=1, source_target_pairs={{0,1},{1,2},{2,3},{3,4},{4,5},{5,6},{6,7},{7,8},{8,9},{9,10},{10,1... | collective-permute-start | bytes 1572872 | tf_op jit(solution)/shard_map/ppermute | solution.py:15
  230.4 71.6 %copy-start.5 = (bf16[128,1024]{1,0:T(8,128)(2,1)}, bf16[128,1024]{1,0:T(8,128)(2,1)S(1)}, u32[]{:S(2)}) copy-start(bf16[128,1024]{1,0:T(8,128)(2,1)S(1)} %collective-permute-done.5) | copy-start | bytes 786436
  230.4 32.3 %collective-permute-start.6 = (bf16[128,1024]{1,0:T(8,128)(2,1)S(1)}, bf16[128,1024]{1,0:T(8,128)(2,1)S(1)}, u32[]{:S(2)}, u32[]{:S(2)}) collective-permute-start(bf16[128,1024]{1,0:T(8,128)(2,1)S(1)} %collective-permute-done.5), channel_id=1, source_target_pairs={{0,1},{1,2},{2,3},{3,4},{4,5},{5,6},{6,7},{7,8},{8,9},{9,10},{10,1... | collective-permute-start | bytes 786440 | tf_op jit(solution)/shard_map/ppermute | solution.py:15
  232.6 0.6 copy-start.9
  251.9 18.4 %collective-permute-start.13 = (f32[128,1024]{1,0:T(8,128)S(1)}, f32[128,1024]{1,0:T(8,128)S(1)}, u32[]{:S(2)}, u32[]{:S(2)}) collective-permute-start(f32[128,1024]{1,0:T(8,128)S(1)} %add.156), channel_id=1, source_target_pairs={{0,1},{1,2},{2,3},{3,4},{4,5},{5,6},{6,7},{7,8},{8,9},{9,10},{10,1... | collective-permute-start | bytes 1572872 | tf_op jit(solution)/shard_map/ppermute | solution.py:15
  262.7 39.3 %copy-start.14 = (bf16[128,1024]{1,0:T(8,128)(2,1)}, bf16[128,1024]{1,0:T(8,128)(2,1)S(1)}, u32[]{:S(2)}) copy-start(bf16[128,1024]{1,0:T(8,128)(2,1)S(1)} %collective-permute-done.6) | copy-start | bytes 786436
  263.0 0.6 copy-start.12
  270.4 31.4 %collective-permute-start.14 = (f32[128,1024]{1,0:T(8,128)S(1)}, f32[128,1024]{1,0:T(8,128)S(1)}, u32[]{:S(2)}, u32[]{:S(2)}) collective-permute-start(f32[128,1024]{1,0:T(8,128)S(1)} %add.157), channel_id=1, source_target_pairs={{0,505},{1,506},{2,507},{3,508},{4,509},{5,510},{6,511},{7,0},{8,1... | collective-permute-start | bytes 1572872 | tf_op jit(solution)/shard_map/ppermute | solution.py:15
  305.0 54.0 %all-to-all-start = ((bf16[128,32,128]{0,2,1:T(8,128)(2,1)}), bf16[128,32,128]{0,2,1:T(8,128)(2,1)S(1)}, u32[]{:S(2)}, u32[]{:S(2)}) async-start(bf16[128,32,128]{0,2,1:T(8,128)(2,1)} %bitcast.62), calls=%async_computation | async-start | bytes 2097152 | tf_op jit(solution)/shard_map/all_to_all | solution.py:101
  318.1 278.9 %reduce-scatter.4.cloned.1.call-start = ((), (), s32[]{:S(2)}) async-start(), calls=%async_computation.3 | async-start | bytes 557056
  319.6 192.5 %copy-start.4 = (bf16[128,1024]{1,0:T(8,128)(2,1)S(1)}, bf16[128,1024]{1,0:T(8,128)(2,1)}, u32[]{:S(2)}) copy-start(bf16[128,1024]{1,0:T(8,128)(2,1)} %copy-done.3) | copy-start | bytes 786436
  319.6 192.5 %copy-start.8 = (bf16[128,128]{1,0:T(8,128)(2,1)S(1)}, bf16[128,128]{1,0:T(8,128)(2,1)}, u32[]{:S(2)}) copy-start(bf16[128,128]{1,0:T(8,128)(2,1)} %copy-done.7) | copy-start | bytes 98308
  319.8 192.5 %copy-start.6 = (bf16[128,1024]{1,0:T(8,128)(2,1)S(1)}, bf16[128,1024]{1,0:T(8,128)(2,1)}, u32[]{:S(2)}) copy-start(bf16[128,1024]{1,0:T(8,128)(2,1)} %copy-done.5) | copy-start | bytes 786436
  319.8 192.5 %copy-start.10 = (bf16[128,128]{1,0:T(8,128)(2,1)S(1)}, bf16[128,128]{1,0:T(8,128)(2,1)}, u32[]{:S(2)}) copy-start(bf16[128,128]{1,0:T(8,128)(2,1)} %copy-done.9) | copy-start | bytes 98308
  359.6 153.0 %copy-start.1 = (bf16[128,1024]{1,0:T(8,128)(2,1)S(1)}, bf16[128,1024]{1,0:T(8,128)(2,1)}, u32[]{:S(2)}) copy-start(bf16[128,1024]{1,0:T(8,128)(2,1)} %param.6) | copy-start | bytes 786436
  359.6 153.0 %copy-start.13 = (bf16[128,128]{1,0:T(8,128)(2,1)S(1)}, bf16[128,128]{1,0:T(8,128)(2,1)}, u32[]{:S(2)}) copy-start(bf16[128,128]{1,0:T(8,128)(2,1)} %copy-done.12) | copy-start | bytes 98308
Sparse Core Ops, SparseCore 0:
  303.1 201.9 all-gather.1
  512.0 84.9 reduce-scatter.3
where the time goes:
time: 605 us; the launch traced here: 604 us
  waiting for transfers between devices  505 us (83%)
  starting transfers between devices  57 us (9%)
  between operations  15.9 us (3%)
  matrix products  13.2 us (2%)
  other arithmetic  7.36 us (1%)
    ppermute x15, waiting for transfers between devices, shifted(): return lax.ppermute(value, axis, pairs)  239 us
    all_gather x1, waiting for transfers between devices, on_device(): lax.all_gather(caption_embedding_grad, 'inner', axis=0, tiled=True)  145 us
    unnamed x3, waiting for transfers between devices  82.2 us
    ppermute x15, starting transfers between devices, shifted(): return lax.ppermute(value, axis, pairs)  43.9 us
    all_to_all x1, waiting for transfers between devices, on_device(): lax.all_to_all(ordered, 'inner', split_axis=1, concat_axis=0, tiled=True)  39.1 us
    all_to_all x1, starting transfers between devices, on_device(): lax.all_to_all(ordered, 'inner', split_axis=1, concat_axis=0, tiled=True)  13.1 us
  transfers between devices with their start and end apart: 18, of which 17 were waited for; matrix products, arithmetic and copies ran while one was open for 2% of the time, Pallas kernels for 0%

commit v1 on v0

v1 whole, which is shorter than its diff:
```python
import jax
import jax.numpy as jnp
from jax import lax
from jax.experimental import pallas as pl
from jax.experimental.pallas import tpu as pltpu
from jax.sharding import Mesh, PartitionSpec as P

EPSILON = 1e-06
ROWS = 128
WIDTH = 1024
BLOCKS = 512
AXES = ("zl", "x", "y", "zh", "c")
LIMIT = 40 * 1024 * 1024


def moved(value, target_of):
    return lax.ppermute(value, AXES, [(r, target_of(r) % BLOCKS) for r in range(BLOCKS)])


def moved_by(value, steps):
    return moved(value, lambda r: r + steps)


def swapped(value):
    return lax.ppermute(value, "c", [(0, 1), (1, 0)])


def after(value, *others):
    return lax.optimization_barrier((value, *others))[0]


def low_rows(wide):
    inverse = 1.0 / jnp.sqrt(jnp.sum(wide * wide, axis=-1, keepdims=True) + EPSILON)
    return (wide * inverse).astype(jnp.bfloat16)


def window_gradient(scalars, match, own, others, low):
    sharpness = scalars[0]
    offset = scalars[1]
    start = 0
    for ref in others:
        rows = ref.shape[0]
        low[start : start + rows, :] = low_rows(ref[...].astype(jnp.float32))
        start += rows
    wide = own[...].astype(jnp.float32)
    length = jnp.sqrt(jnp.sum(wide * wide, axis=-1, keepdims=True) + EPSILON)
    unit = wide / length
    logits = sharpness * lax.dot_general(
        unit.astype(jnp.bfloat16),
        low[...],
        (((1,), (1,)), ((), ())),
        preferred_element_type=jnp.float32,
    ) + offset
    first = logits[:, :ROWS]
    target = jnp.where(match, 1.0, -1.0)
    first_slope = -target * jax.nn.sigmoid(-target * first)
    slope = jnp.concatenate([first_slope, jax.nn.sigmoid(logits[:, ROWS:])], axis=1)
    total = sharpness * jnp.dot(
        slope.astype(jnp.bfloat16), low[...], preferred_element_type=jnp.float32
    )
    return (total - unit * jnp.sum(unit * total, axis=-1, keepdims=True)) / length


def caption_kernel(scalars, pair_row, own, *refs):
    *others, out, spread, low = refs
    rows = lax.broadcasted_iota(jnp.int32, (ROWS, ROWS), 0)
    match = rows == lax.rem(pair_row[...], ROWS)
    grad = window_gradient(scalars, match, own, others, low).astype(jnp.bfloat16)
    out[...] = grad
    for x in range(4):
        for y in range(4):
            spread[x, y] = grad[:, y * 256 : (y + 1) * 256]


def picture_kernel(scalars, pair_column, own, *refs):
    *others, out, low = refs
    columns = lax.broadcasted_iota(jnp.int32, (ROWS, ROWS), 1)
    match = columns == lax.rem(pair_column[...], ROWS)
    out[...] = window_gradient(scalars, match, own, others, low).astype(jnp.bfloat16)


def window_call(body, outs, *args):
    return pl.pallas_call(
        body,
        out_shape=outs,
        in_specs=[pl.BlockSpec(memory_space=pltpu.SMEM)]
        + [pl.BlockSpec(memory_space=pltpu.VMEM)] * (len(args) - 1),
        out_specs=jax.tree.map(lambda _: pl.BlockSpec(memory_space=pltpu.VMEM), outs),
        scratch_shapes=[pltpu.VMEM((8 * ROWS, WIDTH), jnp.bfloat16)],
        compiler_params=pltpu.CompilerParams(vmem_limit_bytes=LIMIT),
        cost_estimate=pl.CostEstimate(
            flops=4 * ROWS * 8 * ROWS * WIDTH, bytes_accessed=4_000_000, transcendentals=ROWS * 1024
        ),
    )(*args)


def head_kernel(place, caps, f0, f1, f2, f3, keep, give, table):
    y = place[0]
    c = place[1]
    total = None
    for step, feats in enumerate((f0, f1, f2, f3)):
        source = lax.rem(y + 4 - step, 4)
        rows = jnp.concatenate([caps[x, source] for x in range(4)], axis=0)
        part = lax.dot_general(
            rows, feats[...], (((0,), (0,)), ((), ())), preferred_element_type=jnp.float32
        )
        total = part if total is None else total + part
    table[...] = total.T
    for zl in range(4):
        for zh in range(4):
            for yy in range(4):
                base = zl * 256 + yy * 64 + zh * 16
                to = (zl * 16 + zh * 4 + yy) * 8
                keep[to : to + 8, :] = table[pl.ds(pl.multiple_of(base + c * 8, 8), 8), :]
                give[to : to + 8, :] = table[pl.ds(pl.multiple_of(base + 8 - c * 8, 8), 8), :]


def head_call(place, caps, feats):
    vmem = pl.BlockSpec(memory_space=pltpu.VMEM)
    half = jax.ShapeDtypeStruct((512, 256), jnp.float32)
    return pl.pallas_call(
        head_kernel,
        out_shape=(half, half),
        in_specs=[pl.BlockSpec(memory_space=pltpu.SMEM)] + [vmem] * 5,
        out_specs=(vmem, vmem),
        scratch_shapes=[pltpu.VMEM((1024, 256), jnp.float32)],
        compiler_params=pltpu.CompilerParams(vmem_limit_bytes=LIMIT),
        cost_estimate=pl.CostEstimate(
            flops=2 * 2048 * 1024 * 256, bytes_accessed=6_000_000, transcendentals=0
        ),
    )(place, caps, *feats)


def on_device(image_proj, report_proj, report_feats, pair_index, natural_log_factor, logit_bias):
    scalars = jnp.concatenate([jnp.exp(natural_log_factor), logit_bias])
    place = jnp.stack([lax.axis_index("y"), lax.axis_index("c")]).astype(jnp.int32)

    image_beside = moved(image_proj, lambda r: r - 1 if r % 2 else r - 7)
    image_1 = moved_by(image_proj, -2)
    image_3 = moved_by(image_proj, -6)

    ordered = report_feats.reshape(ROWS, 4, 4, 256).transpose(2, 0, 1, 3).reshape(512, 1024)
    columns = lax.all_to_all(ordered, "x", split_axis=0, concat_axis=0, tiled=True)
    feats = [columns] + [
        lax.ppermute(columns, "y", [(i, (i + k) % 4) for i in range(4)]) for k in (1, 2, 3)
    ]

    image_2a = moved_by(image_1[:64], -2)
    image_2b = moved_by(image_3[64:], 2)
    images = (image_proj, image_beside, image_1, swapped(image_1), image_3, swapped(image_3))
    images += (image_2a, image_2b, swapped(image_2a), swapped(image_2b))
    caption_grad, caption_spread = window_call(
        caption_kernel,
        (
            jax.ShapeDtypeStruct((ROWS, WIDTH), jnp.bfloat16),
            jax.ShapeDtypeStruct((4, 4, ROWS, 256), jnp.bfloat16),
        ),
        scalars,
        pair_index.reshape(1, ROWS),
        report_proj,
        *images,
    )

    report_late = after(report_proj, image_2a, image_2b)
    report_beside = moved(report_late, lambda r: r + 7 if r % 2 else r + 1)
    report_1 = moved_by(report_late, 2)
    report_3 = moved_by(report_late, 6)
    report_2a = moved_by(report_1[:64], 2)
    report_2b = moved_by(report_3[64:], -2)
    reports = (report_proj, report_beside, report_1, swapped(report_1), report_3, swapped(report_3))
    reports += (report_2a, report_2b, swapped(report_2a), swapped(report_2b))
    picture_grad = window_call(
        picture_kernel,
        jax.ShapeDtypeStruct((ROWS, WIDTH), jnp.bfloat16),
        scalars,
        pair_index.reshape(ROWS, 1),
        image_proj,
        *reports,
    )

    caps = lax.all_to_all(
        caption_spread.reshape(16 * ROWS, 256), ("x", "y"), split_axis=0, concat_axis=0, tiled=True
    ).reshape(4, 4, ROWS, 256)
    keep, give = head_call(place, caps, feats)
    part = (keep + swapped(give)).astype(jnp.bfloat16)
    parts = lax.all_to_all(part, ("zl", "zh", "y"), split_axis=0, concat_axis=0, tiled=True)
    head = jnp.sum(parts.reshape(16, 4, 8, 256).astype(jnp.float32), axis=0)
    head_grad = head.transpose(1, 0, 2).reshape(8, WIDTH)
    return (picture_grad, caption_grad, head_grad)


def solution(mesh):
    fine = Mesh(mesh.devices.reshape(4, 4, 4, 4, 2), AXES)
    rows = P(AXES, None)
    return jax.shard_map(
        on_device,
        mesh=fine,
        in_specs=(rows, rows, rows, P(AXES), P(), P()),
        out_specs=(rows, rows, rows),
        check_vma=False,
    )
```

time: 605 us -> 241 us (0.40)
  the two profiles are of different devices: /device:TPU:8 before, /device:TPU:65 now
where the time goes in v1:
time: 241 us; the launch traced here: 240 us
  starting transfers between devices  132 us (55%)
  waiting for transfers between devices  88.7 us (37%)
  Pallas kernels  9.46 us (4%)
  local copies, waits for them, and re-layouts  5.58 us (2%)
    ppermute x10, starting transfers between devices, moved(): lax.ppermute(value, AXES, [(r, target_of(r) % BLOCKS) for r in range(BLOC...  72 us
    all_to_all x1, waiting for transfers between devices, on_device(): lax.all_to_all(caption_spread.reshape(16 * ROWS, 256), ('x', 'y'), split_...  44.7 us
    ppermute x10, waiting for transfers between devices, moved(): lax.ppermute(value, AXES, [(r, target_of(r) % BLOCKS) for r in range(BLOC...  41.6 us
    ppermute x9, starting transfers between devices, swapped(): return lax.ppermute(value, 'c', [(0, 1), (1, 0)])  30.8 us
    all_to_all x1, starting transfers between devices, on_device(): lax.all_to_all(part, ('zl', 'zh', 'y'), split_axis=0, concat_axis=0, tile...  9.19 us
    ppermute x3, starting transfers between devices, on_device(): lax.ppermute(columns, 'y', [(i, (i + k) % 4) for i in range(4)])  8.43 us
    all_to_all x1, starting transfers between devices, on_device(): lax.all_to_all(caption_spread.reshape(16 * ROWS, 256), ('x', 'y'), split_...  7.93 us
    pallas_call x2, Pallas kernels, window_call(): pl.pallas_call(body, out_shape=outs, in_specs=[pl.BlockSpec(memory_space=...  6.07 us
  transfers between devices with their start and end apart: 25, of which 7 were waited for; matrix products, arithmetic and copies ran while one was open for 0% of the time, Pallas kernels for 3%

profile of v1, /device:TPU:65, one launch (start us, length us, event | category | flops | bytes accessed | tf_op | source)
XLA Modules:
  0.0 240.0 jit_solution(14491974060307807915)
XLA Ops:
  0.6 1.9 reshape.39
  2.5 0.4 copy.10
  2.9 1.6 all_to_all.21
  4.5 4.1 %all-to-all-start.1 = ((bf16[4,128,1024]{2,1,0:T(8,128)(2,1)}), bf16[4,128,1024]{2,1,0:T(8,128)(2,1)S(1)}, u32[]{:S(2)}, u32[]{:S(2)}) async-start(bf16[4,128,1024]{2,1,0:T(8,128)(2,1)} %all_to_all.21), calls=%async_computation.1 | async-start | bytes 2097152 | tf_op jit(solution)/shard_map/all_to_all | solution.py:143
  8.6 12.4 %collective-permute-start.2 = (bf16[128,1024]{1,0:T(8,128)(2,1)S(1)}, bf16[128,1024]{1,0:T(8,128)(2,1)S(1)}, u32[]{:S(2)}, u32[]{:S(2)}) collective-permute-start(bf16[128,1024]{1,0:T(8,128)(2,1)S(1)} %copy-done), channel_id=1, source_target_pairs={{0,506},{1,507},{2,508},{3,509},{4,510},{5,511},{6,0},{7,1},{8,2},... | collective-permute-start | bytes 786440 | tf_op jit(solution)/shard_map/ppermute | solution.py:17
  21.1 5.6 %collective-permute-start = (bf16[128,1024]{1,0:T(8,128)(2,1)S(1)}, bf16[128,1024]{1,0:T(8,128)(2,1)S(1)}, u32[]{:S(2)}, u32[]{:S(2)}) collective-permute-start(bf16[128,1024]{1,0:T(8,128)(2,1)S(1)} %copy-done), channel_id=1, source_target_pairs={{0,510},{1,511},{2,0},{3,1},{4,2},{5,3},{6,4},{7,5},{8,6},{9,7},{1... | collective-permute-start | bytes 786440 | tf_op jit(solution)/shard_map/ppermute | solution.py:17
  26.6 3.4 %collective-permute-start.13 = (bf16[128,1024]{1,0:T(8,128)(2,1)S(1)}, bf16[128,1024]{1,0:T(8,128)(2,1)S(1)}, u32[]{:S(2)}, u32[]{:S(2)}) collective-permute-start(bf16[128,1024]{1,0:T(8,128)(2,1)S(1)} %copy-done), channel_id=1, source_target_pairs={{0,505},{1,0},{2,507},{3,2},{4,509},{5,4},{6,511},{7,6},{8,1},{9,8... | collective-permute-start | bytes 786440 | tf_op jit(solution)/shard_map/ppermute | solution.py:17
  30.1 8.5 %collective-permute-done.2.refs_4_ = bf16[128,1024]{1,0:T(8,128)(2,1)S(1)} collective-permute-done((bf16[128,1024]{1,0:T(8,128)(2,1)S(1)}, bf16[128,1024]{1,0:T(8,128)(2,1)S(1)}, u32[]{:S(2)}, u32[]{:S(2)}) %collective-permute-start.2) | collective-permute-done | bytes 262176 | tf_op jit(solution)/shard_map/ppermute | solution.py:17
  38.6 6.8 %collective-permute-start.3 = (bf16[64,1024]{1,0:T(8,128)(2,1)S(1)}, bf16[64,1024]{1,0:T(8,128)(2,1)S(1)}, u32[]{:S(2)}, u32[]{:S(2)}) collective-permute-start(bf16[64,1024]{1,0:T(8,128)(2,1)S(1)} %slice.17), channel_id=1, source_target_pairs={{0,2},{1,3},{2,4},{3,5},{4,6},{5,7},{6,8},{7,9},{8,10},{9,11},{10,... | collective-permute-start | bytes 393224 | tf_op jit(solution)/shard_map/ppermute | solution.py:17
  45.4 2.7 %collective-permute-start.15 = (bf16[128,1024]{1,0:T(8,128)(2,1)S(1)}, bf16[128,1024]{1,0:T(8,128)(2,1)S(1)}, u32[]{:S(2)}, u32[]{:S(2)}) collective-permute-start(bf16[128,1024]{1,0:T(8,128)(2,1)S(1)} %collective-permute-done.2.refs_4_), channel_id=1, source_target_pairs={{0,1},{1,0},{2,3},{3,2},{4,5},{5,4},{6,7},{7,6},{8,9},{9,8},{10,11... | collective-permute-start | bytes 786440 | tf_op jit(solution)/shard_map/ppermute | solution.py:25
  48.2 16.2 %collective-permute-start.1 = (bf16[64,1024]{1,0:T(8,128)(2,1)S(1)}, bf16[64,1024]{1,0:T(8,128)(2,1)S(1)}, u32[]{:S(2)}, u32[]{:S(2)}) collective-permute-start(bf16[64,1024]{1,0:T(8,128)(2,1)S(1)} %slice.16), channel_id=1, source_target_pairs={{0,510},{1,511},{2,0},{3,1},{4,2},{5,3},{6,4},{7,5},{8,6},{9,7},{1... | collective-permute-start | bytes 393224 | tf_op jit(solution)/shard_map/ppermute | solution.py:17
  64.4 2.2 collective-permute-start.14
  66.7 2.2 collective-permute-start.17
  68.9 3.0 %collective-permute-done.1.refs_6_ = bf16[64,1024]{1,0:T(8,128)(2,1)S(1)} collective-permute-done((bf16[64,1024]{1,0:T(8,128)(2,1)S(1)}, bf16[64,1024]{1,0:T(8,128)(2,1)S(1)}, u32[]{:S(2)}, u32[]{:S(2)}) %collective-permute-start.1) | collective-permute-done | bytes 131104 | tf_op jit(solution)/shard_map/ppermute | solution.py:17
  71.9 2.4 collective-permute-start.16
  75.6 0.0 collective-permute-done.13.refs_1_
  75.6 0.0 all-to-all-done.1
  75.7 4.0 %collective-permute-start.20 = (bf16[512,1024]{1,0:T(8,128)(2,1)S(1)}, bf16[512,1024]{1,0:T(8,128)(2,1)}, u32[]{:S(2)}, u32[]{:S(2)}) collective-permute-start(bf16[512,1024]{1,0:T(8,128)(2,1)S(1)} %bitcast.15), channel_id=1, source_target_pairs={{0,24},{8,0},{16,8},{24,16},{1,25},{9,1},{17,9},{25,17},{2,26},{10... | collective-permute-start | bytes 3145736 | tf_op jit(solution)/shard_map/ppermute | solution.py:145
  79.7 1.9 collective-permute-start.19
  81.6 2.5 %collective-permute-start.18 = (bf16[512,1024]{1,0:T(8,128)(2,1)S(1)}, bf16[512,1024]{1,0:T(8,128)(2,1)}, u32[]{:S(2)}, u32[]{:S(2)}) collective-permute-start(bf16[512,1024]{1,0:T(8,128)(2,1)S(1)} %bitcast.17), channel_id=1, source_target_pairs={{0,8},{8,16},{16,24},{24,0},{1,9},{9,17},{17,25},{25,1},{2,10},{10... | collective-permute-start | bytes 3145736 | tf_op jit(solution)/shard_map/ppermute | solution.py:145
  84.1 0.1 pad_maximum_fusion.scalars
  84.2 0.6 copy-done.3
  84.9 3.1 %shard_map.86 = (bf16[128,1024]{1,0:T(8,128)(2,1)}, bf16[4,4,128,256]{3,2,1,0:T(8,128)(2,1)S(1)}) custom-call(f32[2]{0:T(128)S(1)} %pad_maximum_fusion.scalars, s32[1,128]{1,0:T(1,128)S(1)} %bitcast.21, bf16[128,1024]{1,0:T(8,128)(2,1)S(1)} %copy-done.1, bf16[128,1024]{1,0:T(8,128)(2,1)S(1)} %copy-done, ...), custom_call_target="tpu_custom_call" | custom-call | flops 536870912 | bytes 4000000 | tf_op jit(solution)/shard_map/pallas_call | solution.py:83
  87.9 1.0 copy-done.2
  88.9 7.9 %all-to-all-start = ((bf16[16,128,256]{2,1,0:T(8,128)(2,1)}), bf16[16,128,256]{2,1,0:T(8,128)(2,1)S(1)}, u32[]{:S(2)}, u32[]{:S(2)}) async-start(bf16[16,128,256]{2,1,0:T(8,128)(2,1)} %bitcast.20), calls=%async_computation | async-start | bytes 2097152 | tf_op jit(solution)/shard_map/all_to_all | solution.py:181
  96.8 0.1 pad_add_fusion.place
  96.9 44.7 %all-to-all-done = bf16[16,128,256]{2,1,0:T(8,128)(2,1)S(1)} async-done(((bf16[16,128,256]{2,1,0:T(8,128)(2,1)}), bf16[16,128,256]{2,1,0:T(8,128)(2,1)S(1)}, u32[]{:S(2)}, u32[]{:S(2)}) %all-to-all-start) | async-done | bytes 1048608 | tf_op jit(solution)/shard_map/all_to_all | solution.py:181
  141.6 0.0 collective-permute-done.20.f3
  141.6 3.4 %shard_map.87 = (f32[512,256]{1,0:T(8,128)S(1)}, f32[512,256]{1,0:T(8,128)S(1)}) custom-call(s32[2]{0:T(128)S(1)} %pad_add_fusion.place, bf16[4,4,128,256]{3,2,1,0:T(8,128)(2,1)S(1)} %bitcast.19, bf16[512,1024]{1,0:T(8,128)(2,1)S(1)} %bitcast.18, bf16[512,1024]{1,0:T(8,128)(2,1)} %collective-permute-done.18.f1, ...), custom_call_target="tpu_custom_call" | custom-call | flops 1073741824 | bytes 6000000 | tf_op jit(solution)/shard_map/pallas_call | solution.py:121
  145.0 3.0 %collective-permute-start.21 = (f32[512,256]{1,0:T(8,128)S(1)}, f32[512,256]{1,0:T(8,128)S(1)}, u32[]{:S(2)}, u32[]{:S(2)}) collective-permute-start(f32[512,256]{1,0:T(8,128)S(1)} %get-tuple-element.12), channel_id=1, source_target_pairs={{0,1},{1,0},{2,3},{3,2},{4,5},{5,4},{6,7},{7,6},{8,9},{9,8},{10,11... | collective-permute-start | bytes 1572872 | tf_op jit(solution)/shard_map/ppermute | solution.py:25
  148.0 1.5 collective-permute-done.21
  149.5 0.8 fusion
  150.2 9.2 %all-to-all-start.2 = ((bf16[64,8,256]{2,1,0:T(8,128)(2,1)}), bf16[64,8,256]{2,1,0:T(8,128)(2,1)S(1)}, u32[]{:S(2)}, u32[]{:S(2)}) async-start(bf16[64,8,256]{2,1,0:T(8,128)(2,1)} %fusion), calls=%async_computation.2 | async-start | bytes 524288 | tf_op jit(solution)/shard_map/all_to_all | solution.py:186
  159.4 5.3 %collective-permute-start.7 = (bf16[128,1024]{1,0:T(8,128)(2,1)S(1)}, bf16[128,1024]{1,0:T(8,128)(2,1)S(1)}, u32[]{:S(2)}, u32[]{:S(2)}) collective-permute-start(bf16[128,1024]{1,0:T(8,128)(2,1)S(1)} %copy-done.1), channel_id=1, source_target_pairs={{0,6},{1,7},{2,8},{3,9},{4,10},{5,11},{6,12},{7,13},{8,14},{9,15},... | collective-permute-start | bytes 786440 | tf_op jit(solution)/shard_map/ppermute | solution.py:17
  164.7 4.8 %collective-permute-start.5 = (bf16[128,1024]{1,0:T(8,128)(2,1)S(1)}, bf16[128,1024]{1,0:T(8,128)(2,1)S(1)}, u32[]{:S(2)}, u32[]{:S(2)}) collective-permute-start(bf16[128,1024]{1,0:T(8,128)(2,1)S(1)} %copy-done.1), channel_id=1, source_target_pairs={{0,2},{1,3},{2,4},{3,5},{4,6},{5,7},{6,8},{7,9},{8,10},{9,11},{10,... | collective-permute-start | bytes 786440 | tf_op jit(solution)/shard_map/ppermute | solution.py:17
  169.5 4.5 %collective-permute-start.4 = (bf16[128,1024]{1,0:T(8,128)(2,1)S(1)}, bf16[128,1024]{1,0:T(8,128)(2,1)S(1)}, u32[]{:S(2)}, u32[]{:S(2)}) collective-permute-start(bf16[128,1024]{1,0:T(8,128)(2,1)S(1)} %copy-done.1), channel_id=1, source_target_pairs={{0,1},{1,8},{2,3},{3,10},{4,5},{5,12},{6,7},{7,14},{8,9},{9,16},{1... | collective-permute-start | bytes 786440 | tf_op jit(solution)/shard_map/ppermute | solution.py:17
  174.0 25.9 %collective-permute-done.7.refs_4_ = bf16[128,1024]{1,0:T(8,128)(2,1)S(1)} collective-permute-done((bf16[128,1024]{1,0:T(8,128)(2,1)S(1)}, bf16[128,1024]{1,0:T(8,128)(2,1)S(1)}, u32[]{:S(2)}, u32[]{:S(2)}) %collective-permute-start.7) | collective-permute-done | bytes 262176 | tf_op jit(solution)/shard_map/ppermute | solution.py:17
  200.0 9.6 %collective-permute-start.10 = (bf16[64,1024]{1,0:T(8,128)(2,1)S(1)}, bf16[64,1024]{1,0:T(8,128)(2,1)S(1)}, u32[]{:S(2)}, u32[]{:S(2)}) collective-permute-start(bf16[64,1024]{1,0:T(8,128)(2,1)S(1)} %slice.19), channel_id=1, source_target_pairs={{0,510},{1,511},{2,0},{3,1},{4,2},{5,3},{6,4},{7,5},{8,6},{9,7},{1... | collective-permute-start | bytes 393224 | tf_op jit(solution)/shard_map/ppermute | solution.py:17
  209.6 3.4 %collective-permute-start.9 = (bf16[64,1024]{1,0:T(8,128)(2,1)S(1)}, bf16[64,1024]{1,0:T(8,128)(2,1)S(1)}, u32[]{:S(2)}, u32[]{:S(2)}) collective-permute-start(bf16[64,1024]{1,0:T(8,128)(2,1)S(1)} %slice.18), channel_id=1, source_target_pairs={{0,2},{1,3},{2,4},{3,5},{4,6},{5,7},{6,8},{7,9},{8,10},{9,11},{10,... | collective-permute-start | bytes 393224 | tf_op jit(solution)/shard_map/ppermute | solution.py:17
  212.9 7.8 %collective-permute-start.8 = (bf16[128,1024]{1,0:T(8,128)(2,1)S(1)}, bf16[128,1024]{1,0:T(8,128)(2,1)S(1)}, u32[]{:S(2)}, u32[]{:S(2)}) collective-permute-start(bf16[128,1024]{1,0:T(8,128)(2,1)S(1)} %collective-permute-done.7.refs_4_), channel_id=1, source_target_pairs={{0,1},{1,0},{2,3},{3,2},{4,5},{5,4},{6,7},{7,6},{8,9},{9,8},{10,11... | collective-permute-start | bytes 786440 | tf_op jit(solution)/shard_map/ppermute | solution.py:25
  220.7 1.9 collective-permute-start.6
  222.7 5.4 %collective-permute-start.12 = (bf16[64,1024]{1,0:T(8,128)(2,1)S(1)}, bf16[64,1024]{1,0:T(8,128)(2,1)S(1)}, u32[]{:S(2)}, u32[]{:S(2)}) collective-permute-start(bf16[64,1024]{1,0:T(8,128)(2,1)S(1)} %collective-permute-done.10.refs_7_), channel_id=1, source_target_pairs={{0,1},{1,0},{2,3},{3,2},{4,5},{5,4},{6,7},{7,6},{8,9},{9,8},{10,11... | collective-permute-start | bytes 393224 | tf_op jit(solution)/shard_map/ppermute | solution.py:25
  228.1 4.2 %collective-permute-done.9.refs_6_ = bf16[64,1024]{1,0:T(8,128)(2,1)S(1)} collective-permute-done((bf16[64,1024]{1,0:T(8,128)(2,1)S(1)}, bf16[64,1024]{1,0:T(8,128)(2,1)S(1)}, u32[]{:S(2)}, u32[]{:S(2)}) %collective-permute-start.9) | collective-permute-done | bytes 131104 | tf_op jit(solution)/shard_map/ppermute | solution.py:17
  232.3 3.1 %collective-permute-start.11 = (bf16[64,1024]{1,0:T(8,128)(2,1)S(1)}, bf16[64,1024]{1,0:T(8,128)(2,1)S(1)}, u32[]{:S(2)}, u32[]{:S(2)}) collective-permute-start(bf16[64,1024]{1,0:T(8,128)(2,1)S(1)} %collective-permute-done.9.refs_6_), channel_id=1, source_target_pairs={{0,1},{1,0},{2,3},{3,2},{4,5},{5,4},{6,7},{7,6},{8,9},{9,8},{10,11... | collective-permute-start | bytes 393224 | tf_op jit(solution)/shard_map/ppermute | solution.py:25
  235.4 0.1 copy.9.pair_column
  235.5 0.8 collective-permute-done.11.refs_8_
  236.4 3.0 %shard_map.85 = bf16[128,1024]{1,0:T(8,128)(2,1)} custom-call(f32[2]{0:T(128)S(1)} %pad_maximum_fusion.scalars, s32[128,1]{1,0:T(8,128)S(1)} %copy.9.pair_column, bf16[128,1024]{1,0:T(8,128)(2,1)S(1)} %copy-done, bf16[128,1024]{1,0:T(8,128)(2,1)S(1)} %copy-done.1, bf16[128,1024]{1,0:T(8,128)(2,1)S(1)} %collective-permute-done.4.refs_1_, ...), custom_call_target="tpu_custom_call" | custom-call | flops 536870912 | bytes 4000000 | tf_op jit(solution)/shard_map/pallas_call | solution.py:83
  239.4 0.7 convert_reduce_fusion
  (25 shorter events, 0.1 us)
Async XLA Ops:
  4.5 4.1 %copy-start = (bf16[128,1024]{1,0:T(8,128)(2,1)S(1)}, bf16[128,1024]{1,0:T(8,128)(2,1)}, u32[]{:S(2)}) copy-start(bf16[128,1024]{1,0:T(8,128)(2,1)} %refs_0_.3) | copy-start | bytes 786436
  4.5 71.2 %all-to-all-start.1 = ((bf16[4,128,1024]{2,1,0:T(8,128)(2,1)}), bf16[4,128,1024]{2,1,0:T(8,128)(2,1)S(1)}, u32[]{:S(2)}, u32[]{:S(2)}) async-start(bf16[4,128,1024]{2,1,0:T(8,128)(2,1)} %all_to_all.21), calls=%async_computation.1 | async-start | bytes 2097152 | tf_op jit(solution)/shard_map/all_to_all | solution.py:143
  8.6 75.6 %copy-start.1 = (bf16[128,1024]{1,0:T(8,128)(2,1)S(1)}, bf16[128,1024]{1,0:T(8,128)(2,1)}, u32[]{:S(2)}) copy-start(bf16[128,1024]{1,0:T(8,128)(2,1)} %own.3) | copy-start | bytes 786436
  8.6 29.9 %collective-permute-start.2 = (bf16[128,1024]{1,0:T(8,128)(2,1)S(1)}, bf16[128,1024]{1,0:T(8,128)(2,1)S(1)}, u32[]{:S(2)}, u32[]{:S(2)}) collective-permute-start(bf16[128,1024]{1,0:T(8,128)(2,1)S(1)} %copy-done), channel_id=1, source_target_pairs={{0,506},{1,507},{2,508},{3,509},{4,510},{5,511},{6,0},{7,1},{8,2},... | collective-permute-start | bytes 786440 | tf_op jit(solution)/shard_map/ppermute | solution.py:17
  21.1 27.1 %collective-permute-start = (bf16[128,1024]{1,0:T(8,128)(2,1)S(1)}, bf16[128,1024]{1,0:T(8,128)(2,1)S(1)}, u32[]{:S(2)}, u32[]{:S(2)}) collective-permute-start(bf16[128,1024]{1,0:T(8,128)(2,1)S(1)} %copy-done), channel_id=1, source_target_pairs={{0,510},{1,511},{2,0},{3,1},{4,2},{5,3},{6,4},{7,5},{8,6},{9,7},{1... | collective-permute-start | bytes 786440 | tf_op jit(solution)/shard_map/ppermute | solution.py:17
  26.6 49.0 %collective-permute-start.13 = (bf16[128,1024]{1,0:T(8,128)(2,1)S(1)}, bf16[128,1024]{1,0:T(8,128)(2,1)S(1)}, u32[]{:S(2)}, u32[]{:S(2)}) collective-permute-start(bf16[128,1024]{1,0:T(8,128)(2,1)S(1)} %copy-done), channel_id=1, source_target_pairs={{0,505},{1,0},{2,507},{3,2},{4,509},{5,4},{6,511},{7,6},{8,1},{9,8... | collective-permute-start | bytes 786440 | tf_op jit(solution)/shard_map/ppermute | solution.py:17
  38.6 28.1 %collective-permute-start.3 = (bf16[64,1024]{1,0:T(8,128)(2,1)S(1)}, bf16[64,1024]{1,0:T(8,128)(2,1)S(1)}, u32[]{:S(2)}, u32[]{:S(2)}) collective-permute-start(bf16[64,1024]{1,0:T(8,128)(2,1)S(1)} %slice.17), channel_id=1, source_target_pairs={{0,2},{1,3},{2,4},{3,5},{4,6},{5,7},{6,8},{7,9},{8,10},{9,11},{10,... | collective-permute-start | bytes 393224 | tf_op jit(solution)/shard_map/ppermute | solution.py:17
  45.4 36.2 %collective-permute-start.15 = (bf16[128,1024]{1,0:T(8,128)(2,1)S(1)}, bf16[128,1024]{1,0:T(8,128)(2,1)S(1)}, u32[]{:S(2)}, u32[]{:S(2)}) collective-permute-start(bf16[128,1024]{1,0:T(8,128)(2,1)S(1)} %collective-permute-done.2.refs_4_), channel_id=1, source_target_pairs={{0,1},{1,0},{2,3},{3,2},{4,5},{5,4},{6,7},{7,6},{8,9},{9,8},{10,11... | collective-permute-start | bytes 786440 | tf_op jit(solution)/shard_map/ppermute | solution.py:25
  48.2 23.7 %collective-permute-start.1 = (bf16[64,1024]{1,0:T(8,128)(2,1)S(1)}, bf16[64,1024]{1,0:T(8,128)(2,1)S(1)}, u32[]{:S(2)}, u32[]{:S(2)}) collective-permute-start(bf16[64,1024]{1,0:T(8,128)(2,1)S(1)} %slice.16), channel_id=1, source_target_pairs={{0,510},{1,511},{2,0},{3,1},{4,2},{5,3},{6,4},{7,5},{8,6},{9,7},{1... | collective-permute-start | bytes 393224 | tf_op jit(solution)/shard_map/ppermute | solution.py:17
  64.4 19.8 %collective-permute-start.14 = (bf16[128,1024]{1,0:T(8,128)(2,1)S(1)}, bf16[128,1024]{1,0:T(8,128)(2,1)S(1)}, u32[]{:S(2)}, u32[]{:S(2)}) collective-permute-start(bf16[128,1024]{1,0:T(8,128)(2,1)S(1)} %collective-permute-done.refs_2_), channel_id=1, source_target_pairs={{0,1},{1,0},{2,3},{3,2},{4,5},{5,4},{6,7},{7,6},{8,9},{9,8},{10,11... | collective-permute-start | bytes 786440 | tf_op jit(solution)/shard_map/ppermute | solution.py:25
  66.7 13.0 %collective-permute-start.17 = (bf16[64,1024]{1,0:T(8,128)(2,1)S(1)}, bf16[64,1024]{1,0:T(8,128)(2,1)S(1)}, u32[]{:S(2)}, u32[]{:S(2)}) collective-permute-start(bf16[64,1024]{1,0:T(8,128)(2,1)S(1)} %collective-permute-done.3.refs_7_), channel_id=1, source_target_pairs={{0,1},{1,0},{2,3},{3,2},{4,5},{5,4},{6,7},{7,6},{8,9},{9,8},{10,11... | collective-permute-start | bytes 393224 | tf_op jit(solution)/shard_map/ppermute | solution.py:25
  71.9 12.3 %collective-permute-start.16 = (bf16[64,1024]{1,0:T(8,128)(2,1)S(1)}, bf16[64,1024]{1,0:T(8,128)(2,1)S(1)}, u32[]{:S(2)}, u32[]{:S(2)}) collective-permute-start(bf16[64,1024]{1,0:T(8,128)(2,1)S(1)} %collective-permute-done.1.refs_6_), channel_id=1, source_target_pairs={{0,1},{1,0},{2,3},{3,2},{4,5},{5,4},{6,7},{7,6},{8,9},{9,8},{10,11... | collective-permute-start | bytes 393224 | tf_op jit(solution)/shard_map/ppermute | solution.py:25
  75.7 65.9 %collective-permute-start.20 = (bf16[512,1024]{1,0:T(8,128)(2,1)S(1)}, bf16[512,1024]{1,0:T(8,128)(2,1)}, u32[]{:S(2)}, u32[]{:S(2)}) collective-permute-start(bf16[512,1024]{1,0:T(8,128)(2,1)S(1)} %bitcast.15), channel_id=1, source_target_pairs={{0,24},{8,0},{16,8},{24,16},{1,25},{9,1},{17,9},{25,17},{2,26},{10... | collective-permute-start | bytes 3145736 | tf_op jit(solution)/shard_map/ppermute | solution.py:145
  79.7 61.9 %collective-permute-start.19 = (bf16[512,1024]{1,0:T(8,128)(2,1)S(1)}, bf16[512,1024]{1,0:T(8,128)(2,1)}, u32[]{:S(2)}, u32[]{:S(2)}) collective-permute-start(bf16[512,1024]{1,0:T(8,128)(2,1)S(1)} %bitcast.16), channel_id=1, source_target_pairs={{0,16},{8,24},{16,0},{24,8},{1,17},{9,25},{17,1},{25,9},{2,18},{10... | collective-permute-start | bytes 3145736 | tf_op jit(solution)/shard_map/ppermute | solution.py:145
  81.6 59.9 %collective-permute-start.18 = (bf16[512,1024]{1,0:T(8,128)(2,1)S(1)}, bf16[512,1024]{1,0:T(8,128)(2,1)}, u32[]{:S(2)}, u32[]{:S(2)}) collective-permute-start(bf16[512,1024]{1,0:T(8,128)(2,1)S(1)} %bitcast.17), channel_id=1, source_target_pairs={{0,8},{8,16},{16,24},{24,0},{1,9},{9,17},{17,25},{25,1},{2,10},{10... | collective-permute-start | bytes 3145736 | tf_op jit(solution)/shard_map/ppermute | solution.py:145
  84.2 0.7 copy-start.3
  87.9 1.0 copy-start.2
  88.9 52.7 %all-to-all-start = ((bf16[16,128,256]{2,1,0:T(8,128)(2,1)}), bf16[16,128,256]{2,1,0:T(8,128)(2,1)S(1)}, u32[]{:S(2)}, u32[]{:S(2)}) async-start(bf16[16,128,256]{2,1,0:T(8,128)(2,1)} %bitcast.20), calls=%async_computation | async-start | bytes 2097152 | tf_op jit(solution)/shard_map/all_to_all | solution.py:181
  145.0 4.5 %collective-permute-start.21 = (f32[512,256]{1,0:T(8,128)S(1)}, f32[512,256]{1,0:T(8,128)S(1)}, u32[]{:S(2)}, u32[]{:S(2)}) collective-permute-start(f32[512,256]{1,0:T(8,128)S(1)} %get-tuple-element.12), channel_id=1, source_target_pairs={{0,1},{1,0},{2,3},{3,2},{4,5},{5,4},{6,7},{7,6},{8,9},{9,8},{10,11... | collective-permute-start | bytes 1572872 | tf_op jit(solution)/shard_map/ppermute | solution.py:25
  150.2 89.1 %all-to-all-start.2 = ((bf16[64,8,256]{2,1,0:T(8,128)(2,1)}), bf16[64,8,256]{2,1,0:T(8,128)(2,1)S(1)}, u32[]{:S(2)}, u32[]{:S(2)}) async-start(bf16[64,8,256]{2,1,0:T(8,128)(2,1)} %fusion), calls=%async_computation.2 | async-start | bytes 524288 | tf_op jit(solution)/shard_map/all_to_all | solution.py:186
  159.4 40.5 %collective-permute-start.7 = (bf16[128,1024]{1,0:T(8,128)(2,1)S(1)}, bf16[128,1024]{1,0:T(8,128)(2,1)S(1)}, u32[]{:S(2)}, u32[]{:S(2)}) collective-permute-start(bf16[128,1024]{1,0:T(8,128)(2,1)S(1)} %copy-done.1), channel_id=1, source_target_pairs={{0,6},{1,7},{2,8},{3,9},{4,10},{5,11},{6,12},{7,13},{8,14},{9,15},... | collective-permute-start | bytes 786440 | tf_op jit(solution)/shard_map/ppermute | solution.py:17
  164.7 44.8 %collective-permute-start.5 = (bf16[128,1024]{1,0:T(8,128)(2,1)S(1)}, bf16[128,1024]{1,0:T(8,128)(2,1)S(1)}, u32[]{:S(2)}, u32[]{:S(2)}) collective-permute-start(bf16[128,1024]{1,0:T(8,128)(2,1)S(1)} %copy-done.1), channel_id=1, source_target_pairs={{0,2},{1,3},{2,4},{3,5},{4,6},{5,7},{6,8},{7,9},{8,10},{9,11},{10,... | collective-permute-start | bytes 786440 | tf_op jit(solution)/shard_map/ppermute | solution.py:17
  169.5 66.0 %collective-permute-start.4 = (bf16[128,1024]{1,0:T(8,128)(2,1)S(1)}, bf16[128,1024]{1,0:T(8,128)(2,1)S(1)}, u32[]{:S(2)}, u32[]{:S(2)}) collective-permute-start(bf16[128,1024]{1,0:T(8,128)(2,1)S(1)} %copy-done.1), channel_id=1, source_target_pairs={{0,1},{1,8},{2,3},{3,10},{4,5},{5,12},{6,7},{7,14},{8,9},{9,16},{1... | collective-permute-start | bytes 786440 | tf_op jit(solution)/shard_map/ppermute | solution.py:17
  200.0 22.7 %collective-permute-start.10 = (bf16[64,1024]{1,0:T(8,128)(2,1)S(1)}, bf16[64,1024]{1,0:T(8,128)(2,1)S(1)}, u32[]{:S(2)}, u32[]{:S(2)}) collective-permute-start(bf16[64,1024]{1,0:T(8,128)(2,1)S(1)} %slice.19), channel_id=1, source_target_pairs={{0,510},{1,511},{2,0},{3,1},{4,2},{5,3},{6,4},{7,5},{8,6},{9,7},{1... | collective-permute-start | bytes 393224 | tf_op jit(solution)/shard_map/ppermute | solution.py:17
  209.6 22.7 %collective-permute-start.9 = (bf16[64,1024]{1,0:T(8,128)(2,1)S(1)}, bf16[64,1024]{1,0:T(8,128)(2,1)S(1)}, u32[]{:S(2)}, u32[]{:S(2)}) collective-permute-start(bf16[64,1024]{1,0:T(8,128)(2,1)S(1)} %slice.18), channel_id=1, source_target_pairs={{0,2},{1,3},{2,4},{3,5},{4,6},{5,7},{6,8},{7,9},{8,10},{9,11},{10,... | collective-permute-start | bytes 393224 | tf_op jit(solution)/shard_map/ppermute | solution.py:17
  212.9 22.6 %collective-permute-start.8 = (bf16[128,1024]{1,0:T(8,128)(2,1)S(1)}, bf16[128,1024]{1,0:T(8,128)(2,1)S(1)}, u32[]{:S(2)}, u32[]{:S(2)}) collective-permute-start(bf16[128,1024]{1,0:T(8,128)(2,1)S(1)} %collective-permute-done.7.refs_4_), channel_id=1, source_target_pairs={{0,1},{1,0},{2,3},{3,2},{4,5},{5,4},{6,7},{7,6},{8,9},{9,8},{10,11... | collective-permute-start | bytes 786440 | tf_op jit(solution)/shard_map/ppermute | solution.py:25
  220.7 15.6 %collective-permute-start.6 = (bf16[128,1024]{1,0:T(8,128)(2,1)S(1)}, bf16[128,1024]{1,0:T(8,128)(2,1)S(1)}, u32[]{:S(2)}, u32[]{:S(2)}) collective-permute-start(bf16[128,1024]{1,0:T(8,128)(2,1)S(1)} %collective-permute-done.5.refs_2_), channel_id=1, source_target_pairs={{0,1},{1,0},{2,3},{3,2},{4,5},{5,4},{6,7},{7,6},{8,9},{9,8},{10,11... | collective-permute-start | bytes 786440 | tf_op jit(solution)/shard_map/ppermute | solution.py:25
  222.7 12.9 %collective-permute-start.12 = (bf16[64,1024]{1,0:T(8,128)(2,1)S(1)}, bf16[64,1024]{1,0:T(8,128)(2,1)S(1)}, u32[]{:S(2)}, u32[]{:S(2)}) collective-permute-start(bf16[64,1024]{1,0:T(8,128)(2,1)S(1)} %collective-permute-done.10.refs_7_), channel_id=1, source_target_pairs={{0,1},{1,0},{2,3},{3,2},{4,5},{5,4},{6,7},{7,6},{8,9},{9,8},{10,11... | collective-permute-start | bytes 393224 | tf_op jit(solution)/shard_map/ppermute | solution.py:25
  232.3 4.1 %collective-permute-start.11 = (bf16[64,1024]{1,0:T(8,128)(2,1)S(1)}, bf16[64,1024]{1,0:T(8,128)(2,1)S(1)}, u32[]{:S(2)}, u32[]{:S(2)}) collective-permute-start(bf16[64,1024]{1,0:T(8,128)(2,1)S(1)} %collective-permute-done.9.refs_6_), channel_id=1, source_target_pairs={{0,1},{1,0},{2,3},{3,2},{4,5},{5,4},{6,7},{7,6},{8,9},{9,8},{10,11... | collective-permute-start | bytes 393224 | tf_op jit(solution)/shard_map/ppermute | solution.py:25

commit v2 on v1

v2 whole, which is shorter than its diff:
```python
import jax
import jax.numpy as jnp
from jax import lax
from jax.experimental import pallas as pl
from jax.experimental.pallas import tpu as pltpu
from jax.sharding import Mesh, PartitionSpec as P

EPSILON = 1e-06
ROWS = 128
WIDTH = 1024
BLOCKS = 512
AXES = ("zl", "x", "y", "zh", "c")
LIMIT = 40 * 1024 * 1024
WINDOW_FLOPS = 4 * ROWS * 8 * ROWS * WIDTH
CAPTION_FLOPS = 70 * WINDOW_FLOPS
READY_FLOPS = 60 * WINDOW_FLOPS
PICTURE_FLOPS = 1 * WINDOW_FLOPS
HEAD_FLOPS = 2 * 2048 * 1024 * 256


def moved(value, target_of):
    return lax.ppermute(value, AXES, [(r, target_of(r) % BLOCKS) for r in range(BLOCKS)])


def moved_by(value, steps):
    return moved(value, lambda r: r + steps)


def swapped(value):
    return lax.ppermute(value, "c", [(0, 1), (1, 0)])


def after(value, *others):
    return lax.optimization_barrier((value, *others))[0]


def low_rows(wide):
    inverse = 1.0 / jnp.sqrt(jnp.sum(wide * wide, axis=-1, keepdims=True) + EPSILON)
    return (wide * inverse).astype(jnp.bfloat16)


def window_gradient(scalars, match, own, others, low):
    sharpness = scalars[0]
    offset = scalars[1]
    start = 0
    for ref in others:
        rows = ref.shape[0]
        low[start : start + rows, :] = low_rows(ref[...].astype(jnp.float32))
        start += rows
    wide = own[...].astype(jnp.float32)
    length = jnp.sqrt(jnp.sum(wide * wide, axis=-1, keepdims=True) + EPSILON)
    unit = wide / length
    logits = sharpness * lax.dot_general(
        unit.astype(jnp.bfloat16),
        low[...],
        (((1,), (1,)), ((), ())),
        preferred_element_type=jnp.float32,
    ) + offset
    first = logits[:, :ROWS]
    target = jnp.where(match, 1.0, -1.0)
    first_slope = -target * jax.nn.sigmoid(-target * first)
    slope = jnp.concatenate([first_slope, jax.nn.sigmoid(logits[:, ROWS:])], axis=1)
    total = sharpness * jnp.dot(
        slope.astype(jnp.bfloat16), low[...], preferred_element_type=jnp.float32
    )
    return (total - unit * jnp.sum(unit * total, axis=-1, keepdims=True)) / length


def caption_kernel(scalars, pair_row, own, *refs):
    *others, out, spread, low = refs
    rows = lax.broadcasted_iota(jnp.int32, (ROWS, ROWS), 0)
    match = rows == lax.rem(pair_row[...], ROWS)
    grad = window_gradient(scalars, match, own, others, low).astype(jnp.bfloat16)
    out[...] = grad
    for x in range(4):
        for y in range(4):
            spread[x, y] = grad[:, y * 256 : (y + 1) * 256]


def picture_kernel(scalars, pair_column, own, *refs):
    *others, out, low = refs
    columns = lax.broadcasted_iota(jnp.int32, (ROWS, ROWS), 1)
    match = columns == lax.rem(pair_column[...], ROWS)
    out[...] = window_gradient(scalars, match, own, others, low).astype(jnp.bfloat16)


def window_call(body, outs, flops, *args):
    return pl.pallas_call(
        body,
        out_shape=outs,
        in_specs=[pl.BlockSpec(memory_space=pltpu.SMEM)]
        + [pl.BlockSpec(memory_space=pltpu.VMEM)] * (len(args) - 1),
        out_specs=jax.tree.map(lambda _: pl.BlockSpec(memory_space=pltpu.VMEM), outs),
        scratch_shapes=[pltpu.VMEM((8 * ROWS, WIDTH), jnp.bfloat16)],
        compiler_params=pltpu.CompilerParams(vmem_limit_bytes=LIMIT),
        cost_estimate=pl.CostEstimate(
            flops=flops, bytes_accessed=4_000_000, transcendentals=ROWS * 1024
        ),
    )(*args)


def head_kernel(place, caps, feats, arrived, keep, give, table):
    c = place[0]
    total = lax.dot_general(
        caps[...], feats[...], (((0,), (0,)), ((), ())), preferred_element_type=jnp.float32
    )
    table[...] = total.T
    for zl in range(4):
        for zh in range(4):
            for y in range(4):
                base = zl * 256 + y * 64 + zh * 16
                to = (zl * 16 + zh * 4 + y) * 8
                keep[to : to + 8, :] = table[pl.ds(pl.multiple_of(base + c * 8, 8), 8), :]
                give[to : to + 8, :] = table[pl.ds(pl.multiple_of(base + 8 - c * 8, 8), 8), :]


def head_call(place, caps, feats, arrived):
    vmem = pl.BlockSpec(memory_space=pltpu.VMEM)
    half = jax.ShapeDtypeStruct((512, 256), jnp.float32)
    return pl.pallas_call(
        head_kernel,
        out_shape=(half, half),
        in_specs=[pl.BlockSpec(memory_space=pltpu.SMEM)] + [vmem] * 3,
        out_specs=(vmem, vmem),
        scratch_shapes=[pltpu.VMEM((1024, 256), jnp.float32)],
        compiler_params=pltpu.CompilerParams(vmem_limit_bytes=LIMIT),
        cost_estimate=pl.CostEstimate(
            flops=HEAD_FLOPS, bytes_accessed=6_000_000, transcendentals=0
        ),
    )(place, caps, feats, arrived)


def ready_kernel(first, second, out):
    out[...] = first[...].astype(jnp.float32) + second[...].astype(jnp.float32)


def ready(first, second):
    return pl.pallas_call(
        ready_kernel,
        grid=(1,),
        out_shape=jax.ShapeDtypeStruct((16, 128), jnp.float32),
        in_specs=[pl.BlockSpec((16, 128), lambda i: (0, 0))] * 2,
        out_specs=pl.BlockSpec((16, 128), lambda i: (0, 0)),
        cost_estimate=pl.CostEstimate(flops=READY_FLOPS, bytes_accessed=16384, transcendentals=0),
    )(first, second)


def on_device(image_proj, report_proj, report_feats, pair_index, natural_log_factor, logit_bias):
    scalars = jnp.concatenate([jnp.exp(natural_log_factor), logit_bias])
    place = lax.axis_index("c").astype(jnp.int32).reshape(1)

    with jax.named_scope("image_near"):
        image_1 = moved_by(image_proj, -2)
    with jax.named_scope("image_far"):
        image_3 = moved_by(image_proj, -6)
    with jax.named_scope("image_beside"):
        image_beside = moved(image_proj, lambda r: r - 1 if r % 2 else r - 7)

    with jax.named_scope("feats"):
        ordered = report_feats.reshape(ROWS, 4, 4, 256).transpose(2, 0, 1, 3)
        ordered = jnp.broadcast_to(ordered[:, None], (4, 4, ROWS, 4, 256)).reshape(16 * ROWS, WIDTH)
        feats = lax.all_to_all(ordered, ("x", "y"), split_axis=0, concat_axis=0, tiled=True)

    with jax.named_scope("image_relay_near"):
        image_2a = moved_by(image_1[:64], -2)
    with jax.named_scope("image_relay_far"):
        image_2b = moved_by(image_3[64:], 2)
    with jax.named_scope("image_swap"):
        images = (image_proj, image_beside, image_1, swapped(image_1), image_3, swapped(image_3))
        images += (image_2a, image_2b, swapped(image_2a), swapped(image_2b))
    with jax.named_scope("caption_kernel"):
        caption_grad, caption_spread = window_call(
            caption_kernel,
            (
                jax.ShapeDtypeStruct((ROWS, WIDTH), jnp.bfloat16),
                jax.ShapeDtypeStruct((4, 4, ROWS, 256), jnp.bfloat16),
            ),
            CAPTION_FLOPS,
            scalars,
            pair_index.reshape(1, ROWS),
            report_proj,
            *images,
        )

    report_late = after(report_proj, image_2a, image_2b)
    with jax.named_scope("report_near"):
        report_1 = moved_by(report_late, 2)
    with jax.named_scope("report_far"):
        report_3 = moved_by(report_late, 6)
    with jax.named_scope("report_beside"):
        report_beside = moved(report_late, lambda r: r + 7 if r % 2 else r + 1)
    with jax.named_scope("report_relay_near"):
        report_2a = moved_by(report_1[:64], 2)
    with jax.named_scope("report_relay_far"):
        report_2b = moved_by(report_3[64:], -2)
    with jax.named_scope("report_swap"):
        report_1s = swapped(report_1)
        report_3s = swapped(report_3)
        reports = (report_proj, report_beside, report_1, report_1s, report_3, report_3s)
        reports += (report_2a, report_2b, swapped(report_2a), swapped(report_2b))
    with jax.named_scope("picture_kernel"):
        picture_grad = window_call(
            picture_kernel,
            jax.ShapeDtypeStruct((ROWS, WIDTH), jnp.bfloat16),
            PICTURE_FLOPS,
            scalars,
            pair_index.reshape(ROWS, 1),
            image_proj,
            *reports,
        )

    with jax.named_scope("captions"):
        caps = lax.all_to_all(
            after(caption_spread, feats).reshape(16 * ROWS, 256),
            ("x", "y"),
            split_axis=0,
            concat_axis=0,
            tiled=True,
        )
    with jax.named_scope("head_kernel"):
        keep, give = head_call(place, caps, feats, ready(report_1, report_3))
    with jax.named_scope("head_swap"):
        part = (keep + swapped(give)).astype(jnp.bfloat16)
    with jax.named_scope("head_sum"):
        parts = lax.all_to_all(part, ("zl", "zh", "y"), split_axis=0, concat_axis=0, tiled=True)
        head = jnp.sum(parts.reshape(16, 4, 8, 256).astype(jnp.float32), axis=0)
        head_grad = head.transpose(1, 0, 2).reshape(8, WIDTH)
    return (picture_grad, caption_grad, head_grad)


def solution(mesh):
    fine = Mesh(mesh.devices.reshape(4, 4, 4, 4, 2), AXES)
    rows = P(AXES, None)
    return jax.shard_map(
        on_device,
        mesh=fine,
        in_specs=(rows, rows, rows, P(AXES), P(), P()),
        out_specs=(rows, rows, rows),
        check_vma=False,
    )
```

time: 241 us -> 211 us (0.88)
  the two profiles are of different devices: /device:TPU:65 before, /device:TPU:97 now
where the time goes in v2:
time: 211 us; the launch traced here: 209 us
  starting transfers between devices  136 us (64%)
  waiting for transfers between devices  42.5 us (20%)
  local copies, waits for them, and re-layouts  15.9 us (8%)
  Pallas kernels  11.5 us (5%)
  between operations  2.34 us (1%)
    ppermute x10, starting transfers between devices, moved(): lax.ppermute(value, AXES, [(r, target_of(r) % BLOCKS) for r in range(BLOC...  73.4 us
    ppermute x10, waiting for transfers between devices, moved(): lax.ppermute(value, AXES, [(r, target_of(r) % BLOCKS) for r in range(BLOC...  25.6 us
    ppermute x9, starting transfers between devices, swapped(): return lax.ppermute(value, 'c', [(0, 1), (1, 0)])  21.9 us
    all_to_all x1, starting transfers between devices, on_device(): lax.all_to_all(after(caption_spread, feats).reshape(16 * ROWS, 256), ('x'...  19.7 us
    all_to_all x1, starting transfers between devices, on_device(): lax.all_to_all(part, ('zl', 'zh', 'y'), split_axis=0, concat_axis=0, tile...  16 us
    all_to_all x1, waiting for transfers between devices, on_device(): lax.all_to_all(after(caption_spread, feats).reshape(16 * ROWS, 256), ('x'...  14.2 us
    all_to_all x1, local copies, waits for them, and re-layouts, on_device(): lax.all_to_all(ordered, ('x', 'y'), split_axis=0, concat_axis=0, tiled=True)  7.77 us
    pallas_call x2, Pallas kernels, window_call(): pl.pallas_call(body, out_shape=outs, in_specs=[pl.BlockSpec(memory_space=...  6.52 us
  transfers between devices with their start and end apart: 22, of which 6 were waited for; matrix products, arithmetic and copies ran while one was open for 3% of the time, Pallas kernels for 4%

profile of v2, /device:TPU:97, one launch (start us, length us, event | category | flops | bytes accessed | tf_op | source)
XLA Modules:
  0.0 209.4 jit_solution(4963781212974620675)
XLA Ops:
  0.6 14.8 %collective-permute-start = (bf16[128,1024]{1,0:T(8,128)(2,1)}, bf16[128,1024]{1,0:T(8,128)(2,1)S(1)}, u32[]{:S(2)}, u32[]{:S(2)}) collective-permute-start(bf16[128,1024]{1,0:T(8,128)(2,1)} %refs_0_.3), channel_id=1, source_target_pairs={{0,510},{1,511},{2,0},{3,1},{4,2},{5,3},{6,4},{7,5},{8,6},{9,7},{1... | collective-permute-start | bytes 786440 | tf_op jit(solution)/shard_map/image_near/ppermute | solution.py:22
  15.5 1.9 collective-permute-start.2
  17.4 1.9 reshape.39
  19.3 0.4 copy.10
  19.7 3.6 %broadcast_in_dim.2 = bf16[4,4,128,4,256]{4,3,2,1,0:T(4,128)(2,1)} broadcast(bf16[4,128,4,256]{3,2,1,0:T(4,128)(2,1)S(1)} %copy.10), dimensions={0,2,3,4} | broadcast | bytes 5242880 | tf_op jit(solution)/shard_map/feats/broadcast_in_dim | solution.py:161
  23.3 7.8 %all_to_all.20 = bf16[16,128,1024]{2,1,0:T(8,128)(2,1)} reshape(bf16[4,4,128,4,256]{4,3,2,1,0:T(4,128)(2,1)} %broadcast_in_dim.2) | data formatting | bytes 8388608 | tf_op jit(solution)/shard_map/feats/all_to_all | solution.py:162
  31.1 4.7 %all-to-all-start = ((bf16[16,128,1024]{2,1,0:T(8,128)(2,1)}), bf16[16,128,1024]{2,1,0:T(8,128)(2,1)}, u32[]{:S(2)}, u32[]{:S(2)}) async-start(bf16[16,128,1024]{2,1,0:T(8,128)(2,1)} %all_to_all.20), calls=%async_computation | async-start | bytes 8388608 | tf_op jit(solution)/shard_map/feats/all_to_all | solution.py:162
  35.7 2.9 %collective-permute-start.13 = (bf16[128,1024]{1,0:T(8,128)(2,1)S(1)}, bf16[128,1024]{1,0:T(8,128)(2,1)S(1)}, u32[]{:S(2)}, u32[]{:S(2)}) collective-permute-start(bf16[128,1024]{1,0:T(8,128)(2,1)S(1)} %copy-done.4), channel_id=1, source_target_pairs={{0,505},{1,0},{2,507},{3,2},{4,509},{5,4},{6,511},{7,6},{8,1},{9,8... | collective-permute-start | bytes 786440 | tf_op jit(solution)/shard_map/image_beside/ppermute | solution.py:22
  38.6 0.0 collective-permute-done.refs_2_
  38.6 12.6 %collective-permute-start.1 = (bf16[64,1024]{1,0:T(8,128)(2,1)S(1)}, bf16[64,1024]{1,0:T(8,128)(2,1)S(1)}, u32[]{:S(2)}, u32[]{:S(2)}) collective-permute-start(bf16[64,1024]{1,0:T(8,128)(2,1)S(1)} %slice.16), channel_id=1, source_target_pairs={{0,510},{1,511},{2,0},{3,1},{4,2},{5,3},{6,4},{7,5},{8,6},{9,7},{1... | collective-permute-start | bytes 393224 | tf_op jit(solution)/shard_map/image_relay_near/ppermute | solution.py:22
  51.3 1.9 collective-permute-start.3
  53.2 2.2 %collective-permute-start.14 = (bf16[128,1024]{1,0:T(8,128)(2,1)S(1)}, bf16[128,1024]{1,0:T(8,128)(2,1)S(1)}, u32[]{:S(2)}, u32[]{:S(2)}) collective-permute-start(bf16[128,1024]{1,0:T(8,128)(2,1)S(1)} %collective-permute-done.refs_2_), channel_id=1, source_target_pairs={{0,1},{1,0},{2,3},{3,2},{4,5},{5,4},{6,7},{7,6},{8,9},{9,8},{10,11... | collective-permute-start | bytes 786440 | tf_op jit(solution)/shard_map/image_swap/ppermute | solution.py:30
  55.4 2.1 %collective-permute-start.15 = (bf16[128,1024]{1,0:T(8,128)(2,1)S(1)}, bf16[128,1024]{1,0:T(8,128)(2,1)S(1)}, u32[]{:S(2)}, u32[]{:S(2)}) collective-permute-start(bf16[128,1024]{1,0:T(8,128)(2,1)S(1)} %collective-permute-done.2.refs_4_), channel_id=1, source_target_pairs={{0,1},{1,0},{2,3},{3,2},{4,5},{5,4},{6,7},{7,6},{8,9},{9,8},{10,11... | collective-permute-start | bytes 786440 | tf_op jit(solution)/shard_map/image_swap/ppermute | solution.py:30
  57.6 4.2 %collective-permute-start.16 = (bf16[64,1024]{1,0:T(8,128)(2,1)S(1)}, bf16[64,1024]{1,0:T(8,128)(2,1)S(1)}, u32[]{:S(2)}, u32[]{:S(2)}) collective-permute-start(bf16[64,1024]{1,0:T(8,128)(2,1)S(1)} %collective-permute-done.1.refs_6_), channel_id=1, source_target_pairs={{0,1},{1,0},{2,3},{3,2},{4,5},{5,4},{6,7},{7,6},{8,9},{9,8},{10,11... | collective-permute-start | bytes 393224 | tf_op jit(solution)/shard_map/image_swap/ppermute | solution.py:30
  61.7 14.1 %collective-permute-done.3.refs_7_ = bf16[64,1024]{1,0:T(8,128)(2,1)S(1)} collective-permute-done((bf16[64,1024]{1,0:T(8,128)(2,1)S(1)}, bf16[64,1024]{1,0:T(8,128)(2,1)S(1)}, u32[]{:S(2)}, u32[]{:S(2)}) %collective-permute-start.3) | collective-permute-done | bytes 131104 | tf_op jit(solution)/shard_map/image_relay_far/ppermute | solution.py:22
  75.8 2.8 %collective-permute-start.17 = (bf16[64,1024]{1,0:T(8,128)(2,1)S(1)}, bf16[64,1024]{1,0:T(8,128)(2,1)S(1)}, u32[]{:S(2)}, u32[]{:S(2)}) collective-permute-start(bf16[64,1024]{1,0:T(8,128)(2,1)S(1)} %collective-permute-done.3.refs_7_), channel_id=1, source_target_pairs={{0,1},{1,0},{2,3},{3,2},{4,5},{5,4},{6,7},{7,6},{8,9},{9,8},{10,11... | collective-permute-start | bytes 393224 | tf_op jit(solution)/shard_map/image_swap/ppermute | solution.py:30
  80.0 0.1 pad_maximum_fusion.scalars
  80.0 1.9 collective-permute-done.13.refs_1_
  81.9 10.7 %collective-permute-start.5 = (bf16[128,1024]{1,0:T(8,128)(2,1)S(1)}, bf16[128,1024]{1,0:T(8,128)(2,1)S(1)}, u32[]{:S(2)}, u32[]{:S(2)}) collective-permute-start(bf16[128,1024]{1,0:T(8,128)(2,1)S(1)} %copy-done.5), channel_id=1, source_target_pairs={{0,2},{1,3},{2,4},{3,5},{4,6},{5,7},{6,8},{7,9},{8,10},{9,11},{10,... | collective-permute-start | bytes 786440 | tf_op jit(solution)/shard_map/report_near/ppermute | solution.py:22
  92.6 0.0 collective-permute-done.16.refs_8_
  92.6 10.4 %collective-permute-start.7 = (bf16[128,1024]{1,0:T(8,128)(2,1)S(1)}, bf16[128,1024]{1,0:T(8,128)(2,1)S(1)}, u32[]{:S(2)}, u32[]{:S(2)}) collective-permute-start(bf16[128,1024]{1,0:T(8,128)(2,1)S(1)} %copy-done.5), channel_id=1, source_target_pairs={{0,6},{1,7},{2,8},{3,9},{4,10},{5,11},{6,12},{7,13},{8,14},{9,15},... | collective-permute-start | bytes 786440 | tf_op jit(solution)/shard_map/report_far/ppermute | solution.py:22
  103.1 0.0 collective-permute-done.17.refs_9_
  103.1 0.0 collective-permute-done.14.refs_3_
  103.1 3.5 %caption_kernel.1 = (bf16[128,1024]{1,0:T(8,128)(2,1)}, bf16[4,4,128,256]{3,2,1,0:T(8,128)(2,1)}) custom-call(f32[2]{0:T(128)S(1)} %pad_maximum_fusion.scalars, s32[1,128]{1,0:T(1,128)S(1)} %bitcast.15, bf16[128,1024]{1,0:T(8,128)(2,1)S(1)} %copy-done.5, bf16[128,1024]{1,0:T(8,128)(2,1)S(1)} %copy-done.4, ...), custom_call_target="tpu_custom_call" | custom-call | flops 37580963840 | bytes 4000000 | tf_op jit(solution)/shard_map/caption_kernel/pallas_call | solution.py:88
  106.6 19.7 %all-to-all-start.1 = ((bf16[16,128,256]{2,1,0:T(8,128)(2,1)}), bf16[16,128,256]{2,1,0:T(8,128)(2,1)S(1)}, u32[]{:S(2)}, u32[]{:S(2)}) async-start(bf16[16,128,256]{2,1,0:T(8,128)(2,1)} %bitcast.5), calls=%async_computation.1 | async-start | bytes 2097152 | tf_op jit(solution)/shard_map/captions/all_to_all | solution.py:213
  126.3 0.0 copy-start
  126.3 0.7 copy-done
  127.0 0.7 copy-done.2
  127.7 1.3 head_kernel.2.arrived
  129.0 14.2 %all-to-all-done.1 = bf16[16,128,256]{2,1,0:T(8,128)(2,1)S(1)} async-done(((bf16[16,128,256]{2,1,0:T(8,128)(2,1)}), bf16[16,128,256]{2,1,0:T(8,128)(2,1)S(1)}, u32[]{:S(2)}, u32[]{:S(2)}) %all-to-all-start.1) | async-done | bytes 1048608 | tf_op jit(solution)/shard_map/captions/all_to_all | solution.py:213
  143.2 0.7 copy-done.6
  143.9 3.7 %head_kernel.3 = (f32[512,256]{1,0:T(8,128)S(1)}, f32[512,256]{1,0:T(8,128)S(1)}) custom-call(s32[1]{0:T(128)} %bitcast.2.place, bf16[2048,256]{1,0:T(8,128)(2,1)S(1)} %bitcast.14, bf16[2048,1024]{1,0:T(8,128)(2,1)} %bitcast.4.feats, f32[16,128]{1,0:T(8,128)S(1)} %copy-done.6), custom_call_target="tpu_custom_call" | custom-call | flops 1073741824 | bytes 6000000 | tf_op jit(solution)/shard_map/head_kernel/pallas_call | solution.py:120
  147.6 1.9 collective-permute-start.18
  149.6 1.9 collective-permute-done.18
  151.5 0.7 fusion
  152.2 16.0 %all-to-all-start.2 = ((bf16[64,8,256]{2,1,0:T(8,128)(2,1)}), bf16[64,8,256]{2,1,0:T(8,128)(2,1)S(1)}, u32[]{:S(2)}, u32[]{:S(2)}) async-start(bf16[64,8,256]{2,1,0:T(8,128)(2,1)} %fusion), calls=%async_computation.2 | async-start | bytes 524288 | tf_op jit(solution)/shard_map/head_sum/all_to_all | solution.py:225
  168.2 3.8 %collective-permute-start.4 = (bf16[128,1024]{1,0:T(8,128)(2,1)S(1)}, bf16[128,1024]{1,0:T(8,128)(2,1)S(1)}, u32[]{:S(2)}, u32[]{:S(2)}) collective-permute-start(bf16[128,1024]{1,0:T(8,128)(2,1)S(1)} %copy-done.5), channel_id=1, source_target_pairs={{0,1},{1,8},{2,3},{3,10},{4,5},{5,12},{6,7},{7,14},{8,9},{9,16},{1... | collective-permute-start | bytes 786440 | tf_op jit(solution)/shard_map/report_beside/ppermute | solution.py:22
  172.1 7.0 %collective-permute-start.9 = (bf16[64,1024]{1,0:T(8,128)(2,1)S(1)}, bf16[64,1024]{1,0:T(8,128)(2,1)S(1)}, u32[]{:S(2)}, u32[]{:S(2)}) collective-permute-start(bf16[64,1024]{1,0:T(8,128)(2,1)S(1)} %slice.18), channel_id=1, source_target_pairs={{0,2},{1,3},{2,4},{3,5},{4,6},{5,7},{6,8},{7,9},{8,10},{9,11},{10,... | collective-permute-start | bytes 393224 | tf_op jit(solution)/shard_map/report_relay_near/ppermute | solution.py:22
  179.2 7.3 %collective-permute-start.10 = (bf16[64,1024]{1,0:T(8,128)(2,1)S(1)}, bf16[64,1024]{1,0:T(8,128)(2,1)S(1)}, u32[]{:S(2)}, u32[]{:S(2)}) collective-permute-start(bf16[64,1024]{1,0:T(8,128)(2,1)S(1)} %slice.19), channel_id=1, source_target_pairs={{0,510},{1,511},{2,0},{3,1},{4,2},{5,3},{6,4},{7,5},{8,6},{9,7},{1... | collective-permute-start | bytes 393224 | tf_op jit(solution)/shard_map/report_relay_far/ppermute | solution.py:22
  186.4 1.9 collective-permute-start.6
  188.4 2.4 %collective-permute-start.8 = (bf16[128,1024]{1,0:T(8,128)(2,1)S(1)}, bf16[128,1024]{1,0:T(8,128)(2,1)S(1)}, u32[]{:S(2)}, u32[]{:S(2)}) collective-permute-start(bf16[128,1024]{1,0:T(8,128)(2,1)S(1)} %copy-done.3), channel_id=1, source_target_pairs={{0,1},{1,0},{2,3},{3,2},{4,5},{5,4},{6,7},{7,6},{8,9},{9,8},{10,11... | collective-permute-start | bytes 786440 | tf_op jit(solution)/shard_map/report_swap/ppermute | solution.py:30
  190.8 9.6 %collective-permute-done.9.refs_6_ = bf16[64,1024]{1,0:T(8,128)(2,1)S(1)} collective-permute-done((bf16[64,1024]{1,0:T(8,128)(2,1)S(1)}, bf16[64,1024]{1,0:T(8,128)(2,1)S(1)}, u32[]{:S(2)}, u32[]{:S(2)}) %collective-permute-start.9) | collective-permute-done | bytes 131104 | tf_op jit(solution)/shard_map/report_relay_near/ppermute | solution.py:22
  200.4 1.9 collective-permute-start.11
  202.3 2.4 %collective-permute-start.12 = (bf16[64,1024]{1,0:T(8,128)(2,1)S(1)}, bf16[64,1024]{1,0:T(8,128)(2,1)S(1)}, u32[]{:S(2)}, u32[]{:S(2)}) collective-permute-start(bf16[64,1024]{1,0:T(8,128)(2,1)S(1)} %collective-permute-done.10.refs_7_), channel_id=1, source_target_pairs={{0,1},{1,0},{2,3},{3,2},{4,5},{5,4},{6,7},{7,6},{8,9},{9,8},{10,11... | collective-permute-start | bytes 393224 | tf_op jit(solution)/shard_map/report_swap/ppermute | solution.py:30
  204.7 0.1 copy.9.pair_column
  204.9 0.8 collective-permute-done.12.refs_9_
  205.7 3.0 %picture_kernel.1 = bf16[128,1024]{1,0:T(8,128)(2,1)} custom-call(f32[2]{0:T(128)S(1)} %pad_maximum_fusion.scalars, s32[128,1]{1,0:T(8,128)S(1)} %copy.9.pair_column, bf16[128,1024]{1,0:T(8,128)(2,1)S(1)} %copy-done.4, bf16[128,1024]{1,0:T(8,128)(2,1)S(1)} %copy-done.5, bf16[128,1024]{1,0:T(8,128)(2,1)S(1)} %collective-permute-done.4.refs_1_, ...), custom_call_target="tpu_custom_call" | custom-call | flops 536870912 | bytes 4000000 | tf_op jit(solution)/shard_map/picture_kernel/pallas_call | solution.py:88
  208.7 0.7 convert_reduce_fusion
  (28 shorter events, 0.1 us)
Async XLA Ops:
  0.6 38.0 %collective-permute-start = (bf16[128,1024]{1,0:T(8,128)(2,1)}, bf16[128,1024]{1,0:T(8,128)(2,1)S(1)}, u32[]{:S(2)}, u32[]{:S(2)}) collective-permute-start(bf16[128,1024]{1,0:T(8,128)(2,1)} %refs_0_.3), channel_id=1, source_target_pairs={{0,510},{1,511},{2,0},{3,1},{4,2},{5,3},{6,4},{7,5},{8,6},{9,7},{1... | collective-permute-start | bytes 786440 | tf_op jit(solution)/shard_map/image_near/ppermute | solution.py:22
  15.5 35.8 %collective-permute-start.2 = (bf16[128,1024]{1,0:T(8,128)(2,1)}, bf16[128,1024]{1,0:T(8,128)(2,1)S(1)}, u32[]{:S(2)}, u32[]{:S(2)}) collective-permute-start(bf16[128,1024]{1,0:T(8,128)(2,1)} %refs_0_.3), channel_id=1, source_target_pairs={{0,506},{1,507},{2,508},{3,509},{4,510},{5,511},{6,0},{7,1},{8,2},... | collective-permute-start | bytes 786440 | tf_op jit(solution)/shard_map/image_far/ppermute | solution.py:22
  31.0 4.7 %copy-start.4 = (bf16[128,1024]{1,0:T(8,128)(2,1)S(1)}, bf16[128,1024]{1,0:T(8,128)(2,1)}, u32[]{:S(2)}) copy-start(bf16[128,1024]{1,0:T(8,128)(2,1)} %refs_0_.3) | copy-start | bytes 786436
  31.1 50.9 %copy-start.5 = (bf16[128,1024]{1,0:T(8,128)(2,1)S(1)}, bf16[128,1024]{1,0:T(8,128)(2,1)}, u32[]{:S(2)}) copy-start(bf16[128,1024]{1,0:T(8,128)(2,1)} %own.3) | copy-start | bytes 786436
  31.1 72.0 %copy-start.7 = (s32[128]{0:T(128)S(1)}, s32[128]{0:T(128)}, u32[]{:S(2)}) copy-start(s32[128]{0:T(128)} %param.9) | copy-start | bytes 1540
  31.1 75.6 %all-to-all-start = ((bf16[16,128,1024]{2,1,0:T(8,128)(2,1)}), bf16[16,128,1024]{2,1,0:T(8,128)(2,1)}, u32[]{:S(2)}, u32[]{:S(2)}) async-start(bf16[16,128,1024]{2,1,0:T(8,128)(2,1)} %all_to_all.20), calls=%async_computation | async-start | bytes 8388608 | tf_op jit(solution)/shard_map/feats/all_to_all | solution.py:162
  35.7 46.2 %collective-permute-start.13 = (bf16[128,1024]{1,0:T(8,128)(2,1)S(1)}, bf16[128,1024]{1,0:T(8,128)(2,1)S(1)}, u32[]{:S(2)}, u32[]{:S(2)}) collective-permute-start(bf16[128,1024]{1,0:T(8,128)(2,1)S(1)} %copy-done.4), channel_id=1, source_target_pairs={{0,505},{1,0},{2,507},{3,2},{4,509},{5,4},{6,511},{7,6},{8,1},{9,8... | collective-permute-start | bytes 786440 | tf_op jit(solution)/shard_map/image_beside/ppermute | solution.py:22
  38.6 18.9 %collective-permute-start.1 = (bf16[64,1024]{1,0:T(8,128)(2,1)S(1)}, bf16[64,1024]{1,0:T(8,128)(2,1)S(1)}, u32[]{:S(2)}, u32[]{:S(2)}) collective-permute-start(bf16[64,1024]{1,0:T(8,128)(2,1)S(1)} %slice.16), channel_id=1, source_target_pairs={{0,510},{1,511},{2,0},{3,1},{4,2},{5,3},{6,4},{7,5},{8,6},{9,7},{1... | collective-permute-start | bytes 393224 | tf_op jit(solution)/shard_map/image_relay_near/ppermute | solution.py:22
  51.3 24.6 %collective-permute-start.3 = (bf16[64,1024]{1,0:T(8,128)(2,1)S(1)}, bf16[64,1024]{1,0:T(8,128)(2,1)S(1)}, u32[]{:S(2)}, u32[]{:S(2)}) collective-permute-start(bf16[64,1024]{1,0:T(8,128)(2,1)S(1)} %slice.17), channel_id=1, source_target_pairs={{0,2},{1,3},{2,4},{3,5},{4,6},{5,7},{6,8},{7,9},{8,10},{9,11},{10,... | collective-permute-start | bytes 393224 | tf_op jit(solution)/shard_map/image_relay_far/ppermute | solution.py:22
  53.2 49.9 %collective-permute-start.14 = (bf16[128,1024]{1,0:T(8,128)(2,1)S(1)}, bf16[128,1024]{1,0:T(8,128)(2,1)S(1)}, u32[]{:S(2)}, u32[]{:S(2)}) collective-permute-start(bf16[128,1024]{1,0:T(8,128)(2,1)S(1)} %collective-permute-done.refs_2_), channel_id=1, source_target_pairs={{0,1},{1,0},{2,3},{3,2},{4,5},{5,4},{6,7},{7,6},{8,9},{9,8},{10,11... | collective-permute-start | bytes 786440 | tf_op jit(solution)/shard_map/image_swap/ppermute | solution.py:30
  55.4 47.7 %collective-permute-start.15 = (bf16[128,1024]{1,0:T(8,128)(2,1)S(1)}, bf16[128,1024]{1,0:T(8,128)(2,1)S(1)}, u32[]{:S(2)}, u32[]{:S(2)}) collective-permute-start(bf16[128,1024]{1,0:T(8,128)(2,1)S(1)} %collective-permute-done.2.refs_4_), channel_id=1, source_target_pairs={{0,1},{1,0},{2,3},{3,2},{4,5},{5,4},{6,7},{7,6},{8,9},{9,8},{10,11... | collective-permute-start | bytes 786440 | tf_op jit(solution)/shard_map/image_swap/ppermute | solution.py:30
  57.6 35.1 %collective-permute-start.16 = (bf16[64,1024]{1,0:T(8,128)(2,1)S(1)}, bf16[64,1024]{1,0:T(8,128)(2,1)S(1)}, u32[]{:S(2)}, u32[]{:S(2)}) collective-permute-start(bf16[64,1024]{1,0:T(8,128)(2,1)S(1)} %collective-permute-done.1.refs_6_), channel_id=1, source_target_pairs={{0,1},{1,0},{2,3},{3,2},{4,5},{5,4},{6,7},{7,6},{8,9},{9,8},{10,11... | collective-permute-start | bytes 393224 | tf_op jit(solution)/shard_map/image_swap/ppermute | solution.py:30
  75.8 27.2 %collective-permute-start.17 = (bf16[64,1024]{1,0:T(8,128)(2,1)S(1)}, bf16[64,1024]{1,0:T(8,128)(2,1)S(1)}, u32[]{:S(2)}, u32[]{:S(2)}) collective-permute-start(bf16[64,1024]{1,0:T(8,128)(2,1)S(1)} %collective-permute-done.3.refs_7_), channel_id=1, source_target_pairs={{0,1},{1,0},{2,3},{3,2},{4,5},{5,4},{6,7},{7,6},{8,9},{9,8},{10,11... | collective-permute-start | bytes 393224 | tf_op jit(solution)/shard_map/image_swap/ppermute | solution.py:30
  81.9 44.4 %collective-permute-start.5 = (bf16[128,1024]{1,0:T(8,128)(2,1)S(1)}, bf16[128,1024]{1,0:T(8,128)(2,1)S(1)}, u32[]{:S(2)}, u32[]{:S(2)}) collective-permute-start(bf16[128,1024]{1,0:T(8,128)(2,1)S(1)} %copy-done.5), channel_id=1, source_target_pairs={{0,2},{1,3},{2,4},{3,5},{4,6},{5,7},{6,8},{7,9},{8,10},{9,11},{10,... | collective-permute-start | bytes 786440 | tf_op jit(solution)/shard_map/report_near/ppermute | solution.py:22
  92.6 33.7 %collective-permute-start.7 = (bf16[128,1024]{1,0:T(8,128)(2,1)S(1)}, bf16[128,1024]{1,0:T(8,128)(2,1)S(1)}, u32[]{:S(2)}, u32[]{:S(2)}) collective-permute-start(bf16[128,1024]{1,0:T(8,128)(2,1)S(1)} %copy-done.5), channel_id=1, source_target_pairs={{0,6},{1,7},{2,8},{3,9},{4,10},{5,11},{6,12},{7,13},{8,14},{9,15},... | collective-permute-start | bytes 786440 | tf_op jit(solution)/shard_map/report_far/ppermute | solution.py:22
  106.6 36.6 %all-to-all-start.1 = ((bf16[16,128,256]{2,1,0:T(8,128)(2,1)}), bf16[16,128,256]{2,1,0:T(8,128)(2,1)S(1)}, u32[]{:S(2)}, u32[]{:S(2)}) async-start(bf16[16,128,256]{2,1,0:T(8,128)(2,1)} %bitcast.5), calls=%async_computation.1 | async-start | bytes 2097152 | tf_op jit(solution)/shard_map/captions/all_to_all | solution.py:213
  126.3 0.7 copy-start
  127.0 0.7 copy-start.2
  129.0 43.1 %copy-start.1 = (bf16[128,1024]{1,0:T(8,128)(2,1)S(1)}, bf16[128,1024]{1,0:T(8,128)(2,1)}, u32[]{:S(2)}) copy-start(bf16[128,1024]{1,0:T(8,128)(2,1)} %copy-done) | copy-start | bytes 786436
  129.0 50.1 %copy-start.3 = (bf16[128,1024]{1,0:T(8,128)(2,1)S(1)}, bf16[128,1024]{1,0:T(8,128)(2,1)}, u32[]{:S(2)}) copy-start(bf16[128,1024]{1,0:T(8,128)(2,1)} %copy-done.2) | copy-start | bytes 786436
  143.2 0.7 copy-start.6
  147.6 3.8 %collective-permute-start.18 = (f32[512,256]{1,0:T(8,128)S(1)}, f32[512,256]{1,0:T(8,128)S(1)}, u32[]{:S(2)}, u32[]{:S(2)}) collective-permute-start(f32[512,256]{1,0:T(8,128)S(1)} %get-tuple-element.14), channel_id=1, source_target_pairs={{0,1},{1,0},{2,3},{3,2},{4,5},{5,4},{6,7},{7,6},{8,9},{9,8},{10,11... | collective-permute-start | bytes 1572872 | tf_op jit(solution)/shard_map/head_swap/ppermute | solution.py:30
  152.2 56.5 %all-to-all-start.2 = ((bf16[64,8,256]{2,1,0:T(8,128)(2,1)}), bf16[64,8,256]{2,1,0:T(8,128)(2,1)S(1)}, u32[]{:S(2)}, u32[]{:S(2)}) async-start(bf16[64,8,256]{2,1,0:T(8,128)(2,1)} %fusion), calls=%async_computation.2 | async-start | bytes 524288 | tf_op jit(solution)/shard_map/head_sum/all_to_all | solution.py:225
  168.2 36.6 %collective-permute-start.4 = (bf16[128,1024]{1,0:T(8,128)(2,1)S(1)}, bf16[128,1024]{1,0:T(8,128)(2,1)S(1)}, u32[]{:S(2)}, u32[]{:S(2)}) collective-permute-start(bf16[128,1024]{1,0:T(8,128)(2,1)S(1)} %copy-done.5), channel_id=1, source_target_pairs={{0,1},{1,8},{2,3},{3,10},{4,5},{5,12},{6,7},{7,14},{8,9},{9,16},{1... | collective-permute-start | bytes 786440 | tf_op jit(solution)/shard_map/report_beside/ppermute | solution.py:22
  172.1 28.3 %collective-permute-start.9 = (bf16[64,1024]{1,0:T(8,128)(2,1)S(1)}, bf16[64,1024]{1,0:T(8,128)(2,1)S(1)}, u32[]{:S(2)}, u32[]{:S(2)}) collective-permute-start(bf16[64,1024]{1,0:T(8,128)(2,1)S(1)} %slice.18), channel_id=1, source_target_pairs={{0,2},{1,3},{2,4},{3,5},{4,6},{5,7},{6,8},{7,9},{8,10},{9,11},{10,... | collective-permute-start | bytes 393224 | tf_op jit(solution)/shard_map/report_relay_near/ppermute | solution.py:22
  179.2 23.1 %collective-permute-start.10 = (bf16[64,1024]{1,0:T(8,128)(2,1)S(1)}, bf16[64,1024]{1,0:T(8,128)(2,1)S(1)}, u32[]{:S(2)}, u32[]{:S(2)}) collective-permute-start(bf16[64,1024]{1,0:T(8,128)(2,1)S(1)} %slice.19), channel_id=1, source_target_pairs={{0,510},{1,511},{2,0},{3,1},{4,2},{5,3},{6,4},{7,5},{8,6},{9,7},{1... | collective-permute-start | bytes 393224 | tf_op jit(solution)/shard_map/report_relay_far/ppermute | solution.py:22
  186.4 19.2 %collective-permute-start.6 = (bf16[128,1024]{1,0:T(8,128)(2,1)S(1)}, bf16[128,1024]{1,0:T(8,128)(2,1)S(1)}, u32[]{:S(2)}, u32[]{:S(2)}) collective-permute-start(bf16[128,1024]{1,0:T(8,128)(2,1)S(1)} %copy-done.1), channel_id=1, source_target_pairs={{0,1},{1,0},{2,3},{3,2},{4,5},{5,4},{6,7},{7,6},{8,9},{9,8},{10,11... | collective-permute-start | bytes 786440 | tf_op jit(solution)/shard_map/report_swap/ppermute | solution.py:30
  188.4 17.3 %collective-permute-start.8 = (bf16[128,1024]{1,0:T(8,128)(2,1)S(1)}, bf16[128,1024]{1,0:T(8,128)(2,1)S(1)}, u32[]{:S(2)}, u32[]{:S(2)}) collective-permute-start(bf16[128,1024]{1,0:T(8,128)(2,1)S(1)} %copy-done.3), channel_id=1, source_target_pairs={{0,1},{1,0},{2,3},{3,2},{4,5},{5,4},{6,7},{7,6},{8,9},{9,8},{10,11... | collective-permute-start | bytes 786440 | tf_op jit(solution)/shard_map/report_swap/ppermute | solution.py:30
  200.4 4.5 %collective-permute-start.11 = (bf16[64,1024]{1,0:T(8,128)(2,1)S(1)}, bf16[64,1024]{1,0:T(8,128)(2,1)S(1)}, u32[]{:S(2)}, u32[]{:S(2)}) collective-permute-start(bf16[64,1024]{1,0:T(8,128)(2,1)S(1)} %collective-permute-done.9.refs_6_), channel_id=1, source_target_pairs={{0,1},{1,0},{2,3},{3,2},{4,5},{5,4},{6,7},{7,6},{8,9},{9,8},{10,11... | collective-permute-start | bytes 393224 | tf_op jit(solution)/shard_map/report_swap/ppermute | solution.py:30
  202.3 3.4 %collective-permute-start.12 = (bf16[64,1024]{1,0:T(8,128)(2,1)S(1)}, bf16[64,1024]{1,0:T(8,128)(2,1)S(1)}, u32[]{:S(2)}, u32[]{:S(2)}) collective-permute-start(bf16[64,1024]{1,0:T(8,128)(2,1)S(1)} %collective-permute-done.10.refs_7_), channel_id=1, source_target_pairs={{0,1},{1,0},{2,3},{3,2},{4,5},{5,4},{6,7},{7,6},{8,9},{9,8},{10,11... | collective-permute-start | bytes 393224 | tf_op jit(solution)/shard_map/report_swap/ppermute | solution.py:30

commit v3 on v2

--- a/solution.py
+++ b/solution.py
@@ -13,7 +13,7 @@
 LIMIT = 40 * 1024 * 1024
 WINDOW_FLOPS = 4 * ROWS * 8 * ROWS * WIDTH
 CAPTION_FLOPS = 70 * WINDOW_FLOPS
-READY_FLOPS = 60 * WINDOW_FLOPS
+READY_FLOPS = 14 * WINDOW_FLOPS
 PICTURE_FLOPS = 1 * WINDOW_FLOPS
 HEAD_FLOPS = 2 * 2048 * 1024 * 256
 
@@ -130,6 +130,27 @@
     )(place, caps, feats, arrived)
 
 
+def columns_kernel(feats, out):
+    for x in range(4):
+        for zl in range(4):
+            piece = feats[:, zl * 1024 + x * 256 : zl * 1024 + x * 256 + 256]
+            for y in range(4):
+                row = (x * 4 + y) * ROWS
+                out[row : row + ROWS, zl * 256 : zl * 256 + 256] = piece
+
+
+def columns_call(feats):
+    vmem = pl.BlockSpec(memory_space=pltpu.VMEM)
+    return pl.pallas_call(
+        columns_kernel,
+        out_shape=jax.ShapeDtypeStruct((16 * ROWS, WIDTH), jnp.bfloat16),
+        in_specs=[vmem],
+        out_specs=vmem,
+        compiler_params=pltpu.CompilerParams(vmem_limit_bytes=LIMIT),
+        cost_estimate=pl.CostEstimate(flops=0, bytes_accessed=5_000_000, transcendentals=0),
+    )(feats)
+
+
 def ready_kernel(first, second, out):
     out[...] = first[...].astype(jnp.float32) + second[...].astype(jnp.float32)
 
@@ -157,8 +178,7 @@
         image_beside = moved(image_proj, lambda r: r - 1 if r % 2 else r - 7)
 
     with jax.named_scope("feats"):
-        ordered = report_feats.reshape(ROWS, 4, 4, 256).transpose(2, 0, 1, 3)
-        ordered = jnp.broadcast_to(ordered[:, None], (4, 4, ROWS, 4, 256)).reshape(16 * ROWS, WIDTH)
+        ordered = columns_call(after(report_feats, image_beside))
         feats = lax.all_to_all(ordered, ("x", "y"), split_axis=0, concat_axis=0, tiled=True)
 
     with jax.named_scope("image_relay_near"):
@@ -218,7 +238,7 @@
             tiled=True,
         )
     with jax.named_scope("head_kernel"):
-        keep, give = head_call(place, caps, feats, ready(report_1, report_3))
+        keep, give = head_call(place, caps, feats, ready(report_2a, report_2b))
     with jax.named_scope("head_swap"):
         part = (keep + swapped(give)).astype(jnp.bfloat16)
     with jax.named_scope("head_sum"):

time: 211 us -> 181 us (0.86)
  the two profiles are of different devices: /device:TPU:97 before, /device:TPU:128 now
where the time goes in v3:
time: 181 us; the launch traced here: 180 us
  starting transfers between devices  115 us (64%)
  waiting for transfers between devices  44.4 us (25%)
  Pallas kernels  12 us (7%)
  local copies, waits for them, and re-layouts  4.8 us (3%)
  between operations  2.33 us (1%)
    ppermute x10, starting transfers between devices, moved(): lax.ppermute(value, AXES, [(r, target_of(r) % BLOCKS) for r in range(BLOC...  61 us
    ppermute x10, waiting for transfers between devices, moved(): lax.ppermute(value, AXES, [(r, target_of(r) % BLOCKS) for r in range(BLOC...  34.8 us
    ppermute x9, starting transfers between devices, swapped(): return lax.ppermute(value, 'c', [(0, 1), (1, 0)])  19.8 us
    all_to_all x1, starting transfers between devices, on_device(): lax.all_to_all(after(caption_spread, feats).reshape(16 * ROWS, 256), ('x'...  18.2 us
    all_to_all x1, starting transfers between devices, on_device(): lax.all_to_all(part, ('zl', 'zh', 'y'), split_axis=0, concat_axis=0, tile...  10.8 us
    all_to_all x1, waiting for transfers between devices, on_device(): lax.all_to_all(ordered, ('x', 'y'), split_axis=0, concat_axis=0, tiled=True)  7.68 us
    pallas_call x2, Pallas kernels, window_call(): pl.pallas_call(body, out_shape=outs, in_specs=[pl.BlockSpec(memory_space=...  6.49 us
    all_to_all x1, starting transfers between devices, on_device(): lax.all_to_all(ordered, ('x', 'y'), split_axis=0, concat_axis=0, tiled=True)  4.67 us
  transfers between devices with their start and end apart: 22, of which 8 were waited for; matrix products, arithmetic and copies ran while one was open for 0% of the time, Pallas kernels for 5%

profile of v3, /device:TPU:128, one launch (start us, length us, event | category | flops | bytes accessed | tf_op | source)
XLA Modules:
  0.0 179.6 jit_solution(7212326892026922898)
XLA Ops:
  0.6 10.6 %collective-permute-start.13 = (bf16[128,1024]{1,0:T(8,128)(2,1)}, bf16[128,1024]{1,0:T(8,128)(2,1)S(1)}, u32[]{:S(2)}, u32[]{:S(2)}) collective-permute-start(bf16[128,1024]{1,0:T(8,128)(2,1)} %refs_0_.3), channel_id=1, source_target_pairs={{0,505},{1,0},{2,507},{3,2},{4,509},{5,4},{6,511},{7,6},{8,1},{9,8... | collective-permute-start | bytes 786440 | tf_op jit(solution)/shard_map/image_beside/ppermute | solution.py:22
  11.3 1.9 %collective-permute-start = (bf16[128,1024]{1,0:T(8,128)(2,1)}, bf16[128,1024]{1,0:T(8,128)(2,1)S(1)}, u32[]{:S(2)}, u32[]{:S(2)}) collective-permute-start(bf16[128,1024]{1,0:T(8,128)(2,1)} %refs_0_.3), channel_id=1, source_target_pairs={{0,510},{1,511},{2,0},{3,1},{4,2},{5,3},{6,4},{7,5},{8,6},{9,7},{1... | collective-permute-start | bytes 786440 | tf_op jit(solution)/shard_map/image_near/ppermute | solution.py:22
  13.2 8.0 %collective-permute-start.2 = (bf16[128,1024]{1,0:T(8,128)(2,1)}, bf16[128,1024]{1,0:T(8,128)(2,1)S(1)}, u32[]{:S(2)}, u32[]{:S(2)}) collective-permute-start(bf16[128,1024]{1,0:T(8,128)(2,1)} %refs_0_.3), channel_id=1, source_target_pairs={{0,506},{1,507},{2,508},{3,509},{4,510},{5,511},{6,0},{7,1},{8,2},... | collective-permute-start | bytes 786440 | tf_op jit(solution)/shard_map/image_far/ppermute | solution.py:22
  21.2 0.0 collective-permute-done.13.refs_1_
  21.2 1.2 copy-done.1
  22.4 0.5 feats.1
  23.0 2.0 %copy-done = bf16[2048,1024]{1,0:T(8,128)(2,1)} copy-done((bf16[2048,1024]{1,0:T(8,128)(2,1)}, bf16[2048,1024]{1,0:T(8,128)(2,1)S(1)}, u32[]{:S(2)}) %copy-start) | copy-done | bytes 4194328
  25.0 4.7 %all-to-all-start = ((bf16[16,128,1024]{2,1,0:T(8,128)(2,1)}), bf16[16,128,1024]{2,1,0:T(8,128)(2,1)}, u32[]{:S(2)}, u32[]{:S(2)}) async-start(bf16[16,128,1024]{2,1,0:T(8,128)(2,1)} %bitcast.14), calls=%async_computation | async-start | bytes 8388608 | tf_op jit(solution)/shard_map/feats/all_to_all | solution.py:182
  29.7 0.3 collective-permute-done.refs_2_
  30.0 1.9 %collective-permute-start.1 = (bf16[64,1024]{1,0:T(8,128)(2,1)S(1)}, bf16[64,1024]{1,0:T(8,128)(2,1)S(1)}, u32[]{:S(2)}, u32[]{:S(2)}) collective-permute-start(bf16[64,1024]{1,0:T(8,128)(2,1)S(1)} %slice.16), channel_id=1, source_target_pairs={{0,510},{1,511},{2,0},{3,1},{4,2},{5,3},{6,4},{7,5},{8,6},{9,7},{1... | collective-permute-start | bytes 393224 | tf_op jit(solution)/shard_map/image_relay_near/ppermute | solution.py:22
  31.9 3.7 %collective-permute-done.2.refs_4_ = bf16[128,1024]{1,0:T(8,128)(2,1)S(1)} collective-permute-done((bf16[128,1024]{1,0:T(8,128)(2,1)}, bf16[128,1024]{1,0:T(8,128)(2,1)S(1)}, u32[]{:S(2)}, u32[]{:S(2)}) %collective-permute-start.2) | collective-permute-done | bytes 262176 | tf_op jit(solution)/shard_map/image_far/ppermute | solution.py:22
  35.7 13.2 %collective-permute-start.3 = (bf16[64,1024]{1,0:T(8,128)(2,1)S(1)}, bf16[64,1024]{1,0:T(8,128)(2,1)S(1)}, u32[]{:S(2)}, u32[]{:S(2)}) collective-permute-start(bf16[64,1024]{1,0:T(8,128)(2,1)S(1)} %slice.17), channel_id=1, source_target_pairs={{0,2},{1,3},{2,4},{3,5},{4,6},{5,7},{6,8},{7,9},{8,10},{9,11},{10,... | collective-permute-start | bytes 393224 | tf_op jit(solution)/shard_map/image_relay_far/ppermute | solution.py:22
  48.8 1.9 %collective-permute-start.14 = (bf16[128,1024]{1,0:T(8,128)(2,1)S(1)}, bf16[128,1024]{1,0:T(8,128)(2,1)S(1)}, u32[]{:S(2)}, u32[]{:S(2)}) collective-permute-start(bf16[128,1024]{1,0:T(8,128)(2,1)S(1)} %collective-permute-done.refs_2_), channel_id=1, source_target_pairs={{0,1},{1,0},{2,3},{3,2},{4,5},{5,4},{6,7},{7,6},{8,9},{9,8},{10,11... | collective-permute-start | bytes 786440 | tf_op jit(solution)/shard_map/image_swap/ppermute | solution.py:30
  50.8 2.4 %collective-permute-start.15 = (bf16[128,1024]{1,0:T(8,128)(2,1)S(1)}, bf16[128,1024]{1,0:T(8,128)(2,1)S(1)}, u32[]{:S(2)}, u32[]{:S(2)}) collective-permute-start(bf16[128,1024]{1,0:T(8,128)(2,1)S(1)} %collective-permute-done.2.refs_4_), channel_id=1, source_target_pairs={{0,1},{1,0},{2,3},{3,2},{4,5},{5,4},{6,7},{7,6},{8,9},{9,8},{10,11... | collective-permute-start | bytes 786440 | tf_op jit(solution)/shard_map/image_swap/ppermute | solution.py:30
  53.2 0.0 collective-permute-done.1.refs_6_
  53.2 1.9 %collective-permute-start.16 = (bf16[64,1024]{1,0:T(8,128)(2,1)S(1)}, bf16[64,1024]{1,0:T(8,128)(2,1)S(1)}, u32[]{:S(2)}, u32[]{:S(2)}) collective-permute-start(bf16[64,1024]{1,0:T(8,128)(2,1)S(1)} %collective-permute-done.1.refs_6_), channel_id=1, source_target_pairs={{0,1},{1,0},{2,3},{3,2},{4,5},{5,4},{6,7},{7,6},{8,9},{9,8},{10,11... | collective-permute-start | bytes 393224 | tf_op jit(solution)/shard_map/image_swap/ppermute | solution.py:30
  55.1 4.1 %collective-permute-done.3.refs_7_ = bf16[64,1024]{1,0:T(8,128)(2,1)S(1)} collective-permute-done((bf16[64,1024]{1,0:T(8,128)(2,1)S(1)}, bf16[64,1024]{1,0:T(8,128)(2,1)S(1)}, u32[]{:S(2)}, u32[]{:S(2)}) %collective-permute-start.3) | collective-permute-done | bytes 131104 | tf_op jit(solution)/shard_map/image_relay_far/ppermute | solution.py:22
  59.2 1.9 %collective-permute-start.17 = (bf16[64,1024]{1,0:T(8,128)(2,1)S(1)}, bf16[64,1024]{1,0:T(8,128)(2,1)S(1)}, u32[]{:S(2)}, u32[]{:S(2)}) collective-permute-start(bf16[64,1024]{1,0:T(8,128)(2,1)S(1)} %collective-permute-done.3.refs_7_), channel_id=1, source_target_pairs={{0,1},{1,0},{2,3},{3,2},{4,5},{5,4},{6,7},{7,6},{8,9},{9,8},{10,11... | collective-permute-start | bytes 393224 | tf_op jit(solution)/shard_map/image_swap/ppermute | solution.py:30
  62.5 0.1 pad_maximum_fusion.scalars
  62.5 8.5 %collective-permute-start.7 = (bf16[128,1024]{1,0:T(8,128)(2,1)S(1)}, bf16[128,1024]{1,0:T(8,128)(2,1)S(1)}, u32[]{:S(2)}, u32[]{:S(2)}) collective-permute-start(bf16[128,1024]{1,0:T(8,128)(2,1)S(1)} %copy-done.3), channel_id=1, source_target_pairs={{0,6},{1,7},{2,8},{3,9},{4,10},{5,11},{6,12},{7,13},{8,14},{9,15},... | collective-permute-start | bytes 786440 | tf_op jit(solution)/shard_map/report_far/ppermute | solution.py:22
  71.1 5.2 %collective-permute-start.5 = (bf16[128,1024]{1,0:T(8,128)(2,1)S(1)}, bf16[128,1024]{1,0:T(8,128)(2,1)S(1)}, u32[]{:S(2)}, u32[]{:S(2)}) collective-permute-start(bf16[128,1024]{1,0:T(8,128)(2,1)S(1)} %copy-done.3), channel_id=1, source_target_pairs={{0,2},{1,3},{2,4},{3,5},{4,6},{5,7},{6,8},{7,9},{8,10},{9,11},{10,... | collective-permute-start | bytes 786440 | tf_op jit(solution)/shard_map/report_near/ppermute | solution.py:22
  76.3 0.0 collective-permute-done.17.refs_9_
  76.3 0.0 collective-permute-done.15.refs_5_
  76.3 3.5 %caption_kernel.1 = (bf16[128,1024]{1,0:T(8,128)(2,1)}, bf16[4,4,128,256]{3,2,1,0:T(8,128)(2,1)}) custom-call(f32[2]{0:T(128)S(1)} %pad_maximum_fusion.scalars, s32[1,128]{1,0:T(1,128)S(1)} %bitcast.16, bf16[128,1024]{1,0:T(8,128)(2,1)S(1)} %copy-done.3, bf16[128,1024]{1,0:T(8,128)(2,1)S(1)} %copy-done.2, ...), custom_call_target="tpu_custom_call" | custom-call | flops 37580963840 | bytes 4000000 | tf_op jit(solution)/shard_map/caption_kernel/pallas_call | solution.py:88
  79.8 7.7 %all-to-all-done = bf16[16,128,1024]{2,1,0:T(8,128)(2,1)} async-done(((bf16[16,128,1024]{2,1,0:T(8,128)(2,1)}), bf16[16,128,1024]{2,1,0:T(8,128)(2,1)}, u32[]{:S(2)}, u32[]{:S(2)}) %all-to-all-start) | async-done | bytes 4194336 | tf_op jit(solution)/shard_map/feats/all_to_all | solution.py:182
  87.5 18.2 %all-to-all-start.1 = ((bf16[16,128,256]{2,1,0:T(8,128)(2,1)}), bf16[16,128,256]{2,1,0:T(8,128)(2,1)S(1)}, u32[]{:S(2)}, u32[]{:S(2)}) async-start(bf16[16,128,256]{2,1,0:T(8,128)(2,1)} %bitcast.5), calls=%async_computation.1 | async-start | bytes 2097152 | tf_op jit(solution)/shard_map/captions/all_to_all | solution.py:233
  105.8 4.8 %collective-permute-start.10 = (bf16[64,1024]{1,0:T(8,128)(2,1)S(1)}, bf16[64,1024]{1,0:T(8,128)(2,1)S(1)}, u32[]{:S(2)}, u32[]{:S(2)}) collective-permute-start(bf16[64,1024]{1,0:T(8,128)(2,1)S(1)} %slice.19), channel_id=1, source_target_pairs={{0,510},{1,511},{2,0},{3,1},{4,2},{5,3},{6,4},{7,5},{8,6},{9,7},{1... | collective-permute-start | bytes 393224 | tf_op jit(solution)/shard_map/report_relay_far/ppermute | solution.py:22
  110.6 5.0 %collective-permute-start.9 = (bf16[64,1024]{1,0:T(8,128)(2,1)S(1)}, bf16[64,1024]{1,0:T(8,128)(2,1)S(1)}, u32[]{:S(2)}, u32[]{:S(2)}) collective-permute-start(bf16[64,1024]{1,0:T(8,128)(2,1)S(1)} %slice.18), channel_id=1, source_target_pairs={{0,2},{1,3},{2,4},{3,5},{4,6},{5,7},{6,8},{7,9},{8,10},{9,11},{10,... | collective-permute-start | bytes 393224 | tf_op jit(solution)/shard_map/report_relay_near/ppermute | solution.py:22
  115.6 6.6 %collective-permute-done.10.refs_7_.second = bf16[64,1024]{1,0:T(8,128)(2,1)S(1)} collective-permute-done((bf16[64,1024]{1,0:T(8,128)(2,1)S(1)}, bf16[64,1024]{1,0:T(8,128)(2,1)S(1)}, u32[]{:S(2)}, u32[]{:S(2)}) %collective-permute-start.10) | collective-permute-done | bytes 131104 | tf_op jit(solution)/shard_map/report_relay_far/ppermute | solution.py:22
  122.2 9.9 %collective-permute-done.9.refs_6_.first = bf16[64,1024]{1,0:T(8,128)(2,1)S(1)} collective-permute-done((bf16[64,1024]{1,0:T(8,128)(2,1)S(1)}, bf16[64,1024]{1,0:T(8,128)(2,1)S(1)}, u32[]{:S(2)}, u32[]{:S(2)}) %collective-permute-start.9) | collective-permute-done | bytes 131104 | tf_op jit(solution)/shard_map/report_relay_near/ppermute | solution.py:22
  132.1 0.7 copy-done.6
  132.7 1.3 head_kernel.2.arrived
  134.1 0.0 copy-start.8
  134.1 0.7 copy-done.8
  134.8 3.7 %head_kernel.3 = (f32[512,256]{1,0:T(8,128)S(1)}, f32[512,256]{1,0:T(8,128)S(1)}) custom-call(s32[1]{0:T(128)} %bitcast.2.place, bf16[2048,256]{1,0:T(8,128)(2,1)S(1)} %bitcast.15, bf16[2048,1024]{1,0:T(8,128)(2,1)} %bitcast.4.feats, f32[16,128]{1,0:T(8,128)S(1)} %copy-done.8), custom_call_target="tpu_custom_call" | custom-call | flops 1073741824 | bytes 6000000 | tf_op jit(solution)/shard_map/head_kernel/pallas_call | solution.py:120
  138.5 1.9 %collective-permute-start.18 = (f32[512,256]{1,0:T(8,128)S(1)}, f32[512,256]{1,0:T(8,128)S(1)}, u32[]{:S(2)}, u32[]{:S(2)}) collective-permute-start(f32[512,256]{1,0:T(8,128)S(1)} %get-tuple-element.16), channel_id=1, source_target_pairs={{0,1},{1,0},{2,3},{3,2},{4,5},{5,4},{6,7},{7,6},{8,9},{9,8},{10,11... | collective-permute-start | bytes 1572872 | tf_op jit(solution)/shard_map/head_swap/ppermute | solution.py:30
  140.5 1.9 %collective-permute-done.18 = f32[512,256]{1,0:T(8,128)S(1)} collective-permute-done((f32[512,256]{1,0:T(8,128)S(1)}, f32[512,256]{1,0:T(8,128)S(1)}, u32[]{:S(2)}, u32[]{:S(2)}) %collective-permute-start.18) | collective-permute-done | bytes 524320 | tf_op jit(solution)/shard_map/head_swap/ppermute | solution.py:30
  142.3 0.7 fusion
  143.1 10.8 %all-to-all-start.2 = ((bf16[64,8,256]{2,1,0:T(8,128)(2,1)}), bf16[64,8,256]{2,1,0:T(8,128)(2,1)S(1)}, u32[]{:S(2)}, u32[]{:S(2)}) async-start(bf16[64,8,256]{2,1,0:T(8,128)(2,1)} %fusion), calls=%async_computation.2 | async-start | bytes 524288 | tf_op jit(solution)/shard_map/head_sum/all_to_all | solution.py:245
  153.9 1.9 %collective-permute-start.4 = (bf16[128,1024]{1,0:T(8,128)(2,1)S(1)}, bf16[128,1024]{1,0:T(8,128)(2,1)S(1)}, u32[]{:S(2)}, u32[]{:S(2)}) collective-permute-start(bf16[128,1024]{1,0:T(8,128)(2,1)S(1)} %copy-done.3), channel_id=1, source_target_pairs={{0,1},{1,8},{2,3},{3,10},{4,5},{5,12},{6,7},{7,14},{8,9},{9,16},{1... | collective-permute-start | bytes 786440 | tf_op jit(solution)/shard_map/report_beside/ppermute | solution.py:22
  155.8 3.5 %collective-permute-start.6 = (bf16[128,1024]{1,0:T(8,128)(2,1)S(1)}, bf16[128,1024]{1,0:T(8,128)(2,1)S(1)}, u32[]{:S(2)}, u32[]{:S(2)}) collective-permute-start(bf16[128,1024]{1,0:T(8,128)(2,1)S(1)} %collective-permute-done.5.refs_2_), channel_id=1, source_target_pairs={{0,1},{1,0},{2,3},{3,2},{4,5},{5,4},{6,7},{7,6},{8,9},{9,8},{10,11... | collective-permute-start | bytes 786440 | tf_op jit(solution)/shard_map/report_swap/ppermute | solution.py:30
  159.3 1.9 %collective-permute-start.8 = (bf16[128,1024]{1,0:T(8,128)(2,1)S(1)}, bf16[128,1024]{1,0:T(8,128)(2,1)S(1)}, u32[]{:S(2)}, u32[]{:S(2)}) collective-permute-start(bf16[128,1024]{1,0:T(8,128)(2,1)S(1)} %collective-permute-done.7.refs_4_), channel_id=1, source_target_pairs={{0,1},{1,0},{2,3},{3,2},{4,5},{5,4},{6,7},{7,6},{8,9},{9,8},{10,11... | collective-permute-start | bytes 786440 | tf_op jit(solution)/shard_map/report_swap/ppermute | solution.py:30
  161.2 2.4 %collective-permute-start.11 = (bf16[64,1024]{1,0:T(8,128)(2,1)S(1)}, bf16[64,1024]{1,0:T(8,128)(2,1)S(1)}, u32[]{:S(2)}, u32[]{:S(2)}) collective-permute-start(bf16[64,1024]{1,0:T(8,128)(2,1)S(1)} %copy-done.7), channel_id=1, source_target_pairs={{0,1},{1,0},{2,3},{3,2},{4,5},{5,4},{6,7},{7,6},{8,9},{9,8},{10,11... | collective-permute-start | bytes 393224 | tf_op jit(solution)/shard_map/report_swap/ppermute | solution.py:30
  163.7 1.9 %collective-permute-start.12 = (bf16[64,1024]{1,0:T(8,128)(2,1)S(1)}, bf16[64,1024]{1,0:T(8,128)(2,1)S(1)}, u32[]{:S(2)}, u32[]{:S(2)}) collective-permute-start(bf16[64,1024]{1,0:T(8,128)(2,1)S(1)} %copy-done.5), channel_id=1, source_target_pairs={{0,1},{1,0},{2,3},{3,2},{4,5},{5,4},{6,7},{7,6},{8,9},{9,8},{10,11... | collective-permute-start | bytes 393224 | tf_op jit(solution)/shard_map/report_swap/ppermute | solution.py:30
  165.6 0.1 copy.9.pair_column
  165.7 10.2 %collective-permute-done.4.refs_1_ = bf16[128,1024]{1,0:T(8,128)(2,1)S(1)} collective-permute-done((bf16[128,1024]{1,0:T(8,128)(2,1)S(1)}, bf16[128,1024]{1,0:T(8,128)(2,1)S(1)}, u32[]{:S(2)}, u32[]{:S(2)}) %collective-permute-start.4) | collective-permute-done | bytes 262176 | tf_op jit(solution)/shard_map/report_beside/ppermute | solution.py:22
  175.9 3.0 %picture_kernel.1 = bf16[128,1024]{1,0:T(8,128)(2,1)} custom-call(f32[2]{0:T(128)S(1)} %pad_maximum_fusion.scalars, s32[128,1]{1,0:T(8,128)S(1)} %copy.9.pair_column, bf16[128,1024]{1,0:T(8,128)(2,1)S(1)} %copy-done.2, bf16[128,1024]{1,0:T(8,128)(2,1)S(1)} %copy-done.3, bf16[128,1024]{1,0:T(8,128)(2,1)S(1)} %collective-permute-done.4.refs_1_, ...), custom_call_target="tpu_custom_call" | custom-call | flops 536870912 | bytes 4000000 | tf_op jit(solution)/shard_map/picture_kernel/pallas_call | solution.py:88
  178.9 0.7 convert_reduce_fusion
  (29 shorter events, 0.1 us)
Async XLA Ops:
  0.6 20.6 %collective-permute-start.13 = (bf16[128,1024]{1,0:T(8,128)(2,1)}, bf16[128,1024]{1,0:T(8,128)(2,1)S(1)}, u32[]{:S(2)}, u32[]{:S(2)}) collective-permute-start(bf16[128,1024]{1,0:T(8,128)(2,1)} %refs_0_.3), channel_id=1, source_target_pairs={{0,505},{1,0},{2,507},{3,2},{4,509},{5,4},{6,511},{7,6},{8,1},{9,8... | collective-permute-start | bytes 786440 | tf_op jit(solution)/shard_map/image_beside/ppermute | solution.py:22
  11.3 18.7 %collective-permute-start = (bf16[128,1024]{1,0:T(8,128)(2,1)}, bf16[128,1024]{1,0:T(8,128)(2,1)S(1)}, u32[]{:S(2)}, u32[]{:S(2)}) collective-permute-start(bf16[128,1024]{1,0:T(8,128)(2,1)} %refs_0_.3), channel_id=1, source_target_pairs={{0,510},{1,511},{2,0},{3,1},{4,2},{5,3},{6,4},{7,5},{8,6},{9,7},{1... | collective-permute-start | bytes 786440 | tf_op jit(solution)/shard_map/image_near/ppermute | solution.py:22
  13.2 22.5 %collective-permute-start.2 = (bf16[128,1024]{1,0:T(8,128)(2,1)}, bf16[128,1024]{1,0:T(8,128)(2,1)S(1)}, u32[]{:S(2)}, u32[]{:S(2)}) collective-permute-start(bf16[128,1024]{1,0:T(8,128)(2,1)} %refs_0_.3), channel_id=1, source_target_pairs={{0,506},{1,507},{2,508},{3,509},{4,510},{5,511},{6,0},{7,1},{8,2},... | collective-permute-start | bytes 786440 | tf_op jit(solution)/shard_map/image_far/ppermute | solution.py:22
  21.2 1.2 copy-start.1
  23.0 2.0 %copy-start = (bf16[2048,1024]{1,0:T(8,128)(2,1)}, bf16[2048,1024]{1,0:T(8,128)(2,1)S(1)}, u32[]{:S(2)}) copy-start(bf16[2048,1024]{1,0:T(8,128)(2,1)S(1)} %feats.1) | copy-start | bytes 12582916
  25.0 37.5 %copy-start.3 = (bf16[128,1024]{1,0:T(8,128)(2,1)S(1)}, bf16[128,1024]{1,0:T(8,128)(2,1)}, u32[]{:S(2)}) copy-start(bf16[128,1024]{1,0:T(8,128)(2,1)} %own.3) | copy-start | bytes 786436
  25.0 51.3 %copy-start.2 = (bf16[128,1024]{1,0:T(8,128)(2,1)S(1)}, bf16[128,1024]{1,0:T(8,128)(2,1)}, u32[]{:S(2)}) copy-start(bf16[128,1024]{1,0:T(8,128)(2,1)} %refs_0_.3) | copy-start | bytes 786436
  25.0 51.3 %copy-start.9 = (s32[128]{0:T(128)S(1)}, s32[128]{0:T(128)}, u32[]{:S(2)}) copy-start(s32[128]{0:T(128)} %param.9) | copy-start | bytes 1540
  25.0 62.5 %all-to-all-start = ((bf16[16,128,1024]{2,1,0:T(8,128)(2,1)}), bf16[16,128,1024]{2,1,0:T(8,128)(2,1)}, u32[]{:S(2)}, u32[]{:S(2)}) async-start(bf16[16,128,1024]{2,1,0:T(8,128)(2,1)} %bitcast.14), calls=%async_computation | async-start | bytes 8388608 | tf_op jit(solution)/shard_map/feats/all_to_all | solution.py:182
  30.0 23.2 %collective-permute-start.1 = (bf16[64,1024]{1,0:T(8,128)(2,1)S(1)}, bf16[64,1024]{1,0:T(8,128)(2,1)S(1)}, u32[]{:S(2)}, u32[]{:S(2)}) collective-permute-start(bf16[64,1024]{1,0:T(8,128)(2,1)S(1)} %slice.16), channel_id=1, source_target_pairs={{0,510},{1,511},{2,0},{3,1},{4,2},{5,3},{6,4},{7,5},{8,6},{9,7},{1... | collective-permute-start | bytes 393224 | tf_op jit(solution)/shard_map/image_relay_near/ppermute | solution.py:22
  35.7 23.5 %collective-permute-start.3 = (bf16[64,1024]{1,0:T(8,128)(2,1)S(1)}, bf16[64,1024]{1,0:T(8,128)(2,1)S(1)}, u32[]{:S(2)}, u32[]{:S(2)}) collective-permute-start(bf16[64,1024]{1,0:T(8,128)(2,1)S(1)} %slice.17), channel_id=1, source_target_pairs={{0,2},{1,3},{2,4},{3,5},{4,6},{5,7},{6,8},{7,9},{8,10},{9,11},{10,... | collective-permute-start | bytes 393224 | tf_op jit(solution)/shard_map/image_relay_far/ppermute | solution.py:22
  48.8 27.5 %collective-permute-start.14 = (bf16[128,1024]{1,0:T(8,128)(2,1)S(1)}, bf16[128,1024]{1,0:T(8,128)(2,1)S(1)}, u32[]{:S(2)}, u32[]{:S(2)}) collective-permute-start(bf16[128,1024]{1,0:T(8,128)(2,1)S(1)} %collective-permute-done.refs_2_), channel_id=1, source_target_pairs={{0,1},{1,0},{2,3},{3,2},{4,5},{5,4},{6,7},{7,6},{8,9},{9,8},{10,11... | collective-permute-start | bytes 786440 | tf_op jit(solution)/shard_map/image_swap/ppermute | solution.py:30
  50.8 25.6 %collective-permute-start.15 = (bf16[128,1024]{1,0:T(8,128)(2,1)S(1)}, bf16[128,1024]{1,0:T(8,128)(2,1)S(1)}, u32[]{:S(2)}, u32[]{:S(2)}) collective-permute-start(bf16[128,1024]{1,0:T(8,128)(2,1)S(1)} %collective-permute-done.2.refs_4_), channel_id=1, source_target_pairs={{0,1},{1,0},{2,3},{3,2},{4,5},{5,4},{6,7},{7,6},{8,9},{9,8},{10,11... | collective-permute-start | bytes 786440 | tf_op jit(solution)/shard_map/image_swap/ppermute | solution.py:30
  53.2 17.9 %collective-permute-start.16 = (bf16[64,1024]{1,0:T(8,128)(2,1)S(1)}, bf16[64,1024]{1,0:T(8,128)(2,1)S(1)}, u32[]{:S(2)}, u32[]{:S(2)}) collective-permute-start(bf16[64,1024]{1,0:T(8,128)(2,1)S(1)} %collective-permute-done.1.refs_6_), channel_id=1, source_target_pairs={{0,1},{1,0},{2,3},{3,2},{4,5},{5,4},{6,7},{7,6},{8,9},{9,8},{10,11... | collective-permute-start | bytes 393224 | tf_op jit(solution)/shard_map/image_swap/ppermute | solution.py:30
  59.2 17.1 %collective-permute-start.17 = (bf16[64,1024]{1,0:T(8,128)(2,1)S(1)}, bf16[64,1024]{1,0:T(8,128)(2,1)S(1)}, u32[]{:S(2)}, u32[]{:S(2)}) collective-permute-start(bf16[64,1024]{1,0:T(8,128)(2,1)S(1)} %collective-permute-done.3.refs_7_), channel_id=1, source_target_pairs={{0,1},{1,0},{2,3},{3,2},{4,5},{5,4},{6,7},{7,6},{8,9},{9,8},{10,11... | collective-permute-start | bytes 393224 | tf_op jit(solution)/shard_map/image_swap/ppermute | solution.py:30
  62.5 43.2 %collective-permute-start.7 = (bf16[128,1024]{1,0:T(8,128)(2,1)S(1)}, bf16[128,1024]{1,0:T(8,128)(2,1)S(1)}, u32[]{:S(2)}, u32[]{:S(2)}) collective-permute-start(bf16[128,1024]{1,0:T(8,128)(2,1)S(1)} %copy-done.3), channel_id=1, source_target_pairs={{0,6},{1,7},{2,8},{3,9},{4,10},{5,11},{6,12},{7,13},{8,14},{9,15},... | collective-permute-start | bytes 786440 | tf_op jit(solution)/shard_map/report_far/ppermute | solution.py:22
  71.1 39.5 %collective-permute-start.5 = (bf16[128,1024]{1,0:T(8,128)(2,1)S(1)}, bf16[128,1024]{1,0:T(8,128)(2,1)S(1)}, u32[]{:S(2)}, u32[]{:S(2)}) collective-permute-start(bf16[128,1024]{1,0:T(8,128)(2,1)S(1)} %copy-done.3), channel_id=1, source_target_pairs={{0,2},{1,3},{2,4},{3,5},{4,6},{5,7},{6,8},{7,9},{8,10},{9,11},{10,... | collective-permute-start | bytes 786440 | tf_op jit(solution)/shard_map/report_near/ppermute | solution.py:22
  87.5 46.6 %all-to-all-start.1 = ((bf16[16,128,256]{2,1,0:T(8,128)(2,1)}), bf16[16,128,256]{2,1,0:T(8,128)(2,1)S(1)}, u32[]{:S(2)}, u32[]{:S(2)}) async-start(bf16[16,128,256]{2,1,0:T(8,128)(2,1)} %bitcast.5), calls=%async_computation.1 | async-start | bytes 2097152 | tf_op jit(solution)/shard_map/captions/all_to_all | solution.py:233
  105.8 16.4 %collective-permute-start.10 = (bf16[64,1024]{1,0:T(8,128)(2,1)S(1)}, bf16[64,1024]{1,0:T(8,128)(2,1)S(1)}, u32[]{:S(2)}, u32[]{:S(2)}) collective-permute-start(bf16[64,1024]{1,0:T(8,128)(2,1)S(1)} %slice.19), channel_id=1, source_target_pairs={{0,510},{1,511},{2,0},{3,1},{4,2},{5,3},{6,4},{7,5},{8,6},{9,7},{1... | collective-permute-start | bytes 393224 | tf_op jit(solution)/shard_map/report_relay_far/ppermute | solution.py:22
  110.6 21.5 %collective-permute-start.9 = (bf16[64,1024]{1,0:T(8,128)(2,1)S(1)}, bf16[64,1024]{1,0:T(8,128)(2,1)S(1)}, u32[]{:S(2)}, u32[]{:S(2)}) collective-permute-start(bf16[64,1024]{1,0:T(8,128)(2,1)S(1)} %slice.18), channel_id=1, source_target_pairs={{0,2},{1,3},{2,4},{3,5},{4,6},{5,7},{6,8},{7,9},{8,10},{9,11},{10,... | collective-permute-start | bytes 393224 | tf_op jit(solution)/shard_map/report_relay_near/ppermute | solution.py:22
  122.2 9.9 %copy-start.4 = (bf16[64,1024]{1,0:T(8,128)(2,1)}, bf16[64,1024]{1,0:T(8,128)(2,1)S(1)}, u32[]{:S(2)}) copy-start(bf16[64,1024]{1,0:T(8,128)(2,1)S(1)} %collective-permute-done.10.refs_7_.second) | copy-start | bytes 393220
  132.1 0.7 copy-start.6
  134.1 27.2 %copy-start.7 = (bf16[64,1024]{1,0:T(8,128)(2,1)S(1)}, bf16[64,1024]{1,0:T(8,128)(2,1)}, u32[]{:S(2)}) copy-start(bf16[64,1024]{1,0:T(8,128)(2,1)} %copy-done.6) | copy-start | bytes 393220
  134.1 29.6 %copy-start.5 = (bf16[64,1024]{1,0:T(8,128)(2,1)S(1)}, bf16[64,1024]{1,0:T(8,128)(2,1)}, u32[]{:S(2)}) copy-start(bf16[64,1024]{1,0:T(8,128)(2,1)} %copy-done.4) | copy-start | bytes 393220
  134.1 0.7 copy-start.8
  138.5 3.8 %collective-permute-start.18 = (f32[512,256]{1,0:T(8,128)S(1)}, f32[512,256]{1,0:T(8,128)S(1)}, u32[]{:S(2)}, u32[]{:S(2)}) collective-permute-start(f32[512,256]{1,0:T(8,128)S(1)} %get-tuple-element.16), channel_id=1, source_target_pairs={{0,1},{1,0},{2,3},{3,2},{4,5},{5,4},{6,7},{7,6},{8,9},{9,8},{10,11... | collective-permute-start | bytes 1572872 | tf_op jit(solution)/shard_map/head_swap/ppermute | solution.py:30
  143.1 35.9 %all-to-all-start.2 = ((bf16[64,8,256]{2,1,0:T(8,128)(2,1)}), bf16[64,8,256]{2,1,0:T(8,128)(2,1)S(1)}, u32[]{:S(2)}, u32[]{:S(2)}) async-start(bf16[64,8,256]{2,1,0:T(8,128)(2,1)} %fusion), calls=%async_computation.2 | async-start | bytes 524288 | tf_op jit(solution)/shard_map/head_sum/all_to_all | solution.py:245
  153.9 22.0 %collective-permute-start.4 = (bf16[128,1024]{1,0:T(8,128)(2,1)S(1)}, bf16[128,1024]{1,0:T(8,128)(2,1)S(1)}, u32[]{:S(2)}, u32[]{:S(2)}) collective-permute-start(bf16[128,1024]{1,0:T(8,128)(2,1)S(1)} %copy-done.3), channel_id=1, source_target_pairs={{0,1},{1,8},{2,3},{3,10},{4,5},{5,12},{6,7},{7,14},{8,9},{9,16},{1... | collective-permute-start | bytes 786440 | tf_op jit(solution)/shard_map/report_beside/ppermute | solution.py:22
  155.8 20.1 %collective-permute-start.6 = (bf16[128,1024]{1,0:T(8,128)(2,1)S(1)}, bf16[128,1024]{1,0:T(8,128)(2,1)S(1)}, u32[]{:S(2)}, u32[]{:S(2)}) collective-permute-start(bf16[128,1024]{1,0:T(8,128)(2,1)S(1)} %collective-permute-done.5.refs_2_), channel_id=1, source_target_pairs={{0,1},{1,0},{2,3},{3,2},{4,5},{5,4},{6,7},{7,6},{8,9},{9,8},{10,11... | collective-permute-start | bytes 786440 | tf_op jit(solution)/shard_map/report_swap/ppermute | solution.py:30
  159.3 16.6 %collective-permute-start.8 = (bf16[128,1024]{1,0:T(8,128)(2,1)S(1)}, bf16[128,1024]{1,0:T(8,128)(2,1)S(1)}, u32[]{:S(2)}, u32[]{:S(2)}) collective-permute-start(bf16[128,1024]{1,0:T(8,128)(2,1)S(1)} %collective-permute-done.7.refs_4_), channel_id=1, source_target_pairs={{0,1},{1,0},{2,3},{3,2},{4,5},{5,4},{6,7},{7,6},{8,9},{9,8},{10,11... | collective-permute-start | bytes 786440 | tf_op jit(solution)/shard_map/report_swap/ppermute | solution.py:30
  161.2 14.7 %collective-permute-start.11 = (bf16[64,1024]{1,0:T(8,128)(2,1)S(1)}, bf16[64,1024]{1,0:T(8,128)(2,1)S(1)}, u32[]{:S(2)}, u32[]{:S(2)}) collective-permute-start(bf16[64,1024]{1,0:T(8,128)(2,1)S(1)} %copy-done.7), channel_id=1, source_target_pairs={{0,1},{1,0},{2,3},{3,2},{4,5},{5,4},{6,7},{7,6},{8,9},{9,8},{10,11... | collective-permute-start | bytes 393224 | tf_op jit(solution)/shard_map/report_swap/ppermute | solution.py:30
  163.7 12.2 %collective-permute-start.12 = (bf16[64,1024]{1,0:T(8,128)(2,1)S(1)}, bf16[64,1024]{1,0:T(8,128)(2,1)S(1)}, u32[]{:S(2)}, u32[]{:S(2)}) collective-permute-start(bf16[64,1024]{1,0:T(8,128)(2,1)S(1)} %copy-done.5), channel_id=1, source_target_pairs={{0,1},{1,0},{2,3},{3,2},{4,5},{5,4},{6,7},{7,6},{8,9},{9,8},{10,11... | collective-permute-start | bytes 393224 | tf_op jit(solution)/shard_map/report_swap/ppermute | solution.py:30

commit v4 on v3

v4 whole, which is shorter than its diff:
```python
import jax
import jax.numpy as jnp
from jax import lax
from jax.experimental import pallas as pl
from jax.experimental.pallas import tpu as pltpu
from jax.sharding import Mesh, PartitionSpec as P

EPSILON = 1e-06
ROWS = 128
WIDTH = 1024
BLOCKS = 512
AXES = ("zl", "x", "y", "zh", "c")
LIMIT = 40 * 1024 * 1024
WINDOW_FLOPS = 4 * ROWS * 8 * ROWS * WIDTH
CAPTION_FLOPS = 65 * WINDOW_FLOPS
PICTURE_FLOPS = 1 * WINDOW_FLOPS
HEAD_FLOPS = 2 * 2048 * 1024 * 256


def moved(value, target_of):
    return lax.ppermute(value, AXES, [(r, target_of(r) % BLOCKS) for r in range(BLOCKS)])


def moved_by(value, steps):
    return moved(value, lambda r: r + steps)


def swapped(value):
    return lax.ppermute(value, "c", [(0, 1), (1, 0)])


def beside(value, parity, steps):
    pairs = [(r, (r + steps) % BLOCKS) for r in range(parity, BLOCKS, 2)]
    return lax.ppermute(value, AXES, pairs)


def after(value, *others):
    return lax.optimization_barrier((value, *others))[0]


def low_rows(wide):
    inverse = 1.0 / jnp.sqrt(jnp.sum(wide * wide, axis=-1, keepdims=True) + EPSILON)
    return (wide * inverse).astype(jnp.bfloat16)


def unit_rows(own):
    wide = own[...].astype(jnp.float32)
    length = jnp.sqrt(jnp.sum(wide * wide, axis=-1, keepdims=True) + EPSILON)
    return wide / length, length


def slopes(scalars, rows, blocks):
    logits = lax.dot_general(
        rows.astype(jnp.bfloat16), blocks, (((1,), (1,)), ((), ())), preferred_element_type=jnp.float32
    )
    return scalars[0] * logits + scalars[1]


def window_sums(scalars, match, use_beside, own, other, blocks, beside, mine, theirs, low):
    start = 0
    for ref in blocks:
        rows = ref.shape[0]
        low[start : start + rows, :] = low_rows(ref[...].astype(jnp.float32))
        start += rows
    last = jnp.where(use_beside, beside[...].astype(jnp.float32), blocks[0][...].astype(jnp.float32))
    low[start : start + ROWS, :] = low_rows(last)
    unit, _ = unit_rows(own)
    logits = slopes(scalars, unit, low[:512, :])
    target = jnp.where(match, 1.0, -1.0)
    first = -target * jax.nn.sigmoid(-target * logits[:, :ROWS])
    slope = jnp.concatenate([first, jax.nn.sigmoid(logits[:, ROWS:])], axis=1)
    mine[...] = jnp.dot(
        slope.astype(jnp.bfloat16), low[:512, :], preferred_element_type=jnp.float32
    )
    unit, _ = unit_rows(other)
    slope = jax.nn.sigmoid(slopes(scalars, unit, low[ROWS:, :]))
    theirs[...] = jnp.dot(
        slope.astype(jnp.bfloat16), low[ROWS:, :], preferred_element_type=jnp.float32
    )


def caption_kernel(scalars, place, pair_row, own, other, *refs):
    *blocks, beside, mine, theirs, low = refs
    rows = lax.broadcasted_iota(jnp.int32, (ROWS, ROWS), 0)
    match = rows == lax.rem(pair_row[...], ROWS)
    window_sums(scalars, match, place[0] == 0, own, other, blocks, beside, mine, theirs, low)


def picture_kernel(scalars, place, pair_column, own, other, *refs):
    *blocks, beside, mine, theirs, low = refs
    columns = lax.broadcasted_iota(jnp.int32, (ROWS, ROWS), 1)
    match = columns == lax.rem(pair_column[...], ROWS)
    window_sums(scalars, match, place[0] == 1, own, other, blocks, beside, mine, theirs, low)


def window_call(body, flops, *args):
    vmem = pl.BlockSpec(memory_space=pltpu.VMEM)
    half = jax.ShapeDtypeStruct((ROWS, WIDTH), jnp.float32)
    return pl.pallas_call(
        body,
        out_shape=(half, half),
        in_specs=[pl.BlockSpec(memory_space=pltpu.SMEM)] * 2 + [vmem] * (len(args) - 2),
        out_specs=(vmem, vmem),
        scratch_shapes=[pltpu.VMEM((5 * ROWS, WIDTH), jnp.bfloat16)],
        compiler_params=pltpu.CompilerParams(vmem_limit_bytes=LIMIT),
        cost_estimate=pl.CostEstimate(
            flops=flops, bytes_accessed=4_000_000, transcendentals=ROWS * 1024
        ),
    )(*args)


def finish_kernel(scalars, own, mine, received, out, *spread):
    unit, length = unit_rows(own)
    total = scalars[0] * (mine[...] + received[...])
    grad = (total - unit * jnp.sum(unit * total, axis=-1, keepdims=True)) / length
    grad = grad.astype(jnp.bfloat16)
    out[...] = grad
    for ref in spread:
        for x in range(4):
            for y in range(4):
                row = (x * 4 + y) * ROWS
                ref[row : row + ROWS, :] = grad[:, y * 256 : (y + 1) * 256]


def finish_call(outs, *args):
    vmem = pl.BlockSpec(memory_space=pltpu.VMEM)
    return pl.pallas_call(
        finish_kernel,
        out_shape=outs,
        in_specs=[pl.BlockSpec(memory_space=pltpu.SMEM)] + [vmem] * 3,
        out_specs=tuple([vmem] * len(outs)),
        compiler_params=pltpu.CompilerParams(vmem_limit_bytes=LIMIT),
        cost_estimate=pl.CostEstimate(flops=0, bytes_accessed=1_500_000, transcendentals=0),
    )(*args)


def head_kernel(place, caps, feats, keep, give, table):
    c = place[0]
    total = lax.dot_general(
        caps[...], feats[...], (((0,), (0,)), ((), ())), preferred_element_type=jnp.float32
    )
    table[...] = total.T
    for zl in range(4):
        for zh in range(4):
            for y in range(4):
                base = zl * 256 + y * 64 + zh * 16
                to = (zl * 16 + zh * 4 + y) * 8
                keep[to : to + 8, :] = table[pl.ds(pl.multiple_of(base + c * 8, 8), 8), :]
                give[to : to + 8, :] = table[pl.ds(pl.multiple_of(base + 8 - c * 8, 8), 8), :]


def head_call(place, caps, feats):
    vmem = pl.BlockSpec(memory_space=pltpu.VMEM)
    half = jax.ShapeDtypeStruct((512, 256), jnp.float32)
    return pl.pallas_call(
        head_kernel,
        out_shape=(half, half),
        in_specs=[pl.BlockSpec(memory_space=pltpu.SMEM)] + [vmem] * 2,
        out_specs=(vmem, vmem),
        scratch_shapes=[pltpu.VMEM((1024, 256), jnp.float32)],
        compiler_params=pltpu.CompilerParams(vmem_limit_bytes=LIMIT),
        cost_estimate=pl.CostEstimate(
            flops=HEAD_FLOPS, bytes_accessed=6_000_000, transcendentals=0
        ),
    )(place, caps, feats)


def columns_kernel(feats, out):
    for x in range(4):
        for zl in range(4):
            piece = feats[:, zl * 1024 + x * 256 : zl * 1024 + x * 256 + 256]
            for y in range(4):
                row = (x * 4 + y) * ROWS
                out[row : row + ROWS, zl * 256 : zl * 256 + 256] = piece


def columns_call(feats):
    vmem = pl.BlockSpec(memory_space=pltpu.VMEM)
    return pl.pallas_call(
        columns_kernel,
        out_shape=jax.ShapeDtypeStruct((16 * ROWS, WIDTH), jnp.bfloat16),
        in_specs=[vmem],
        out_specs=vmem,
        compiler_params=pltpu.CompilerParams(vmem_limit_bytes=LIMIT),
        cost_estimate=pl.CostEstimate(flops=0, bytes_accessed=5_000_000, transcendentals=0),
    )(feats)


def on_device(image_proj, report_proj, report_feats, pair_index, natural_log_factor, logit_bias):
    scalars = jnp.concatenate([jnp.exp(natural_log_factor), logit_bias])
    place = lax.axis_index("c").astype(jnp.int32).reshape(1)

    with jax.named_scope("image_near"):
        image_1 = moved_by(image_proj, -2)
    with jax.named_scope("image_far"):
        image_3 = moved_by(image_proj, -6)
    with jax.named_scope("image_beside"):
        image_beside = beside(image_proj, 0, -8)
    with jax.named_scope("core_swap"):
        image_other = swapped(image_proj)
        report_other = after(swapped(report_proj), image_other)

    with jax.named_scope("feats"):
        feats = lax.all_to_all(
            columns_call(report_feats), ("x", "y"), split_axis=0, concat_axis=0, tiled=True
        )

    with jax.named_scope("image_relay_near"):
        image_2a = moved_by(image_1[:64], -2)
    with jax.named_scope("image_relay_far"):
        image_2b = moved_by(image_3[64:], 2)
    with jax.named_scope("caption_kernel"):
        caption_mine, caption_theirs = window_call(
            caption_kernel,
            CAPTION_FLOPS,
            scalars,
            place,
            pair_index.reshape(1, ROWS),
            report_proj,
            report_other,
            image_proj,
            image_1,
            image_2a,
            image_2b,
            image_3,
            image_beside,
        )
    report_late = after(report_proj, image_1, image_3)
    with jax.named_scope("report_near"):
        report_1 = moved_by(report_late, 2)
    with jax.named_scope("report_far"):
        report_3 = moved_by(report_late, 6)
    with jax.named_scope("caption_swap"):
        caption_received = swapped(after(caption_theirs, report_1, report_3))
    with jax.named_scope("caption_finish"):
        caption_grad, caption_spread = finish_call(
            (
                jax.ShapeDtypeStruct((ROWS, WIDTH), jnp.bfloat16),
                jax.ShapeDtypeStruct((16 * ROWS, 256), jnp.bfloat16),
            ),
            scalars,
            report_proj,
            caption_mine,
            caption_received,
        )
    with jax.named_scope("report_relay_near"):
        report_2a = moved_by(report_1[:64], 2)
    with jax.named_scope("report_relay_far"):
        report_2b = moved_by(report_3[64:], -2)
    with jax.named_scope("report_beside"):
        report_beside = beside(report_late, 1, 8)
    with jax.named_scope("picture_kernel"):
        picture_mine, picture_theirs = window_call(
            picture_kernel,
            PICTURE_FLOPS,
            scalars,
            place,
            pair_index.reshape(ROWS, 1),
            image_proj,
            image_other,
            report_proj,
            report_1,
            report_2a,
            report_2b,
            report_3,
            report_beside,
        )
    with jax.named_scope("picture_swap"):
        picture_received = swapped(picture_theirs)
    with jax.named_scope("picture_finish"):
        (picture_grad,) = finish_call(
            (jax.ShapeDtypeStruct((ROWS, WIDTH), jnp.bfloat16),),
            scalars,
            image_proj,
            picture_mine,
            picture_received,
        )

    with jax.named_scope("captions"):
        caps = lax.all_to_all(
            after(caption_spread, feats),
            ("x", "y"),
            split_axis=0,
            concat_axis=0,
            tiled=True,
        )
    with jax.named_scope("head_kernel"):
        keep, give = head_call(place, after(caps, report_2a, report_2b, report_beside), feats)
    with jax.named_scope("head_swap"):
        part = (keep + swapped(give)).astype(jnp.bfloat16)
    with jax.named_scope("head_sum"):
        parts = lax.all_to_all(part, ("zl", "zh", "y"), split_axis=0, concat_axis=0, tiled=True)
        head = jnp.sum(parts.reshape(16, 4, 8, 256).astype(jnp.float32), axis=0)
        head_grad = head.transpose(1, 0, 2).reshape(8, WIDTH)
    return (picture_grad, caption_grad, head_grad)


def solution(mesh):
    fine = Mesh(mesh.devices.reshape(4, 4, 4, 4, 2), AXES)
    rows = P(AXES, None)
    return jax.shard_map(
        on_device,
        mesh=fine,
        in_specs=(rows, rows, rows, P(AXES), P(), P()),
        out_specs=(rows, rows, rows),
        check_vma=False,
    )
```

time: 181 us -> 178 us (0.983)
  the two profiles are of different devices: /device:TPU:128 before, /device:TPU:32 now
where the time goes in v4:
time: 178 us; the launch traced here: 177 us
  starting transfers between devices  87.3 us (49%)
  waiting for transfers between devices  70.8 us (40%)
  Pallas kernels  12.1 us (7%)
  local copies, waits for them, and re-layouts  3.4 us (2%)
  between operations  2.24 us (1%)
    ppermute x8, starting transfers between devices, moved(): lax.ppermute(value, AXES, [(r, target_of(r) % BLOCKS) for r in range(BLOC...  53.5 us
    ppermute x8, waiting for transfers between devices, moved(): lax.ppermute(value, AXES, [(r, target_of(r) % BLOCKS) for r in range(BLOC...  49.8 us
    all_to_all x1, waiting for transfers between devices, on_device(): lax.all_to_all(part, ('zl', 'zh', 'y'), split_axis=0, concat_axis=0, tile...  15.1 us
    all_to_all x1, starting transfers between devices, on_device(): lax.all_to_all(after(caption_spread, feats), ('x', 'y'), split_axis=0, co...  10.5 us
    ppermute x5, starting transfers between devices, swapped(): return lax.ppermute(value, 'c', [(0, 1), (1, 0)])  10.1 us
    ppermute x5, waiting for transfers between devices, swapped(): return lax.ppermute(value, 'c', [(0, 1), (1, 0)])  5.63 us
    all_to_all x1, starting transfers between devices, on_device(): lax.all_to_all(part, ('zl', 'zh', 'y'), split_axis=0, concat_axis=0, tile...  5.29 us
    all_to_all x1, starting transfers between devices, on_device(): lax.all_to_all(columns_call(report_feats), ('x', 'y'), split_axis=0, conc...  4.67 us
  transfers between devices with their start and end apart: 18, of which 11 were waited for; matrix products, arithmetic and copies ran while one was open for 0% of the time, Pallas kernels for 5%

profile of v4, /device:TPU:32, one launch (start us, length us, event | category | flops | bytes accessed | tf_op | source)
XLA Modules:
  0.0 177.4 jit_solution(14565320745038985701)
XLA Ops:
  0.6 12.4 %collective-permute-start.2 = (bf16[128,1024]{1,0:T(8,128)(2,1)}, bf16[128,1024]{1,0:T(8,128)(2,1)S(1)}, u32[]{:S(2)}, u32[]{:S(2)}) collective-permute-start(bf16[128,1024]{1,0:T(8,128)(2,1)} %refs_0_.3), channel_id=1, source_target_pairs={{0,506},{1,507},{2,508},{3,509},{4,510},{5,511},{6,0},{7,1},{8,2},... | collective-permute-start | bytes 786440 | tf_op jit(solution)/shard_map/image_far/ppermute | solution.py:21
  13.0 6.5 %collective-permute-start.1 = (bf16[128,1024]{1,0:T(8,128)(2,1)}, bf16[128,1024]{1,0:T(8,128)(2,1)S(1)}, u32[]{:S(2)}, u32[]{:S(2)}) collective-permute-start(bf16[128,1024]{1,0:T(8,128)(2,1)} %refs_0_.3), channel_id=1, source_target_pairs={{0,510},{1,511},{2,0},{3,1},{4,2},{5,3},{6,4},{7,5},{8,6},{9,7},{1... | collective-permute-start | bytes 786440 | tf_op jit(solution)/shard_map/image_near/ppermute | solution.py:21
  19.5 1.9 %collective-permute-start.9 = (bf16[128,1024]{1,0:T(8,128)(2,1)}, bf16[128,1024]{1,0:T(8,128)(2,1)S(1)}, u32[]{:S(2)}, u32[]{:S(2)}) collective-permute-start(bf16[128,1024]{1,0:T(8,128)(2,1)} %own.7), channel_id=1, source_target_pairs={{0,1},{1,0},{2,3},{3,2},{4,5},{5,4},{6,7},{7,6},{8,9},{9,8},{10,11... | collective-permute-start | bytes 786440 | tf_op jit(solution)/shard_map/core_swap/ppermute | solution.py:29
  21.4 2.4 %collective-permute-start = (bf16[128,1024]{1,0:T(8,128)(2,1)}, bf16[128,1024]{1,0:T(8,128)(2,1)S(1)}, u32[]{:S(2)}, u32[]{:S(2)}) collective-permute-start(bf16[128,1024]{1,0:T(8,128)(2,1)} %refs_0_.3), channel_id=1, source_target_pairs={{0,1},{1,0},{2,3},{3,2},{4,5},{5,4},{6,7},{7,6},{8,9},{9,8},{10,11... | collective-permute-start | bytes 786440 | tf_op jit(solution)/shard_map/core_swap/ppermute | solution.py:29
  23.8 2.7 %collective-permute-start.12 = (bf16[128,1024]{1,0:T(8,128)(2,1)}, bf16[128,1024]{1,0:T(8,128)(2,1)S(1)}, u32[]{:S(2)}, u32[]{:S(2)}) collective-permute-start(bf16[128,1024]{1,0:T(8,128)(2,1)} %refs_0_.3), channel_id=1, source_target_pairs={{0,504},{2,506},{4,508},{6,510},{8,0},{10,2},{12,4},{14,6},{16,8},... | collective-permute-start | bytes 786440 | tf_op jit(solution)/shard_map/image_beside/ppermute | solution.py:34
  26.5 1.2 copy-done.1
  27.7 0.5 feats.2
  28.3 2.0 %copy-done = bf16[2048,1024]{1,0:T(8,128)(2,1)} copy-done((bf16[2048,1024]{1,0:T(8,128)(2,1)}, bf16[2048,1024]{1,0:T(8,128)(2,1)S(1)}, u32[]{:S(2)}) %copy-start) | copy-done | bytes 4194328
  30.3 4.7 %all-to-all-start = ((bf16[16,128,1024]{2,1,0:T(8,128)(2,1)}), bf16[16,128,1024]{2,1,0:T(8,128)(2,1)}, u32[]{:S(2)}, u32[]{:S(2)}) async-start(bf16[16,128,1024]{2,1,0:T(8,128)(2,1)} %bitcast.14), calls=%async_computation | async-start | bytes 8388608 | tf_op jit(solution)/shard_map/feats/all_to_all | solution.py:204
  35.0 0.0 collective-permute-done.2.refs_4_
  35.0 5.5 %collective-permute-start.11 = (bf16[64,1024]{1,0:T(8,128)(2,1)S(1)}, bf16[64,1024]{1,0:T(8,128)(2,1)S(1)}, u32[]{:S(2)}, u32[]{:S(2)}) collective-permute-start(bf16[64,1024]{1,0:T(8,128)(2,1)S(1)} %slice.19), channel_id=1, source_target_pairs={{0,2},{1,3},{2,4},{3,5},{4,6},{5,7},{6,8},{7,9},{8,10},{9,11},{10,... | collective-permute-start | bytes 393224 | tf_op jit(solution)/shard_map/image_relay_far/ppermute | solution.py:21
  40.5 0.6 collective-permute-done.1.refs_1_
  41.1 15.6 %collective-permute-start.10 = (bf16[64,1024]{1,0:T(8,128)(2,1)S(1)}, bf16[64,1024]{1,0:T(8,128)(2,1)S(1)}, u32[]{:S(2)}, u32[]{:S(2)}) collective-permute-start(bf16[64,1024]{1,0:T(8,128)(2,1)S(1)} %slice.18), channel_id=1, source_target_pairs={{0,510},{1,511},{2,0},{3,1},{4,2},{5,3},{6,4},{7,5},{8,6},{9,7},{1... | collective-permute-start | bytes 393224 | tf_op jit(solution)/shard_map/image_relay_near/ppermute | solution.py:21
  58.0 0.1 pad_maximum_fusion.scalars
  58.1 0.0 collective-permute-done.9.other
  58.1 1.9 %collective-permute-start.5 = (bf16[128,1024]{1,0:T(8,128)(2,1)S(1)}, bf16[128,1024]{1,0:T(8,128)(2,1)S(1)}, u32[]{:S(2)}, u32[]{:S(2)}) collective-permute-start(bf16[128,1024]{1,0:T(8,128)(2,1)S(1)} %copy-done.2), channel_id=1, source_target_pairs={{0,6},{1,7},{2,8},{3,9},{4,10},{5,11},{6,12},{7,13},{8,14},{9,15},... | collective-permute-start | bytes 786440 | tf_op jit(solution)/shard_map/report_far/ppermute | solution.py:21
  60.0 0.0 collective-permute-done.other
  60.0 1.9 %collective-permute-start.3 = (bf16[128,1024]{1,0:T(8,128)(2,1)S(1)}, bf16[128,1024]{1,0:T(8,128)(2,1)S(1)}, u32[]{:S(2)}, u32[]{:S(2)}) collective-permute-start(bf16[128,1024]{1,0:T(8,128)(2,1)S(1)} %copy-done.2), channel_id=1, source_target_pairs={{0,2},{1,3},{2,4},{3,5},{4,6},{5,7},{6,8},{7,9},{8,10},{9,11},{10,... | collective-permute-start | bytes 786440 | tf_op jit(solution)/shard_map/report_near/ppermute | solution.py:21
  61.9 0.0 collective-permute-done.12.refs_5_
  61.9 0.0 collective-permute-done.11.refs_3_
  61.9 9.0 %collective-permute-done.10.refs_2_ = bf16[64,1024]{1,0:T(8,128)(2,1)S(1)} collective-permute-done((bf16[64,1024]{1,0:T(8,128)(2,1)S(1)}, bf16[64,1024]{1,0:T(8,128)(2,1)S(1)}, u32[]{:S(2)}, u32[]{:S(2)}) %collective-permute-start.10) | collective-permute-done | bytes 131104 | tf_op jit(solution)/shard_map/image_relay_near/ppermute | solution.py:21
  71.0 2.2 %caption_kernel.1 = (f32[128,1024]{1,0:T(8,128)S(1)}, f32[128,1024]{1,0:T(8,128)S(1)}) custom-call(f32[2]{0:T(128)S(1)} %pad_maximum_fusion.scalars, s32[1]{0:T(128)} %bitcast.place, s32[1,128]{1,0:T(1,128)S(1)} %bitcast.16, bf16[128,1024]{1,0:T(8,128)(2,1)S(1)} %copy-done.2, bf16[128,1024]{1,0:T(8,128)(2,1)S(1)} %collective-permute-done.9.other, ...), custom_call_target="tpu_custom_call" | custom-call | flops 34896609280 | bytes 4000000 | tf_op jit(solution)/shard_map/caption_kernel/pallas_call | solution.py:99
  73.1 26.3 %collective-permute-done.5.refs_4_ = bf16[128,1024]{1,0:T(8,128)(2,1)S(1)} collective-permute-done((bf16[128,1024]{1,0:T(8,128)(2,1)S(1)}, bf16[128,1024]{1,0:T(8,128)(2,1)S(1)}, u32[]{:S(2)}, u32[]{:S(2)}) %collective-permute-start.5) | collective-permute-done | bytes 262176 | tf_op jit(solution)/shard_map/report_far/ppermute | solution.py:21
  99.4 0.9 collective-permute-done.3.refs_1_
  100.4 1.9 %collective-permute-start.13 = (f32[128,1024]{1,0:T(8,128)S(1)}, f32[128,1024]{1,0:T(8,128)S(1)}, u32[]{:S(2)}, u32[]{:S(2)}) collective-permute-start(f32[128,1024]{1,0:T(8,128)S(1)} %get-tuple-element.22), channel_id=1, source_target_pairs={{0,1},{1,0},{2,3},{3,2},{4,5},{5,4},{6,7},{7,6},{8,9},{9,8},{10,11... | collective-permute-start | bytes 1572872 | tf_op jit(solution)/shard_map/caption_swap/ppermute | solution.py:29
  102.3 1.9 %collective-permute-done.13.received = f32[128,1024]{1,0:T(8,128)S(1)} collective-permute-done((f32[128,1024]{1,0:T(8,128)S(1)}, f32[128,1024]{1,0:T(8,128)S(1)}, u32[]{:S(2)}, u32[]{:S(2)}) %collective-permute-start.13) | collective-permute-done | bytes 524320 | tf_op jit(solution)/shard_map/caption_swap/ppermute | solution.py:29
  104.2 2.0 %caption_finish.1 = (bf16[128,1024]{1,0:T(8,128)(2,1)}, bf16[2048,256]{1,0:T(8,128)(2,1)}) custom-call(f32[2]{0:T(128)S(1)} %pad_maximum_fusion.scalars, bf16[128,1024]{1,0:T(8,128)(2,1)S(1)} %copy-done.2, f32[128,1024]{1,0:T(8,128)S(1)} %get-tuple-element.20.mine, f32[128,1024]{1,0:T(8,128)S(1)} %collective-permute-done.13.received), custom_call_target="tpu_custom_call" | custom-call | bytes 1500000 | tf_op jit(solution)/shard_map/caption_finish/pallas_call | solution.py:127
  106.2 0.3 all-to-all-done
  106.5 10.5 %all-to-all-start.1 = ((bf16[16,128,256]{2,1,0:T(8,128)(2,1)}), bf16[16,128,256]{2,1,0:T(8,128)(2,1)S(1)}, u32[]{:S(2)}, u32[]{:S(2)}) async-start(bf16[16,128,256]{2,1,0:T(8,128)(2,1)} %bitcast.5), calls=%async_computation.1 | async-start | bytes 2097152 | tf_op jit(solution)/shard_map/captions/all_to_all | solution.py:280
  117.0 0.7 collective-permute-start.7
  117.7 1.9 %collective-permute-start.6 = (bf16[64,1024]{1,0:T(8,128)(2,1)S(1)}, bf16[64,1024]{1,0:T(8,128)(2,1)S(1)}, u32[]{:S(2)}, u32[]{:S(2)}) collective-permute-start(bf16[64,1024]{1,0:T(8,128)(2,1)S(1)} %slice.17), channel_id=1, source_target_pairs={{0,510},{1,511},{2,0},{3,1},{4,2},{5,3},{6,4},{7,5},{8,6},{9,7},{1... | collective-permute-start | bytes 393224 | tf_op jit(solution)/shard_map/report_relay_far/ppermute | solution.py:21
  119.6 7.8 %collective-permute-start.4 = (bf16[64,1024]{1,0:T(8,128)(2,1)S(1)}, bf16[64,1024]{1,0:T(8,128)(2,1)S(1)}, u32[]{:S(2)}, u32[]{:S(2)}) collective-permute-start(bf16[64,1024]{1,0:T(8,128)(2,1)S(1)} %slice.16), channel_id=1, source_target_pairs={{0,2},{1,3},{2,4},{3,5},{4,6},{5,7},{6,8},{7,9},{8,10},{9,11},{10,... | collective-permute-start | bytes 393224 | tf_op jit(solution)/shard_map/report_relay_near/ppermute | solution.py:21
  127.5 0.0 collective-permute-done.7.refs_5_
  127.5 3.9 %collective-permute-done.6.refs_3_ = bf16[64,1024]{1,0:T(8,128)(2,1)S(1)} collective-permute-done((bf16[64,1024]{1,0:T(8,128)(2,1)S(1)}, bf16[64,1024]{1,0:T(8,128)(2,1)S(1)}, u32[]{:S(2)}, u32[]{:S(2)}) %collective-permute-start.6) | collective-permute-done | bytes 131104 | tf_op jit(solution)/shard_map/report_relay_far/ppermute | solution.py:21
  131.4 9.0 %collective-permute-done.4.refs_2_ = bf16[64,1024]{1,0:T(8,128)(2,1)S(1)} collective-permute-done((bf16[64,1024]{1,0:T(8,128)(2,1)S(1)}, bf16[64,1024]{1,0:T(8,128)(2,1)S(1)}, u32[]{:S(2)}, u32[]{:S(2)}) %collective-permute-start.4) | collective-permute-done | bytes 131104 | tf_op jit(solution)/shard_map/report_relay_near/ppermute | solution.py:21
  140.4 0.0 all-to-all-done.1
  140.4 3.7 %head_kernel.1 = (f32[512,256]{1,0:T(8,128)S(1)}, f32[512,256]{1,0:T(8,128)S(1)}) custom-call(s32[1]{0:T(128)} %bitcast.place, bf16[2048,256]{1,0:T(8,128)(2,1)S(1)} %bitcast.15, bf16[2048,1024]{1,0:T(8,128)(2,1)} %bitcast.4.feats), custom_call_target="tpu_custom_call" | custom-call | flops 1073741824 | bytes 6000000 | tf_op jit(solution)/shard_map/head_kernel/pallas_call | solution.py:155
  144.1 1.9 %collective-permute-start.14 = (f32[512,256]{1,0:T(8,128)S(1)}, f32[512,256]{1,0:T(8,128)S(1)}, u32[]{:S(2)}, u32[]{:S(2)}) collective-permute-start(f32[512,256]{1,0:T(8,128)S(1)} %get-tuple-element.28), channel_id=1, source_target_pairs={{0,1},{1,0},{2,3},{3,2},{4,5},{5,4},{6,7},{7,6},{8,9},{9,8},{10,11... | collective-permute-start | bytes 1572872 | tf_op jit(solution)/shard_map/head_swap/ppermute | solution.py:29
  146.0 1.9 %collective-permute-done.14 = f32[512,256]{1,0:T(8,128)S(1)} collective-permute-done((f32[512,256]{1,0:T(8,128)S(1)}, f32[512,256]{1,0:T(8,128)S(1)}, u32[]{:S(2)}, u32[]{:S(2)}) %collective-permute-start.14) | collective-permute-done | bytes 524320 | tf_op jit(solution)/shard_map/head_swap/ppermute | solution.py:29
  147.9 0.7 fusion
  148.7 5.3 %all-to-all-start.2 = ((bf16[64,8,256]{2,1,0:T(8,128)(2,1)}), bf16[64,8,256]{2,1,0:T(8,128)(2,1)S(1)}, u32[]{:S(2)}, u32[]{:S(2)}) async-start(bf16[64,8,256]{2,1,0:T(8,128)(2,1)} %fusion), calls=%async_computation.2 | async-start | bytes 524288 | tf_op jit(solution)/shard_map/head_sum/all_to_all | solution.py:292
  154.0 0.1 copy.9.pair_column
  154.1 2.2 %picture_kernel.1 = (f32[128,1024]{1,0:T(8,128)S(1)}, f32[128,1024]{1,0:T(8,128)S(1)}) custom-call(f32[2]{0:T(128)S(1)} %pad_maximum_fusion.scalars, s32[1]{0:T(128)} %bitcast.place, s32[128,1]{1,0:T(8,128)S(1)} %copy.9.pair_column, bf16[128,1024]{1,0:T(8,128)(2,1)S(1)} %copy-done.3, bf16[128,1024]{1,0:T(8,128)(2,1)S(1)} %collective-permute-done.other, ...), custom_call_target="tpu_custom_call" | custom-call | flops 536870912 | bytes 4000000 | tf_op jit(solution)/shard_map/picture_kernel/pallas_call | solution.py:99
  156.3 1.9 %collective-permute-start.8 = (f32[128,1024]{1,0:T(8,128)S(1)}, f32[128,1024]{1,0:T(8,128)S(1)}, u32[]{:S(2)}, u32[]{:S(2)}) collective-permute-start(f32[128,1024]{1,0:T(8,128)S(1)} %get-tuple-element.18), channel_id=1, source_target_pairs={{0,1},{1,0},{2,3},{3,2},{4,5},{5,4},{6,7},{7,6},{8,9},{9,8},{10,11... | collective-permute-start | bytes 1572872 | tf_op jit(solution)/shard_map/picture_swap/ppermute | solution.py:29
  158.2 1.9 %collective-permute-done.8.received = f32[128,1024]{1,0:T(8,128)S(1)} collective-permute-done((f32[128,1024]{1,0:T(8,128)S(1)}, f32[128,1024]{1,0:T(8,128)S(1)}, u32[]{:S(2)}, u32[]{:S(2)}) %collective-permute-start.8) | collective-permute-done | bytes 524320 | tf_op jit(solution)/shard_map/picture_swap/ppermute | solution.py:29
  160.1 1.5 picture_finish.1
  161.6 15.1 %all-to-all-done.2 = bf16[64,8,256]{2,1,0:T(8,128)(2,1)S(1)} async-done(((bf16[64,8,256]{2,1,0:T(8,128)(2,1)}), bf16[64,8,256]{2,1,0:T(8,128)(2,1)S(1)}, u32[]{:S(2)}, u32[]{:S(2)}) %all-to-all-start.2) | async-done | bytes 262176 | tf_op jit(solution)/shard_map/head_sum/all_to_all | solution.py:292
  176.7 0.7 convert_reduce_fusion
  (12 shorter events, 0.1 us)
Async XLA Ops:
  0.6 34.3 %collective-permute-start.2 = (bf16[128,1024]{1,0:T(8,128)(2,1)}, bf16[128,1024]{1,0:T(8,128)(2,1)S(1)}, u32[]{:S(2)}, u32[]{:S(2)}) collective-permute-start(bf16[128,1024]{1,0:T(8,128)(2,1)} %refs_0_.3), channel_id=1, source_target_pairs={{0,506},{1,507},{2,508},{3,509},{4,510},{5,511},{6,0},{7,1},{8,2},... | collective-permute-start | bytes 786440 | tf_op jit(solution)/shard_map/image_far/ppermute | solution.py:21
  13.0 28.0 %collective-permute-start.1 = (bf16[128,1024]{1,0:T(8,128)(2,1)}, bf16[128,1024]{1,0:T(8,128)(2,1)S(1)}, u32[]{:S(2)}, u32[]{:S(2)}) collective-permute-start(bf16[128,1024]{1,0:T(8,128)(2,1)} %refs_0_.3), channel_id=1, source_target_pairs={{0,510},{1,511},{2,0},{3,1},{4,2},{5,3},{6,4},{7,5},{8,6},{9,7},{1... | collective-permute-start | bytes 786440 | tf_op jit(solution)/shard_map/image_near/ppermute | solution.py:21
  19.5 38.6 %collective-permute-start.9 = (bf16[128,1024]{1,0:T(8,128)(2,1)}, bf16[128,1024]{1,0:T(8,128)(2,1)S(1)}, u32[]{:S(2)}, u32[]{:S(2)}) collective-permute-start(bf16[128,1024]{1,0:T(8,128)(2,1)} %own.7), channel_id=1, source_target_pairs={{0,1},{1,0},{2,3},{3,2},{4,5},{5,4},{6,7},{7,6},{8,9},{9,8},{10,11... | collective-permute-start | bytes 786440 | tf_op jit(solution)/shard_map/core_swap/ppermute | solution.py:29
  21.4 38.6 %collective-permute-start = (bf16[128,1024]{1,0:T(8,128)(2,1)}, bf16[128,1024]{1,0:T(8,128)(2,1)S(1)}, u32[]{:S(2)}, u32[]{:S(2)}) collective-permute-start(bf16[128,1024]{1,0:T(8,128)(2,1)} %refs_0_.3), channel_id=1, source_target_pairs={{0,1},{1,0},{2,3},{3,2},{4,5},{5,4},{6,7},{7,6},{8,9},{9,8},{10,11... | collective-permute-start | bytes 786440 | tf_op jit(solution)/shard_map/core_swap/ppermute | solution.py:29
  23.8 38.1 %collective-permute-start.12 = (bf16[128,1024]{1,0:T(8,128)(2,1)}, bf16[128,1024]{1,0:T(8,128)(2,1)S(1)}, u32[]{:S(2)}, u32[]{:S(2)}) collective-permute-start(bf16[128,1024]{1,0:T(8,128)(2,1)} %refs_0_.3), channel_id=1, source_target_pairs={{0,504},{2,506},{4,508},{6,510},{8,0},{10,2},{12,4},{14,6},{16,8},... | collective-permute-start | bytes 786440 | tf_op jit(solution)/shard_map/image_beside/ppermute | solution.py:34
  26.5 1.2 copy-start.1
  28.2 2.0 %copy-start = (bf16[2048,1024]{1,0:T(8,128)(2,1)}, bf16[2048,1024]{1,0:T(8,128)(2,1)S(1)}, u32[]{:S(2)}) copy-start(bf16[2048,1024]{1,0:T(8,128)(2,1)S(1)} %feats.2) | copy-start | bytes 12582916
  30.3 27.8 %copy-start.2 = (bf16[128,1024]{1,0:T(8,128)(2,1)S(1)}, bf16[128,1024]{1,0:T(8,128)(2,1)}, u32[]{:S(2)}) copy-start(bf16[128,1024]{1,0:T(8,128)(2,1)} %own.7) | copy-start | bytes 786436
  30.3 40.7 %copy-start.3 = (bf16[128,1024]{1,0:T(8,128)(2,1)S(1)}, bf16[128,1024]{1,0:T(8,128)(2,1)}, u32[]{:S(2)}) copy-start(bf16[128,1024]{1,0:T(8,128)(2,1)} %refs_0_.3) | copy-start | bytes 786436
  30.3 40.7 %copy-start.4 = (s32[128]{0:T(128)S(1)}, s32[128]{0:T(128)}, u32[]{:S(2)}) copy-start(s32[128]{0:T(128)} %param.9) | copy-start | bytes 1540
  30.3 76.2 %all-to-all-start = ((bf16[16,128,1024]{2,1,0:T(8,128)(2,1)}), bf16[16,128,1024]{2,1,0:T(8,128)(2,1)}, u32[]{:S(2)}, u32[]{:S(2)}) async-start(bf16[16,128,1024]{2,1,0:T(8,128)(2,1)} %bitcast.14), calls=%async_computation | async-start | bytes 8388608 | tf_op jit(solution)/shard_map/feats/all_to_all | solution.py:204
  35.0 26.9 %collective-permute-start.11 = (bf16[64,1024]{1,0:T(8,128)(2,1)S(1)}, bf16[64,1024]{1,0:T(8,128)(2,1)S(1)}, u32[]{:S(2)}, u32[]{:S(2)}) collective-permute-start(bf16[64,1024]{1,0:T(8,128)(2,1)S(1)} %slice.19), channel_id=1, source_target_pairs={{0,2},{1,3},{2,4},{3,5},{4,6},{5,7},{6,8},{7,9},{8,10},{9,11},{10,... | collective-permute-start | bytes 393224 | tf_op jit(solution)/shard_map/image_relay_far/ppermute | solution.py:21
  41.1 29.9 %collective-permute-start.10 = (bf16[64,1024]{1,0:T(8,128)(2,1)S(1)}, bf16[64,1024]{1,0:T(8,128)(2,1)S(1)}, u32[]{:S(2)}, u32[]{:S(2)}) collective-permute-start(bf16[64,1024]{1,0:T(8,128)(2,1)S(1)} %slice.18), channel_id=1, source_target_pairs={{0,510},{1,511},{2,0},{3,1},{4,2},{5,3},{6,4},{7,5},{8,6},{9,7},{1... | collective-permute-start | bytes 393224 | tf_op jit(solution)/shard_map/image_relay_near/ppermute | solution.py:21
  58.1 41.4 %collective-permute-start.5 = (bf16[128,1024]{1,0:T(8,128)(2,1)S(1)}, bf16[128,1024]{1,0:T(8,128)(2,1)S(1)}, u32[]{:S(2)}, u32[]{:S(2)}) collective-permute-start(bf16[128,1024]{1,0:T(8,128)(2,1)S(1)} %copy-done.2), channel_id=1, source_target_pairs={{0,6},{1,7},{2,8},{3,9},{4,10},{5,11},{6,12},{7,13},{8,14},{9,15},... | collective-permute-start | bytes 786440 | tf_op jit(solution)/shard_map/report_far/ppermute | solution.py:21
  60.0 40.4 %collective-permute-start.3 = (bf16[128,1024]{1,0:T(8,128)(2,1)S(1)}, bf16[128,1024]{1,0:T(8,128)(2,1)S(1)}, u32[]{:S(2)}, u32[]{:S(2)}) collective-permute-start(bf16[128,1024]{1,0:T(8,128)(2,1)S(1)} %copy-done.2), channel_id=1, source_target_pairs={{0,2},{1,3},{2,4},{3,5},{4,6},{5,7},{6,8},{7,9},{8,10},{9,11},{10,... | collective-permute-start | bytes 786440 | tf_op jit(solution)/shard_map/report_near/ppermute | solution.py:21
  100.4 3.8 %collective-permute-start.13 = (f32[128,1024]{1,0:T(8,128)S(1)}, f32[128,1024]{1,0:T(8,128)S(1)}, u32[]{:S(2)}, u32[]{:S(2)}) collective-permute-start(f32[128,1024]{1,0:T(8,128)S(1)} %get-tuple-element.22), channel_id=1, source_target_pairs={{0,1},{1,0},{2,3},{3,2},{4,5},{5,4},{6,7},{7,6},{8,9},{9,8},{10,11... | collective-permute-start | bytes 1572872 | tf_op jit(solution)/shard_map/caption_swap/ppermute | solution.py:29
  106.5 33.9 %all-to-all-start.1 = ((bf16[16,128,256]{2,1,0:T(8,128)(2,1)}), bf16[16,128,256]{2,1,0:T(8,128)(2,1)S(1)}, u32[]{:S(2)}, u32[]{:S(2)}) async-start(bf16[16,128,256]{2,1,0:T(8,128)(2,1)} %bitcast.5), calls=%async_computation.1 | async-start | bytes 2097152 | tf_op jit(solution)/shard_map/captions/all_to_all | solution.py:280
  117.0 10.5 %collective-permute-start.7 = (bf16[128,1024]{1,0:T(8,128)(2,1)S(1)}, bf16[128,1024]{1,0:T(8,128)(2,1)S(1)}, u32[]{:S(2)}, u32[]{:S(2)}) collective-permute-start(bf16[128,1024]{1,0:T(8,128)(2,1)S(1)} %copy-done.2), channel_id=1, source_target_pairs={{1,9},{3,11},{5,13},{7,15},{9,17},{11,19},{13,21},{15,23},{17,25},... | collective-permute-start | bytes 786440 | tf_op jit(solution)/shard_map/report_beside/ppermute | solution.py:34
  117.7 13.7 %collective-permute-start.6 = (bf16[64,1024]{1,0:T(8,128)(2,1)S(1)}, bf16[64,1024]{1,0:T(8,128)(2,1)S(1)}, u32[]{:S(2)}, u32[]{:S(2)}) collective-permute-start(bf16[64,1024]{1,0:T(8,128)(2,1)S(1)} %slice.17), channel_id=1, source_target_pairs={{0,510},{1,511},{2,0},{3,1},{4,2},{5,3},{6,4},{7,5},{8,6},{9,7},{1... | collective-permute-start | bytes 393224 | tf_op jit(solution)/shard_map/report_relay_far/ppermute | solution.py:21
  119.6 20.8 %collective-permute-start.4 = (bf16[64,1024]{1,0:T(8,128)(2,1)S(1)}, bf16[64,1024]{1,0:T(8,128)(2,1)S(1)}, u32[]{:S(2)}, u32[]{:S(2)}) collective-permute-start(bf16[64,1024]{1,0:T(8,128)(2,1)S(1)} %slice.16), channel_id=1, source_target_pairs={{0,2},{1,3},{2,4},{3,5},{4,6},{5,7},{6,8},{7,9},{8,10},{9,11},{10,... | collective-permute-start | bytes 393224 | tf_op jit(solution)/shard_map/report_relay_near/ppermute | solution.py:21
  144.1 3.8 %collective-permute-start.14 = (f32[512,256]{1,0:T(8,128)S(1)}, f32[512,256]{1,0:T(8,128)S(1)}, u32[]{:S(2)}, u32[]{:S(2)}) collective-permute-start(f32[512,256]{1,0:T(8,128)S(1)} %get-tuple-element.28), channel_id=1, source_target_pairs={{0,1},{1,0},{2,3},{3,2},{4,5},{5,4},{6,7},{7,6},{8,9},{9,8},{10,11... | collective-permute-start | bytes 1572872 | tf_op jit(solution)/shard_map/head_swap/ppermute | solution.py:29
  148.7 28.1 %all-to-all-start.2 = ((bf16[64,8,256]{2,1,0:T(8,128)(2,1)}), bf16[64,8,256]{2,1,0:T(8,128)(2,1)S(1)}, u32[]{:S(2)}, u32[]{:S(2)}) async-start(bf16[64,8,256]{2,1,0:T(8,128)(2,1)} %fusion), calls=%async_computation.2 | async-start | bytes 524288 | tf_op jit(solution)/shard_map/head_sum/all_to_all | solution.py:292
  156.3 3.8 %collective-permute-start.8 = (f32[128,1024]{1,0:T(8,128)S(1)}, f32[128,1024]{1,0:T(8,128)S(1)}, u32[]{:S(2)}, u32[]{:S(2)}) collective-permute-start(f32[128,1024]{1,0:T(8,128)S(1)} %get-tuple-element.18), channel_id=1, source_target_pairs={{0,1},{1,0},{2,3},{3,2},{4,5},{5,4},{6,7},{7,6},{8,9},{9,8},{10,11... | collective-permute-start | bytes 1572872 | tf_op jit(solution)/shard_map/picture_swap/ppermute | solution.py:29

commit v5 on v4

--- a/solution.py
+++ b/solution.py
@@ -12,7 +12,8 @@
 AXES = ("zl", "x", "y", "zh", "c")
 LIMIT = 40 * 1024 * 1024
 WINDOW_FLOPS = 4 * ROWS * 8 * ROWS * WIDTH
-CAPTION_FLOPS = 65 * WINDOW_FLOPS
+CAPTION_FLOPS = 61 * WINDOW_FLOPS
+READY_FLOPS = 20 * WINDOW_FLOPS
 PICTURE_FLOPS = 1 * WINDOW_FLOPS
 HEAD_FLOPS = 2 * 2048 * 1024 * 256
 
@@ -134,7 +135,7 @@
     )(*args)
 
 
-def head_kernel(place, caps, feats, keep, give, table):
+def head_kernel(place, caps, feats, arrived, keep, give, table):
     c = place[0]
     total = lax.dot_general(
         caps[...], feats[...], (((0,), (0,)), ((), ())), preferred_element_type=jnp.float32
@@ -149,20 +150,35 @@
                 give[to : to + 8, :] = table[pl.ds(pl.multiple_of(base + 8 - c * 8, 8), 8), :]
 
 
-def head_call(place, caps, feats):
+def head_call(place, caps, feats, arrived):
     vmem = pl.BlockSpec(memory_space=pltpu.VMEM)
     half = jax.ShapeDtypeStruct((512, 256), jnp.float32)
     return pl.pallas_call(
         head_kernel,
         out_shape=(half, half),
-        in_specs=[pl.BlockSpec(memory_space=pltpu.SMEM)] + [vmem] * 2,
+        in_specs=[pl.BlockSpec(memory_space=pltpu.SMEM)] + [vmem] * 3,
         out_specs=(vmem, vmem),
         scratch_shapes=[pltpu.VMEM((1024, 256), jnp.float32)],
         compiler_params=pltpu.CompilerParams(vmem_limit_bytes=LIMIT),
         cost_estimate=pl.CostEstimate(
             flops=HEAD_FLOPS, bytes_accessed=6_000_000, transcendentals=0
         ),
-    )(place, caps, feats)
+    )(place, caps, feats, arrived)
+
+
+def ready_kernel(first, out):
+    out[...] = first[...].astype(jnp.float32)
+
+
+def ready(first):
+    return pl.pallas_call(
+        ready_kernel,
+        grid=(1,),
+        out_shape=jax.ShapeDtypeStruct((16, 128), jnp.float32),
+        in_specs=[pl.BlockSpec((16, 128), lambda i: (0, 0))],
+        out_specs=pl.BlockSpec((16, 128), lambda i: (0, 0)),
+        cost_estimate=pl.CostEstimate(flops=READY_FLOPS, bytes_accessed=16384, transcendentals=0),
+    )(first)
 
 
 def columns_kernel(feats, out):
@@ -197,12 +213,11 @@
     with jax.named_scope("image_beside"):
         image_beside = beside(image_proj, 0, -8)
     with jax.named_scope("core_swap"):
-        image_other = swapped(image_proj)
-        report_other = after(swapped(report_proj), image_other)
+        report_other = swapped(report_proj)
 
     with jax.named_scope("feats"):
         feats = lax.all_to_all(
-            columns_call(report_feats), ("x", "y"), split_axis=0, concat_axis=0, tiled=True
+            columns_call(after(report_feats, image_beside)), ("x", "y"), split_axis=0, concat_axis=0, tiled=True
         )
 
     with jax.named_scope("image_relay_near"):
@@ -243,12 +258,12 @@
             caption_mine,
             caption_received,
         )
-    with jax.named_scope("report_relay_near"):
-        report_2a = moved_by(report_1[:64], 2)
-    with jax.named_scope("report_relay_far"):
-        report_2b = moved_by(report_3[64:], -2)
+    with jax.named_scope("report_relay"):
+        report_2 = moved_by(report_1, 2)
     with jax.named_scope("report_beside"):
-        report_beside = beside(report_late, 1, 8)
+        report_beside = beside(after(report_late, caption_grad), 1, 8)
+    with jax.named_scope("image_swap"):
+        image_other = swapped(after(image_proj, caption_grad))
     with jax.named_scope("picture_kernel"):
         picture_mine, picture_theirs = window_call(
             picture_kernel,
@@ -260,8 +275,7 @@
             image_other,
             report_proj,
             report_1,
-            report_2a,
-            report_2b,
+            report_2,
             report_3,
             report_beside,
         )
@@ -285,7 +299,7 @@
             tiled=True,
         )
     with jax.named_scope("head_kernel"):
-        keep, give = head_call(place, after(caps, report_2a, report_2b, report_beside), feats)
+        keep, give = head_call(place, after(caps, report_beside), feats, ready(report_2))
     with jax.named_scope("head_swap"):
         part = (keep + swapped(give)).astype(jnp.bfloat16)
     with jax.named_scope("head_sum"):

time: 178 us -> 177 us (level)
  starting transfers between devices: 87.3 us -> 83.6 us
    ppermute x8 -> x7, starting transfers between devices: 53.5 us -> 39 us  [moved(): lax.ppermute(value, AXES, [(r, target_of(r) % BLOCKS) for r in range(BLOC...]
    all_to_all x1, starting transfers between devices: 5.29 us -> 10.1 us  [on_device(): lax.all_to_all(part, ('zl', 'zh', 'y'), split_axis=0, concat_axis=0, tile...]
    ppermute x2, starting transfers between devices: 3.33 us -> 7.33 us  [beside(): return lax.ppermute(value, AXES, pairs)]
    ppermute x8 -> x7, waiting for transfers between devices: 49.8 us -> 53.5 us  [moved(): lax.ppermute(value, AXES, [(r, target_of(r) % BLOCKS) for r in range(BLOC...]
    all_to_all x1, waiting for transfers between devices: 15.1 us -> 11.9 us  [on_device(): lax.all_to_all(part, ('zl', 'zh', 'y'), split_axis=0, concat_axis=0, tile...]
    all_to_all x1, starting transfers between devices: 10.5 us -> 12.8 us  [on_device(): lax.all_to_all(after(caption_spread, feats), ('x', 'y'), split_axis=0, co...]
    unnamed x10 -> x16, local copies, waits for them, and re-layouts: 3.25 us -> 4.66 us
  transfers between devices with their start and end apart: 18 -> 17, of which waited for: 11 -> 9; matrix products, arithmetic and copies ran while one was open for 0% -> 0% of each run, Pallas kernels for 5% -> 5%
where the time goes in v5:
time: 177 us; the launch traced here: 176 us
  starting transfers between devices  83.6 us (47%)
  waiting for transfers between devices  70.3 us (40%)
  Pallas kernels  13.4 us (8%)
  local copies, waits for them, and re-layouts  4.79 us (3%)
  between operations  2.23 us (1%)
    ppermute x7, waiting for transfers between devices, moved(): lax.ppermute(value, AXES, [(r, target_of(r) % BLOCKS) for r in range(BLOC...  53.5 us
    ppermute x7, starting transfers between devices, moved(): lax.ppermute(value, AXES, [(r, target_of(r) % BLOCKS) for r in range(BLOC...  39 us
    all_to_all x1, starting transfers between devices, on_device(): lax.all_to_all(after(caption_spread, feats), ('x', 'y'), split_axis=0, co...  12.8 us
    all_to_all x1, waiting for transfers between devices, on_device(): lax.all_to_all(part, ('zl', 'zh', 'y'), split_axis=0, concat_axis=0, tile...  11.9 us
    all_to_all x1, starting transfers between devices, on_device(): lax.all_to_all(part, ('zl', 'zh', 'y'), split_axis=0, concat_axis=0, tile...  10.1 us
    ppermute x5, starting transfers between devices, swapped(): return lax.ppermute(value, 'c', [(0, 1), (1, 0)])  9.72 us
    ppermute x2, starting transfers between devices, beside(): return lax.ppermute(value, AXES, pairs)  7.33 us
    ppermute x5, waiting for transfers between devices, swapped(): return lax.ppermute(value, 'c', [(0, 1), (1, 0)])  5.01 us
  transfers between devices with their start and end apart: 17, of which 9 were waited for; matrix products, arithmetic and copies ran while one was open for 0% of the time, Pallas kernels for 5%

profile of v5, /device:TPU:32, one launch (start us, length us, event | category | flops | bytes accessed | tf_op | source)
XLA Modules:
  0.0 175.9 jit_solution(6445036143018097628)
XLA Ops:
  0.6 6.7 %collective-permute-start.5 = (bf16[128,1024]{1,0:T(8,128)(2,1)}, bf16[128,1024]{1,0:T(8,128)(2,1)S(1)}, u32[]{:S(2)}, u32[]{:S(2)}) collective-permute-start(bf16[128,1024]{1,0:T(8,128)(2,1)} %own.7), channel_id=1, source_target_pairs={{0,504},{2,506},{4,508},{6,510},{8,0},{10,2},{12,4},{14,6},{16,8},... | collective-permute-start | bytes 786440 | tf_op jit(solution)/shard_map/image_beside/ppermute | solution.py:35
  7.3 8.4 %collective-permute-start.3 = (bf16[128,1024]{1,0:T(8,128)(2,1)}, bf16[128,1024]{1,0:T(8,128)(2,1)S(1)}, u32[]{:S(2)}, u32[]{:S(2)}) collective-permute-start(bf16[128,1024]{1,0:T(8,128)(2,1)} %own.7), channel_id=1, source_target_pairs={{0,506},{1,507},{2,508},{3,509},{4,510},{5,511},{6,0},{7,1},{8,2},... | collective-permute-start | bytes 786440 | tf_op jit(solution)/shard_map/image_far/ppermute | solution.py:22
  15.7 6.5 %collective-permute-start.1 = (bf16[128,1024]{1,0:T(8,128)(2,1)}, bf16[128,1024]{1,0:T(8,128)(2,1)S(1)}, u32[]{:S(2)}, u32[]{:S(2)}) collective-permute-start(bf16[128,1024]{1,0:T(8,128)(2,1)} %own.7), channel_id=1, source_target_pairs={{0,510},{1,511},{2,0},{3,1},{4,2},{5,3},{6,4},{7,5},{8,6},{9,7},{1... | collective-permute-start | bytes 786440 | tf_op jit(solution)/shard_map/image_near/ppermute | solution.py:22
  22.2 0.0 collective-permute-done.5.refs_5_
  22.2 1.2 copy-done.1
  23.4 0.5 feats.1
  23.9 2.0 %copy-done = bf16[2048,1024]{1,0:T(8,128)(2,1)} copy-done((bf16[2048,1024]{1,0:T(8,128)(2,1)}, bf16[2048,1024]{1,0:T(8,128)(2,1)S(1)}, u32[]{:S(2)}) %copy-start) | copy-done | bytes 4194328
  26.0 4.7 %all-to-all-start = ((bf16[16,128,1024]{2,1,0:T(8,128)(2,1)}), bf16[16,128,1024]{2,1,0:T(8,128)(2,1)}, u32[]{:S(2)}, u32[]{:S(2)}) async-start(bf16[16,128,1024]{2,1,0:T(8,128)(2,1)} %bitcast.14), calls=%async_computation | async-start | bytes 8388608 | tf_op jit(solution)/shard_map/feats/all_to_all | solution.py:219
  30.6 1.9 %collective-permute-start = (bf16[128,1024]{1,0:T(8,128)(2,1)S(1)}, bf16[128,1024]{1,0:T(8,128)(2,1)S(1)}, u32[]{:S(2)}, u32[]{:S(2)}) collective-permute-start(bf16[128,1024]{1,0:T(8,128)(2,1)S(1)} %copy-done.2), channel_id=1, source_target_pairs={{0,1},{1,0},{2,3},{3,2},{4,5},{5,4},{6,7},{7,6},{8,9},{9,8},{10,11... | collective-permute-start | bytes 786440 | tf_op jit(solution)/shard_map/core_swap/ppermute | solution.py:30
  32.6 5.6 %collective-permute-done.3.refs_4_ = bf16[128,1024]{1,0:T(8,128)(2,1)S(1)} collective-permute-done((bf16[128,1024]{1,0:T(8,128)(2,1)}, bf16[128,1024]{1,0:T(8,128)(2,1)S(1)}, u32[]{:S(2)}, u32[]{:S(2)}) %collective-permute-start.3) | collective-permute-done | bytes 262176 | tf_op jit(solution)/shard_map/image_far/ppermute | solution.py:22
  38.2 9.5 %collective-permute-start.4 = (bf16[64,1024]{1,0:T(8,128)(2,1)S(1)}, bf16[64,1024]{1,0:T(8,128)(2,1)S(1)}, u32[]{:S(2)}, u32[]{:S(2)}) collective-permute-start(bf16[64,1024]{1,0:T(8,128)(2,1)S(1)} %slice.9), channel_id=1, source_target_pairs={{0,2},{1,3},{2,4},{3,5},{4,6},{5,7},{6,8},{7,9},{8,10},{9,11},{10,... | collective-permute-start | bytes 393224 | tf_op jit(solution)/shard_map/image_relay_far/ppermute | solution.py:22
  47.8 0.0 collective-permute-done.1.refs_1_
  47.8 8.8 %collective-permute-start.2 = (bf16[64,1024]{1,0:T(8,128)(2,1)S(1)}, bf16[64,1024]{1,0:T(8,128)(2,1)S(1)}, u32[]{:S(2)}, u32[]{:S(2)}) collective-permute-start(bf16[64,1024]{1,0:T(8,128)(2,1)S(1)} %slice.8), channel_id=1, source_target_pairs={{0,510},{1,511},{2,0},{3,1},{4,2},{5,3},{6,4},{7,5},{8,6},{9,7},{1... | collective-permute-start | bytes 393224 | tf_op jit(solution)/shard_map/image_relay_near/ppermute | solution.py:22
  58.0 0.1 pad_maximum_fusion.scalars
  58.1 1.9 %collective-permute-start.7 = (bf16[128,1024]{1,0:T(8,128)(2,1)S(1)}, bf16[128,1024]{1,0:T(8,128)(2,1)S(1)}, u32[]{:S(2)}, u32[]{:S(2)}) collective-permute-start(bf16[128,1024]{1,0:T(8,128)(2,1)S(1)} %copy-done.2), channel_id=1, source_target_pairs={{0,6},{1,7},{2,8},{3,9},{4,10},{5,11},{6,12},{7,13},{8,14},{9,15},... | collective-permute-start | bytes 786440 | tf_op jit(solution)/shard_map/report_far/ppermute | solution.py:22
  60.0 1.9 %collective-permute-start.6 = (bf16[128,1024]{1,0:T(8,128)(2,1)S(1)}, bf16[128,1024]{1,0:T(8,128)(2,1)S(1)}, u32[]{:S(2)}, u32[]{:S(2)}) collective-permute-start(bf16[128,1024]{1,0:T(8,128)(2,1)S(1)} %copy-done.2), channel_id=1, source_target_pairs={{0,2},{1,3},{2,4},{3,5},{4,6},{5,7},{6,8},{7,9},{8,10},{9,11},{10,... | collective-permute-start | bytes 786440 | tf_op jit(solution)/shard_map/report_near/ppermute | solution.py:22
  61.9 0.0 collective-permute-done.other
  61.9 0.0 collective-permute-done.4.refs_3_
  61.9 6.7 %collective-permute-done.2.refs_2_ = bf16[64,1024]{1,0:T(8,128)(2,1)S(1)} collective-permute-done((bf16[64,1024]{1,0:T(8,128)(2,1)S(1)}, bf16[64,1024]{1,0:T(8,128)(2,1)S(1)}, u32[]{:S(2)}, u32[]{:S(2)}) %collective-permute-start.2) | collective-permute-done | bytes 131104 | tf_op jit(solution)/shard_map/image_relay_near/ppermute | solution.py:22
  68.6 2.2 %caption_kernel.1 = (f32[128,1024]{1,0:T(8,128)S(1)}, f32[128,1024]{1,0:T(8,128)S(1)}) custom-call(f32[2]{0:T(128)S(1)} %pad_maximum_fusion.scalars, s32[1]{0:T(128)} %bitcast.place, s32[1,128]{1,0:T(1,128)S(1)} %bitcast.16, bf16[128,1024]{1,0:T(8,128)(2,1)S(1)} %copy-done.2, bf16[128,1024]{1,0:T(8,128)(2,1)S(1)} %collective-permute-done.other, ...), custom_call_target="tpu_custom_call" | custom-call | flops 32749125632 | bytes 4000000 | tf_op jit(solution)/shard_map/caption_kernel/pallas_call | solution.py:100
  70.8 18.3 %collective-permute-done.7.refs_3_ = bf16[128,1024]{1,0:T(8,128)(2,1)S(1)} collective-permute-done((bf16[128,1024]{1,0:T(8,128)(2,1)S(1)}, bf16[128,1024]{1,0:T(8,128)(2,1)S(1)}, u32[]{:S(2)}, u32[]{:S(2)}) %collective-permute-start.7) | collective-permute-done | bytes 262176 | tf_op jit(solution)/shard_map/report_far/ppermute | solution.py:22
  89.1 2.3 %collective-permute-done.6.refs_1_ = bf16[128,1024]{1,0:T(8,128)(2,1)S(1)} collective-permute-done((bf16[128,1024]{1,0:T(8,128)(2,1)S(1)}, bf16[128,1024]{1,0:T(8,128)(2,1)S(1)}, u32[]{:S(2)}, u32[]{:S(2)}) %collective-permute-start.6) | collective-permute-done | bytes 262176 | tf_op jit(solution)/shard_map/report_near/ppermute | solution.py:22
  91.4 1.9 %collective-permute-start.8 = (f32[128,1024]{1,0:T(8,128)S(1)}, f32[128,1024]{1,0:T(8,128)S(1)}, u32[]{:S(2)}, u32[]{:S(2)}) collective-permute-start(f32[128,1024]{1,0:T(8,128)S(1)} %get-tuple-element.21), channel_id=1, source_target_pairs={{0,1},{1,0},{2,3},{3,2},{4,5},{5,4},{6,7},{7,6},{8,9},{9,8},{10,11... | collective-permute-start | bytes 1572872 | tf_op jit(solution)/shard_map/caption_swap/ppermute | solution.py:30
  93.3 1.9 %collective-permute-start.10 = (bf16[128,1024]{1,0:T(8,128)(2,1)S(1)}, bf16[128,1024]{1,0:T(8,128)(2,1)S(1)}, u32[]{:S(2)}, u32[]{:S(2)}) collective-permute-start(bf16[128,1024]{1,0:T(8,128)(2,1)S(1)} %collective-permute-done.6.refs_1_), channel_id=1, source_target_pairs={{0,2},{1,3},{2,4},{3,5},{4,6},{5,7},{6,8},{7,9},{8,10},{9,11},{10,... | collective-permute-start | bytes 786440 | tf_op jit(solution)/shard_map/report_relay/ppermute | solution.py:22
  95.3 0.0 collective-permute-done.8.received
  95.3 2.0 %caption_finish.1 = (bf16[128,1024]{1,0:T(8,128)(2,1)}, bf16[2048,256]{1,0:T(8,128)(2,1)}) custom-call(f32[2]{0:T(128)S(1)} %pad_maximum_fusion.scalars, bf16[128,1024]{1,0:T(8,128)(2,1)S(1)} %copy-done.2, f32[128,1024]{1,0:T(8,128)S(1)} %get-tuple-element.18.mine, f32[128,1024]{1,0:T(8,128)S(1)} %collective-permute-done.8.received), custom_call_target="tpu_custom_call" | custom-call | bytes 1500000 | tf_op jit(solution)/shard_map/caption_finish/pallas_call | solution.py:128
  97.3 0.7 collective-permute-start.11
  97.9 0.0 all-to-all-done
  98.0 12.8 %all-to-all-start.1 = ((bf16[16,128,256]{2,1,0:T(8,128)(2,1)}), bf16[16,128,256]{2,1,0:T(8,128)(2,1)S(1)}, u32[]{:S(2)}, u32[]{:S(2)}) async-start(bf16[16,128,256]{2,1,0:T(8,128)(2,1)} %bitcast.5), calls=%async_computation.1 | async-start | bytes 2097152 | tf_op jit(solution)/shard_map/captions/all_to_all | solution.py:294
  110.8 20.5 %collective-permute-done.10.refs_2_.first = bf16[128,1024]{1,0:T(8,128)(2,1)S(1)} collective-permute-done((bf16[128,1024]{1,0:T(8,128)(2,1)S(1)}, bf16[128,1024]{1,0:T(8,128)(2,1)S(1)}, u32[]{:S(2)}, u32[]{:S(2)}) %collective-permute-start.10) | collective-permute-done | bytes 262176 | tf_op jit(solution)/shard_map/report_relay/ppermute | solution.py:22
  131.3 0.7 copy-done.6
  132.0 1.3 head_kernel.2.arrived
  133.3 0.0 collective-permute-done.11.refs_4_
  133.3 0.7 copy-done.4
  134.0 3.8 %head_kernel.3 = (f32[512,256]{1,0:T(8,128)S(1)}, f32[512,256]{1,0:T(8,128)S(1)}) custom-call(s32[1]{0:T(128)} %bitcast.place, bf16[2048,256]{1,0:T(8,128)(2,1)S(1)} %bitcast.15, bf16[2048,1024]{1,0:T(8,128)(2,1)} %bitcast.4.feats, f32[16,128]{1,0:T(8,128)S(1)} %copy-done.4), custom_call_target="tpu_custom_call" | custom-call | flops 1073741824 | bytes 6000000 | tf_op jit(solution)/shard_map/head_kernel/pallas_call | solution.py:156
  137.8 1.9 %collective-permute-start.13 = (f32[512,256]{1,0:T(8,128)S(1)}, f32[512,256]{1,0:T(8,128)S(1)}, u32[]{:S(2)}, u32[]{:S(2)}) collective-permute-start(f32[512,256]{1,0:T(8,128)S(1)} %get-tuple-element.32), channel_id=1, source_target_pairs={{0,1},{1,0},{2,3},{3,2},{4,5},{5,4},{6,7},{7,6},{8,9},{9,8},{10,11... | collective-permute-start | bytes 1572872 | tf_op jit(solution)/shard_map/head_swap/ppermute | solution.py:30
  139.7 1.9 %collective-permute-done.13 = f32[512,256]{1,0:T(8,128)S(1)} collective-permute-done((f32[512,256]{1,0:T(8,128)S(1)}, f32[512,256]{1,0:T(8,128)S(1)}, u32[]{:S(2)}, u32[]{:S(2)}) %collective-permute-start.13) | collective-permute-done | bytes 524320 | tf_op jit(solution)/shard_map/head_swap/ppermute | solution.py:30
  141.6 0.8 fusion
  142.3 10.1 %all-to-all-start.2 = ((bf16[64,8,256]{2,1,0:T(8,128)(2,1)}), bf16[64,8,256]{2,1,0:T(8,128)(2,1)S(1)}, u32[]{:S(2)}, u32[]{:S(2)}) async-start(bf16[64,8,256]{2,1,0:T(8,128)(2,1)} %fusion), calls=%async_computation.2 | async-start | bytes 524288 | tf_op jit(solution)/shard_map/head_sum/all_to_all | solution.py:306
  152.4 1.9 %collective-permute-start.9 = (bf16[128,1024]{1,0:T(8,128)(2,1)S(1)}, bf16[128,1024]{1,0:T(8,128)(2,1)S(1)}, u32[]{:S(2)}, u32[]{:S(2)}) collective-permute-start(bf16[128,1024]{1,0:T(8,128)(2,1)S(1)} %copy-done.3), channel_id=1, source_target_pairs={{0,1},{1,0},{2,3},{3,2},{4,5},{5,4},{6,7},{7,6},{8,9},{9,8},{10,11... | collective-permute-start | bytes 786440 | tf_op jit(solution)/shard_map/image_swap/ppermute | solution.py:30
  154.3 0.1 copy.9.pair_column
  154.5 1.4 collective-permute-done.9.other
  155.9 2.2 %picture_kernel.1 = (f32[128,1024]{1,0:T(8,128)S(1)}, f32[128,1024]{1,0:T(8,128)S(1)}) custom-call(f32[2]{0:T(128)S(1)} %pad_maximum_fusion.scalars, s32[1]{0:T(128)} %bitcast.place, s32[128,1]{1,0:T(8,128)S(1)} %copy.9.pair_column, bf16[128,1024]{1,0:T(8,128)(2,1)S(1)} %copy-done.3, bf16[128,1024]{1,0:T(8,128)(2,1)S(1)} %collective-permute-done.9.other, ...), custom_call_target="tpu_custom_call" | custom-call | flops 536870912 | bytes 4000000 | tf_op jit(solution)/shard_map/picture_kernel/pallas_call | solution.py:100
  158.0 2.1 %collective-permute-start.12 = (f32[128,1024]{1,0:T(8,128)S(1)}, f32[128,1024]{1,0:T(8,128)S(1)}, u32[]{:S(2)}, u32[]{:S(2)}) collective-permute-start(f32[128,1024]{1,0:T(8,128)S(1)} %get-tuple-element.26), channel_id=1, source_target_pairs={{0,1},{1,0},{2,3},{3,2},{4,5},{5,4},{6,7},{7,6},{8,9},{9,8},{10,11... | collective-permute-start | bytes 1572872 | tf_op jit(solution)/shard_map/picture_swap/ppermute | solution.py:30
  160.1 1.7 collective-permute-done.12.received
  161.8 1.5 picture_finish.1
  163.4 11.9 %all-to-all-done.2 = bf16[64,8,256]{2,1,0:T(8,128)(2,1)S(1)} async-done(((bf16[64,8,256]{2,1,0:T(8,128)(2,1)}), bf16[64,8,256]{2,1,0:T(8,128)(2,1)S(1)}, u32[]{:S(2)}, u32[]{:S(2)}) %all-to-all-start.2) | async-done | bytes 262176 | tf_op jit(solution)/shard_map/head_sum/all_to_all | solution.py:306
  175.2 0.7 convert_reduce_fusion
  (15 shorter events, 0.0 us)
Async XLA Ops:
  0.6 21.5 %collective-permute-start.5 = (bf16[128,1024]{1,0:T(8,128)(2,1)}, bf16[128,1024]{1,0:T(8,128)(2,1)S(1)}, u32[]{:S(2)}, u32[]{:S(2)}) collective-permute-start(bf16[128,1024]{1,0:T(8,128)(2,1)} %own.7), channel_id=1, source_target_pairs={{0,504},{2,506},{4,508},{6,510},{8,0},{10,2},{12,4},{14,6},{16,8},... | collective-permute-start | bytes 786440 | tf_op jit(solution)/shard_map/image_beside/ppermute | solution.py:35
  7.3 30.9 %collective-permute-start.3 = (bf16[128,1024]{1,0:T(8,128)(2,1)}, bf16[128,1024]{1,0:T(8,128)(2,1)S(1)}, u32[]{:S(2)}, u32[]{:S(2)}) collective-permute-start(bf16[128,1024]{1,0:T(8,128)(2,1)} %own.7), channel_id=1, source_target_pairs={{0,506},{1,507},{2,508},{3,509},{4,510},{5,511},{6,0},{7,1},{8,2},... | collective-permute-start | bytes 786440 | tf_op jit(solution)/shard_map/image_far/ppermute | solution.py:22
  15.7 32.1 %collective-permute-start.1 = (bf16[128,1024]{1,0:T(8,128)(2,1)}, bf16[128,1024]{1,0:T(8,128)(2,1)S(1)}, u32[]{:S(2)}, u32[]{:S(2)}) collective-permute-start(bf16[128,1024]{1,0:T(8,128)(2,1)} %own.7), channel_id=1, source_target_pairs={{0,510},{1,511},{2,0},{3,1},{4,2},{5,3},{6,4},{7,5},{8,6},{9,7},{1... | collective-permute-start | bytes 786440 | tf_op jit(solution)/shard_map/image_near/ppermute | solution.py:22
  22.2 1.2 copy-start.1
  23.9 2.0 %copy-start = (bf16[2048,1024]{1,0:T(8,128)(2,1)}, bf16[2048,1024]{1,0:T(8,128)(2,1)S(1)}, u32[]{:S(2)}) copy-start(bf16[2048,1024]{1,0:T(8,128)(2,1)S(1)} %feats.1) | copy-start | bytes 12582916
  25.9 4.7 %copy-start.2 = (bf16[128,1024]{1,0:T(8,128)(2,1)S(1)}, bf16[128,1024]{1,0:T(8,128)(2,1)}, u32[]{:S(2)}) copy-start(bf16[128,1024]{1,0:T(8,128)(2,1)} %refs_0_.3) | copy-start | bytes 786436
  25.9 42.7 %copy-start.3 = (bf16[128,1024]{1,0:T(8,128)(2,1)S(1)}, bf16[128,1024]{1,0:T(8,128)(2,1)}, u32[]{:S(2)}) copy-start(bf16[128,1024]{1,0:T(8,128)(2,1)} %own.7) | copy-start | bytes 786436
  25.9 42.7 %copy-start.5 = (s32[128]{0:T(128)S(1)}, s32[128]{0:T(128)}, u32[]{:S(2)}) copy-start(s32[128]{0:T(128)} %param.9) | copy-start | bytes 1540
  26.0 72.0 %all-to-all-start = ((bf16[16,128,1024]{2,1,0:T(8,128)(2,1)}), bf16[16,128,1024]{2,1,0:T(8,128)(2,1)}, u32[]{:S(2)}, u32[]{:S(2)}) async-start(bf16[16,128,1024]{2,1,0:T(8,128)(2,1)} %bitcast.14), calls=%async_computation | async-start | bytes 8388608 | tf_op jit(solution)/shard_map/feats/all_to_all | solution.py:219
  30.6 31.3 %collective-permute-start = (bf16[128,1024]{1,0:T(8,128)(2,1)S(1)}, bf16[128,1024]{1,0:T(8,128)(2,1)S(1)}, u32[]{:S(2)}, u32[]{:S(2)}) collective-permute-start(bf16[128,1024]{1,0:T(8,128)(2,1)S(1)} %copy-done.2), channel_id=1, source_target_pairs={{0,1},{1,0},{2,3},{3,2},{4,5},{5,4},{6,7},{7,6},{8,9},{9,8},{10,11... | collective-permute-start | bytes 786440 | tf_op jit(solution)/shard_map/core_swap/ppermute | solution.py:30
  38.2 23.7 %collective-permute-start.4 = (bf16[64,1024]{1,0:T(8,128)(2,1)S(1)}, bf16[64,1024]{1,0:T(8,128)(2,1)S(1)}, u32[]{:S(2)}, u32[]{:S(2)}) collective-permute-start(bf16[64,1024]{1,0:T(8,128)(2,1)S(1)} %slice.9), channel_id=1, source_target_pairs={{0,2},{1,3},{2,4},{3,5},{4,6},{5,7},{6,8},{7,9},{8,10},{9,11},{10,... | collective-permute-start | bytes 393224 | tf_op jit(solution)/shard_map/image_relay_far/ppermute | solution.py:22
  47.8 20.8 %collective-permute-start.2 = (bf16[64,1024]{1,0:T(8,128)(2,1)S(1)}, bf16[64,1024]{1,0:T(8,128)(2,1)S(1)}, u32[]{:S(2)}, u32[]{:S(2)}) collective-permute-start(bf16[64,1024]{1,0:T(8,128)(2,1)S(1)} %slice.8), channel_id=1, source_target_pairs={{0,510},{1,511},{2,0},{3,1},{4,2},{5,3},{6,4},{7,5},{8,6},{9,7},{1... | collective-permute-start | bytes 393224 | tf_op jit(solution)/shard_map/image_relay_near/ppermute | solution.py:22
  58.1 31.0 %collective-permute-start.7 = (bf16[128,1024]{1,0:T(8,128)(2,1)S(1)}, bf16[128,1024]{1,0:T(8,128)(2,1)S(1)}, u32[]{:S(2)}, u32[]{:S(2)}) collective-permute-start(bf16[128,1024]{1,0:T(8,128)(2,1)S(1)} %copy-done.2), channel_id=1, source_target_pairs={{0,6},{1,7},{2,8},{3,9},{4,10},{5,11},{6,12},{7,13},{8,14},{9,15},... | collective-permute-start | bytes 786440 | tf_op jit(solution)/shard_map/report_far/ppermute | solution.py:22
  60.0 31.4 %collective-permute-start.6 = (bf16[128,1024]{1,0:T(8,128)(2,1)S(1)}, bf16[128,1024]{1,0:T(8,128)(2,1)S(1)}, u32[]{:S(2)}, u32[]{:S(2)}) collective-permute-start(bf16[128,1024]{1,0:T(8,128)(2,1)S(1)} %copy-done.2), channel_id=1, source_target_pairs={{0,2},{1,3},{2,4},{3,5},{4,6},{5,7},{6,8},{7,9},{8,10},{9,11},{10,... | collective-permute-start | bytes 786440 | tf_op jit(solution)/shard_map/report_near/ppermute | solution.py:22
  91.4 3.8 %collective-permute-start.8 = (f32[128,1024]{1,0:T(8,128)S(1)}, f32[128,1024]{1,0:T(8,128)S(1)}, u32[]{:S(2)}, u32[]{:S(2)}) collective-permute-start(f32[128,1024]{1,0:T(8,128)S(1)} %get-tuple-element.21), channel_id=1, source_target_pairs={{0,1},{1,0},{2,3},{3,2},{4,5},{5,4},{6,7},{7,6},{8,9},{9,8},{10,11... | collective-permute-start | bytes 1572872 | tf_op jit(solution)/shard_map/caption_swap/ppermute | solution.py:30
  93.3 38.0 %collective-permute-start.10 = (bf16[128,1024]{1,0:T(8,128)(2,1)S(1)}, bf16[128,1024]{1,0:T(8,128)(2,1)S(1)}, u32[]{:S(2)}, u32[]{:S(2)}) collective-permute-start(bf16[128,1024]{1,0:T(8,128)(2,1)S(1)} %collective-permute-done.6.refs_1_), channel_id=1, source_target_pairs={{0,2},{1,3},{2,4},{3,5},{4,6},{5,7},{6,8},{7,9},{8,10},{9,11},{10,... | collective-permute-start | bytes 786440 | tf_op jit(solution)/shard_map/report_relay/ppermute | solution.py:22
  97.3 36.0 %collective-permute-start.11 = (bf16[128,1024]{1,0:T(8,128)(2,1)S(1)}, bf16[128,1024]{1,0:T(8,128)(2,1)S(1)}, u32[]{:S(2)}, u32[]{:S(2)}) collective-permute-start(bf16[128,1024]{1,0:T(8,128)(2,1)S(1)} %copy-done.2), channel_id=1, source_target_pairs={{1,9},{3,11},{5,13},{7,15},{9,17},{11,19},{13,21},{15,23},{17,25},... | collective-permute-start | bytes 786440 | tf_op jit(solution)/shard_map/report_beside/ppermute | solution.py:35
  98.0 35.4 %all-to-all-start.1 = ((bf16[16,128,256]{2,1,0:T(8,128)(2,1)}), bf16[16,128,256]{2,1,0:T(8,128)(2,1)S(1)}, u32[]{:S(2)}, u32[]{:S(2)}) async-start(bf16[16,128,256]{2,1,0:T(8,128)(2,1)} %bitcast.5), calls=%async_computation.1 | async-start | bytes 2097152 | tf_op jit(solution)/shard_map/captions/all_to_all | solution.py:294
  131.3 0.7 copy-start.6
  133.3 0.7 copy-start.4
  134.0 21.8 %copy-start.7 = (bf16[128,1024]{1,0:T(8,128)(2,1)S(1)}, bf16[128,1024]{1,0:T(8,128)(2,1)}, u32[]{:S(2)}) copy-start(bf16[128,1024]{1,0:T(8,128)(2,1)} %copy-done.6) | copy-start | bytes 786436
  137.8 3.8 %collective-permute-start.13 = (f32[512,256]{1,0:T(8,128)S(1)}, f32[512,256]{1,0:T(8,128)S(1)}, u32[]{:S(2)}, u32[]{:S(2)}) collective-permute-start(f32[512,256]{1,0:T(8,128)S(1)} %get-tuple-element.32), channel_id=1, source_target_pairs={{0,1},{1,0},{2,3},{3,2},{4,5},{5,4},{6,7},{7,6},{8,9},{9,8},{10,11... | collective-permute-start | bytes 1572872 | tf_op jit(solution)/shard_map/head_swap/ppermute | solution.py:30
  142.3 32.9 %all-to-all-start.2 = ((bf16[64,8,256]{2,1,0:T(8,128)(2,1)}), bf16[64,8,256]{2,1,0:T(8,128)(2,1)S(1)}, u32[]{:S(2)}, u32[]{:S(2)}) async-start(bf16[64,8,256]{2,1,0:T(8,128)(2,1)} %fusion), calls=%async_computation.2 | async-start | bytes 524288 | tf_op jit(solution)/shard_map/head_sum/all_to_all | solution.py:306
  152.4 3.4 %collective-permute-start.9 = (bf16[128,1024]{1,0:T(8,128)(2,1)S(1)}, bf16[128,1024]{1,0:T(8,128)(2,1)S(1)}, u32[]{:S(2)}, u32[]{:S(2)}) collective-permute-start(bf16[128,1024]{1,0:T(8,128)(2,1)S(1)} %copy-done.3), channel_id=1, source_target_pairs={{0,1},{1,0},{2,3},{3,2},{4,5},{5,4},{6,7},{7,6},{8,9},{9,8},{10,11... | collective-permute-start | bytes 786440 | tf_op jit(solution)/shard_map/image_swap/ppermute | solution.py:30
  158.0 3.8 %collective-permute-start.12 = (f32[128,1024]{1,0:T(8,128)S(1)}, f32[128,1024]{1,0:T(8,128)S(1)}, u32[]{:S(2)}, u32[]{:S(2)}) collective-permute-start(f32[128,1024]{1,0:T(8,128)S(1)} %get-tuple-element.26), channel_id=1, source_target_pairs={{0,1},{1,0},{2,3},{3,2},{4,5},{5,4},{6,7},{7,6},{8,9},{9,8},{10,11... | collective-permute-start | bytes 1572872 | tf_op jit(solution)/shard_map/picture_swap/ppermute | solution.py:30

commit v6 on v5

--- a/solution.py
+++ b/solution.py
@@ -181,22 +181,39 @@
     )(first)
 
 
-def columns_kernel(feats, out):
+def columns_kernel(feats, out, held, sems):
+    copy = pltpu.make_async_copy(feats, held, sems.at[64])
+    copy.start()
+    copy.wait()
+    copies = []
     for x in range(4):
         for zl in range(4):
-            piece = feats[:, zl * 1024 + x * 256 : zl * 1024 + x * 256 + 256]
             for y in range(4):
                 row = (x * 4 + y) * ROWS
-                out[row : row + ROWS, zl * 256 : zl * 256 + 256] = piece
+                copies.append(
+                    pltpu.make_async_copy(
+                        held.at[:, pl.ds(zl * 1024 + x * 256, 256)],
+                        out.at[pl.ds(row, ROWS), pl.ds(zl * 256, 256)],
+                        sems.at[(x * 4 + zl) * 4 + y],
+                    )
+                )
+    for copy in copies:
+        copy.start()
+    for copy in copies:
+        copy.wait()
 
 
 def columns_call(feats):
-    vmem = pl.BlockSpec(memory_space=pltpu.VMEM)
+    anywhere = pl.BlockSpec(memory_space=pl.ANY)
     return pl.pallas_call(
         columns_kernel,
         out_shape=jax.ShapeDtypeStruct((16 * ROWS, WIDTH), jnp.bfloat16),
-        in_specs=[vmem],
-        out_specs=vmem,
+        in_specs=[anywhere],
+        out_specs=anywhere,
+        scratch_shapes=[
+            pltpu.VMEM((ROWS, 4 * WIDTH), jnp.bfloat16),
+            pltpu.SemaphoreType.DMA((65,)),
+        ],
         compiler_params=pltpu.CompilerParams(vmem_limit_bytes=LIMIT),
         cost_estimate=pl.CostEstimate(flops=0, bytes_accessed=5_000_000, transcendentals=0),
     )(feats)

time: 177 us -> 178 us (level)
  the two profiles are of different devices: /device:TPU:32 before, /device:TPU:34 now
where the time goes in v6:
time: 178 us; the launch traced here: 177 us
  starting transfers between devices  100 us (56%)
  waiting for transfers between devices  54.4 us (31%)
  Pallas kernels  14.4 us (8%)
  local copies, waits for them, and re-layouts  4.78 us (3%)
  between operations  2.24 us (1%)
    ppermute x7, starting transfers between devices, moved(): lax.ppermute(value, AXES, [(r, target_of(r) % BLOCKS) for r in range(BLOC...  37.1 us
    all_to_all x1, starting transfers between devices, on_device(): lax.all_to_all(after(caption_spread, feats), ('x', 'y'), split_axis=0, co...  24 us
    ppermute x7, waiting for transfers between devices, moved(): lax.ppermute(value, AXES, [(r, target_of(r) % BLOCKS) for r in range(BLOC...  22.5 us
    all_to_all x1, starting transfers between devices, on_device(): lax.all_to_all(part, ('zl', 'zh', 'y'), split_axis=0, concat_axis=0, tile...  16.1 us
    all_to_all x1, waiting for transfers between devices, on_device(): lax.all_to_all(part, ('zl', 'zh', 'y'), split_axis=0, concat_axis=0, tile...  11.8 us
    all_to_all x1, waiting for transfers between devices, on_device(): lax.all_to_all(after(caption_spread, feats), ('x', 'y'), split_axis=0, co...  10.8 us
    ppermute x5, starting transfers between devices, swapped(): return lax.ppermute(value, 'c', [(0, 1), (1, 0)])  9.72 us
    all_to_all x1, starting transfers between devices, on_device(): lax.all_to_all(columns_call(after(report_feats, image_beside)), ('x', 'y'...  7.62 us
  transfers between devices with their start and end apart: 17, of which 9 were waited for; matrix products, arithmetic and copies ran while one was open for 0% of the time, Pallas kernels for 6%

profile of v6, /device:TPU:34, one launch (start us, length us, event | category | flops | bytes accessed | tf_op | source)
XLA Modules:
  0.0 177.3 jit_solution(3777250987400383511)
XLA Ops:
  0.6 4.9 %collective-permute-start.5 = (bf16[128,1024]{1,0:T(8,128)(2,1)}, bf16[128,1024]{1,0:T(8,128)(2,1)S(1)}, u32[]{:S(2)}, u32[]{:S(2)}) collective-permute-start(bf16[128,1024]{1,0:T(8,128)(2,1)} %own.7), channel_id=1, source_target_pairs={{0,504},{2,506},{4,508},{6,510},{8,0},{10,2},{12,4},{14,6},{16,8},... | collective-permute-start | bytes 786440 | tf_op jit(solution)/shard_map/image_beside/ppermute | solution.py:35
  5.5 9.3 %collective-permute-start.3 = (bf16[128,1024]{1,0:T(8,128)(2,1)}, bf16[128,1024]{1,0:T(8,128)(2,1)S(1)}, u32[]{:S(2)}, u32[]{:S(2)}) collective-permute-start(bf16[128,1024]{1,0:T(8,128)(2,1)} %own.7), channel_id=1, source_target_pairs={{0,506},{1,507},{2,508},{3,509},{4,510},{5,511},{6,0},{7,1},{8,2},... | collective-permute-start | bytes 786440 | tf_op jit(solution)/shard_map/image_far/ppermute | solution.py:22
  14.8 4.7 %collective-permute-start.1 = (bf16[128,1024]{1,0:T(8,128)(2,1)}, bf16[128,1024]{1,0:T(8,128)(2,1)S(1)}, u32[]{:S(2)}, u32[]{:S(2)}) collective-permute-start(bf16[128,1024]{1,0:T(8,128)(2,1)} %own.7), channel_id=1, source_target_pairs={{0,510},{1,511},{2,0},{3,1},{4,2},{5,3},{6,4},{7,5},{8,6},{9,7},{1... | collective-permute-start | bytes 786440 | tf_op jit(solution)/shard_map/image_near/ppermute | solution.py:22
  19.5 0.0 collective-permute-done.5.refs_5_
  19.5 1.2 copy-done.1
  20.7 1.4 feats.1
  22.2 2.0 %copy-done = bf16[2048,1024]{1,0:T(8,128)(2,1)} copy-done((bf16[2048,1024]{1,0:T(8,128)(2,1)}, bf16[2048,1024]{1,0:T(8,128)(2,1)S(1)}, u32[]{:S(2)}) %copy-start) | copy-done | bytes 4194328
  24.2 7.6 %all-to-all-start = ((bf16[16,128,1024]{2,1,0:T(8,128)(2,1)}), bf16[16,128,1024]{2,1,0:T(8,128)(2,1)}, u32[]{:S(2)}, u32[]{:S(2)}) async-start(bf16[16,128,1024]{2,1,0:T(8,128)(2,1)} %bitcast.14), calls=%async_computation | async-start | bytes 8388608 | tf_op jit(solution)/shard_map/feats/all_to_all | solution.py:236
  31.8 1.9 %collective-permute-start = (bf16[128,1024]{1,0:T(8,128)(2,1)S(1)}, bf16[128,1024]{1,0:T(8,128)(2,1)S(1)}, u32[]{:S(2)}, u32[]{:S(2)}) collective-permute-start(bf16[128,1024]{1,0:T(8,128)(2,1)S(1)} %copy-done.2), channel_id=1, source_target_pairs={{0,1},{1,0},{2,3},{3,2},{4,5},{5,4},{6,7},{7,6},{8,9},{9,8},{10,11... | collective-permute-start | bytes 786440 | tf_op jit(solution)/shard_map/core_swap/ppermute | solution.py:30
  33.7 0.0 collective-permute-done.3.refs_4_
  33.8 4.6 %collective-permute-start.4 = (bf16[64,1024]{1,0:T(8,128)(2,1)S(1)}, bf16[64,1024]{1,0:T(8,128)(2,1)S(1)}, u32[]{:S(2)}, u32[]{:S(2)}) collective-permute-start(bf16[64,1024]{1,0:T(8,128)(2,1)S(1)} %slice.9), channel_id=1, source_target_pairs={{0,2},{1,3},{2,4},{3,5},{4,6},{5,7},{6,8},{7,9},{8,10},{9,11},{10,... | collective-permute-start | bytes 393224 | tf_op jit(solution)/shard_map/image_relay_far/ppermute | solution.py:22
  38.3 2.6 %collective-permute-done.1.refs_1_ = bf16[128,1024]{1,0:T(8,128)(2,1)S(1)} collective-permute-done((bf16[128,1024]{1,0:T(8,128)(2,1)}, bf16[128,1024]{1,0:T(8,128)(2,1)S(1)}, u32[]{:S(2)}, u32[]{:S(2)}) %collective-permute-start.1) | collective-permute-done | bytes 262176 | tf_op jit(solution)/shard_map/image_near/ppermute | solution.py:22
  41.0 9.7 %collective-permute-start.2 = (bf16[64,1024]{1,0:T(8,128)(2,1)S(1)}, bf16[64,1024]{1,0:T(8,128)(2,1)S(1)}, u32[]{:S(2)}, u32[]{:S(2)}) collective-permute-start(bf16[64,1024]{1,0:T(8,128)(2,1)S(1)} %slice.8), channel_id=1, source_target_pairs={{0,510},{1,511},{2,0},{3,1},{4,2},{5,3},{6,4},{7,5},{8,6},{9,7},{1... | collective-permute-start | bytes 393224 | tf_op jit(solution)/shard_map/image_relay_near/ppermute | solution.py:22
  52.0 0.1 pad_maximum_fusion.scalars
  52.1 1.9 %collective-permute-start.7 = (bf16[128,1024]{1,0:T(8,128)(2,1)S(1)}, bf16[128,1024]{1,0:T(8,128)(2,1)S(1)}, u32[]{:S(2)}, u32[]{:S(2)}) collective-permute-start(bf16[128,1024]{1,0:T(8,128)(2,1)S(1)} %copy-done.2), channel_id=1, source_target_pairs={{0,6},{1,7},{2,8},{3,9},{4,10},{5,11},{6,12},{7,13},{8,14},{9,15},... | collective-permute-start | bytes 786440 | tf_op jit(solution)/shard_map/report_far/ppermute | solution.py:22
  54.0 4.2 %collective-permute-start.6 = (bf16[128,1024]{1,0:T(8,128)(2,1)S(1)}, bf16[128,1024]{1,0:T(8,128)(2,1)S(1)}, u32[]{:S(2)}, u32[]{:S(2)}) collective-permute-start(bf16[128,1024]{1,0:T(8,128)(2,1)S(1)} %copy-done.2), channel_id=1, source_target_pairs={{0,2},{1,3},{2,4},{3,5},{4,6},{5,7},{6,8},{7,9},{8,10},{9,11},{10,... | collective-permute-start | bytes 786440 | tf_op jit(solution)/shard_map/report_near/ppermute | solution.py:22
  58.2 0.0 collective-permute-done.other
  58.2 0.0 collective-permute-done.4.refs_3_
  58.2 2.2 %caption_kernel.1 = (f32[128,1024]{1,0:T(8,128)S(1)}, f32[128,1024]{1,0:T(8,128)S(1)}) custom-call(f32[2]{0:T(128)S(1)} %pad_maximum_fusion.scalars, s32[1]{0:T(128)} %bitcast.place, s32[1,128]{1,0:T(1,128)S(1)} %bitcast.16, bf16[128,1024]{1,0:T(8,128)(2,1)S(1)} %copy-done.2, bf16[128,1024]{1,0:T(8,128)(2,1)S(1)} %collective-permute-done.other, ...), custom_call_target="tpu_custom_call" | custom-call | flops 32749125632 | bytes 4000000 | tf_op jit(solution)/shard_map/caption_kernel/pallas_call | solution.py:100
  60.4 17.5 %collective-permute-done.7.refs_3_ = bf16[128,1024]{1,0:T(8,128)(2,1)S(1)} collective-permute-done((bf16[128,1024]{1,0:T(8,128)(2,1)S(1)}, bf16[128,1024]{1,0:T(8,128)(2,1)S(1)}, u32[]{:S(2)}, u32[]{:S(2)}) %collective-permute-start.7) | collective-permute-done | bytes 262176 | tf_op jit(solution)/shard_map/report_far/ppermute | solution.py:22
  78.0 2.3 %collective-permute-done.6.refs_1_ = bf16[128,1024]{1,0:T(8,128)(2,1)S(1)} collective-permute-done((bf16[128,1024]{1,0:T(8,128)(2,1)S(1)}, bf16[128,1024]{1,0:T(8,128)(2,1)S(1)}, u32[]{:S(2)}, u32[]{:S(2)}) %collective-permute-start.6) | collective-permute-done | bytes 262176 | tf_op jit(solution)/shard_map/report_near/ppermute | solution.py:22
  80.3 1.9 %collective-permute-start.8 = (f32[128,1024]{1,0:T(8,128)S(1)}, f32[128,1024]{1,0:T(8,128)S(1)}, u32[]{:S(2)}, u32[]{:S(2)}) collective-permute-start(f32[128,1024]{1,0:T(8,128)S(1)} %get-tuple-element.21), channel_id=1, source_target_pairs={{0,1},{1,0},{2,3},{3,2},{4,5},{5,4},{6,7},{7,6},{8,9},{9,8},{10,11... | collective-permute-start | bytes 1572872 | tf_op jit(solution)/shard_map/caption_swap/ppermute | solution.py:30
  82.2 2.8 %collective-permute-start.10 = (bf16[128,1024]{1,0:T(8,128)(2,1)S(1)}, bf16[128,1024]{1,0:T(8,128)(2,1)S(1)}, u32[]{:S(2)}, u32[]{:S(2)}) collective-permute-start(bf16[128,1024]{1,0:T(8,128)(2,1)S(1)} %collective-permute-done.6.refs_1_), channel_id=1, source_target_pairs={{0,2},{1,3},{2,4},{3,5},{4,6},{5,7},{6,8},{7,9},{8,10},{9,11},{10,... | collective-permute-start | bytes 786440 | tf_op jit(solution)/shard_map/report_relay/ppermute | solution.py:22
  85.0 2.0 %caption_finish.1 = (bf16[128,1024]{1,0:T(8,128)(2,1)}, bf16[2048,256]{1,0:T(8,128)(2,1)}) custom-call(f32[2]{0:T(128)S(1)} %pad_maximum_fusion.scalars, bf16[128,1024]{1,0:T(8,128)(2,1)S(1)} %copy-done.2, f32[128,1024]{1,0:T(8,128)S(1)} %get-tuple-element.18.mine, f32[128,1024]{1,0:T(8,128)S(1)} %collective-permute-done.8.received), custom_call_target="tpu_custom_call" | custom-call | bytes 1500000 | tf_op jit(solution)/shard_map/caption_finish/pallas_call | solution.py:128
  87.0 0.7 collective-permute-start.11
  87.7 4.3 %all-to-all-done = bf16[16,128,1024]{2,1,0:T(8,128)(2,1)} async-done(((bf16[16,128,1024]{2,1,0:T(8,128)(2,1)}), bf16[16,128,1024]{2,1,0:T(8,128)(2,1)}, u32[]{:S(2)}, u32[]{:S(2)}) %all-to-all-start) | async-done | bytes 4194336 | tf_op jit(solution)/shard_map/feats/all_to_all | solution.py:236
  92.0 24.0 %all-to-all-start.1 = ((bf16[16,128,256]{2,1,0:T(8,128)(2,1)}), bf16[16,128,256]{2,1,0:T(8,128)(2,1)S(1)}, u32[]{:S(2)}, u32[]{:S(2)}) async-start(bf16[16,128,256]{2,1,0:T(8,128)(2,1)} %bitcast.5), calls=%async_computation.1 | async-start | bytes 2097152 | tf_op jit(solution)/shard_map/captions/all_to_all | solution.py:311
  115.9 0.0 collective-permute-done.10.refs_2_.first
  115.9 0.0 copy-start.6
  116.0 0.7 copy-done.6
  116.7 1.3 head_kernel.2.arrived
  117.9 0.0 collective-permute-done.11.refs_4_
  117.9 10.8 %all-to-all-done.1 = bf16[16,128,256]{2,1,0:T(8,128)(2,1)S(1)} async-done(((bf16[16,128,256]{2,1,0:T(8,128)(2,1)}), bf16[16,128,256]{2,1,0:T(8,128)(2,1)S(1)}, u32[]{:S(2)}, u32[]{:S(2)}) %all-to-all-start.1) | async-done | bytes 1048608 | tf_op jit(solution)/shard_map/captions/all_to_all | solution.py:311
  128.7 0.7 copy-done.4
  129.4 3.8 %head_kernel.3 = (f32[512,256]{1,0:T(8,128)S(1)}, f32[512,256]{1,0:T(8,128)S(1)}) custom-call(s32[1]{0:T(128)} %bitcast.place, bf16[2048,256]{1,0:T(8,128)(2,1)S(1)} %bitcast.15, bf16[2048,1024]{1,0:T(8,128)(2,1)} %bitcast.4.feats, f32[16,128]{1,0:T(8,128)S(1)} %copy-done.4), custom_call_target="tpu_custom_call" | custom-call | flops 1073741824 | bytes 6000000 | tf_op jit(solution)/shard_map/head_kernel/pallas_call | solution.py:156
  133.2 1.9 %collective-permute-start.13 = (f32[512,256]{1,0:T(8,128)S(1)}, f32[512,256]{1,0:T(8,128)S(1)}, u32[]{:S(2)}, u32[]{:S(2)}) collective-permute-start(f32[512,256]{1,0:T(8,128)S(1)} %get-tuple-element.32), channel_id=1, source_target_pairs={{0,1},{1,0},{2,3},{3,2},{4,5},{5,4},{6,7},{7,6},{8,9},{9,8},{10,11... | collective-permute-start | bytes 1572872 | tf_op jit(solution)/shard_map/head_swap/ppermute | solution.py:30
  135.1 1.9 %collective-permute-done.13 = f32[512,256]{1,0:T(8,128)S(1)} collective-permute-done((f32[512,256]{1,0:T(8,128)S(1)}, f32[512,256]{1,0:T(8,128)S(1)}, u32[]{:S(2)}, u32[]{:S(2)}) %collective-permute-start.13) | collective-permute-done | bytes 524320 | tf_op jit(solution)/shard_map/head_swap/ppermute | solution.py:30
  137.0 0.8 fusion
  137.8 16.1 %all-to-all-start.2 = ((bf16[64,8,256]{2,1,0:T(8,128)(2,1)}), bf16[64,8,256]{2,1,0:T(8,128)(2,1)S(1)}, u32[]{:S(2)}, u32[]{:S(2)}) async-start(bf16[64,8,256]{2,1,0:T(8,128)(2,1)} %fusion), calls=%async_computation.2 | async-start | bytes 524288 | tf_op jit(solution)/shard_map/head_sum/all_to_all | solution.py:323
  153.9 1.9 %collective-permute-start.9 = (bf16[128,1024]{1,0:T(8,128)(2,1)S(1)}, bf16[128,1024]{1,0:T(8,128)(2,1)S(1)}, u32[]{:S(2)}, u32[]{:S(2)}) collective-permute-start(bf16[128,1024]{1,0:T(8,128)(2,1)S(1)} %copy-done.3), channel_id=1, source_target_pairs={{0,1},{1,0},{2,3},{3,2},{4,5},{5,4},{6,7},{7,6},{8,9},{9,8},{10,11... | collective-permute-start | bytes 786440 | tf_op jit(solution)/shard_map/image_swap/ppermute | solution.py:30
  155.8 0.1 copy.9.pair_column
  155.9 1.4 collective-permute-done.9.other
  157.3 2.2 %picture_kernel.1 = (f32[128,1024]{1,0:T(8,128)S(1)}, f32[128,1024]{1,0:T(8,128)S(1)}) custom-call(f32[2]{0:T(128)S(1)} %pad_maximum_fusion.scalars, s32[1]{0:T(128)} %bitcast.place, s32[128,1]{1,0:T(8,128)S(1)} %copy.9.pair_column, bf16[128,1024]{1,0:T(8,128)(2,1)S(1)} %copy-done.3, bf16[128,1024]{1,0:T(8,128)(2,1)S(1)} %collective-permute-done.9.other, ...), custom_call_target="tpu_custom_call" | custom-call | flops 536870912 | bytes 4000000 | tf_op jit(solution)/shard_map/picture_kernel/pallas_call | solution.py:100
  159.5 2.0 %collective-permute-start.12 = (f32[128,1024]{1,0:T(8,128)S(1)}, f32[128,1024]{1,0:T(8,128)S(1)}, u32[]{:S(2)}, u32[]{:S(2)}) collective-permute-start(f32[128,1024]{1,0:T(8,128)S(1)} %get-tuple-element.26), channel_id=1, source_target_pairs={{0,1},{1,0},{2,3},{3,2},{4,5},{5,4},{6,7},{7,6},{8,9},{9,8},{10,11... | collective-permute-start | bytes 1572872 | tf_op jit(solution)/shard_map/picture_swap/ppermute | solution.py:30
  161.5 1.8 collective-permute-done.12.received
  163.3 1.5 picture_finish.1
  164.8 11.8 %all-to-all-done.2 = bf16[64,8,256]{2,1,0:T(8,128)(2,1)S(1)} async-done(((bf16[64,8,256]{2,1,0:T(8,128)(2,1)}), bf16[64,8,256]{2,1,0:T(8,128)(2,1)S(1)}, u32[]{:S(2)}, u32[]{:S(2)}) %all-to-all-start.2) | async-done | bytes 262176 | tf_op jit(solution)/shard_map/head_sum/all_to_all | solution.py:323
  176.6 0.7 convert_reduce_fusion
  (15 shorter events, 0.0 us)
Async XLA Ops:
  0.6 18.9 %collective-permute-start.5 = (bf16[128,1024]{1,0:T(8,128)(2,1)}, bf16[128,1024]{1,0:T(8,128)(2,1)S(1)}, u32[]{:S(2)}, u32[]{:S(2)}) collective-permute-start(bf16[128,1024]{1,0:T(8,128)(2,1)} %own.7), channel_id=1, source_target_pairs={{0,504},{2,506},{4,508},{6,510},{8,0},{10,2},{12,4},{14,6},{16,8},... | collective-permute-start | bytes 786440 | tf_op jit(solution)/shard_map/image_beside/ppermute | solution.py:35
  5.5 28.2 %collective-permute-start.3 = (bf16[128,1024]{1,0:T(8,128)(2,1)}, bf16[128,1024]{1,0:T(8,128)(2,1)S(1)}, u32[]{:S(2)}, u32[]{:S(2)}) collective-permute-start(bf16[128,1024]{1,0:T(8,128)(2,1)} %own.7), channel_id=1, source_target_pairs={{0,506},{1,507},{2,508},{3,509},{4,510},{5,511},{6,0},{7,1},{8,2},... | collective-permute-start | bytes 786440 | tf_op jit(solution)/shard_map/image_far/ppermute | solution.py:22
  14.8 26.1 %collective-permute-start.1 = (bf16[128,1024]{1,0:T(8,128)(2,1)}, bf16[128,1024]{1,0:T(8,128)(2,1)S(1)}, u32[]{:S(2)}, u32[]{:S(2)}) collective-permute-start(bf16[128,1024]{1,0:T(8,128)(2,1)} %own.7), channel_id=1, source_target_pairs={{0,510},{1,511},{2,0},{3,1},{4,2},{5,3},{6,4},{7,5},{8,6},{9,7},{1... | collective-permute-start | bytes 786440 | tf_op jit(solution)/shard_map/image_near/ppermute | solution.py:22
  19.5 1.2 copy-start.1
  22.2 2.0 %copy-start = (bf16[2048,1024]{1,0:T(8,128)(2,1)}, bf16[2048,1024]{1,0:T(8,128)(2,1)S(1)}, u32[]{:S(2)}) copy-start(bf16[2048,1024]{1,0:T(8,128)(2,1)S(1)} %feats.1) | copy-start | bytes 12582916
  24.2 7.6 %copy-start.2 = (bf16[128,1024]{1,0:T(8,128)(2,1)S(1)}, bf16[128,1024]{1,0:T(8,128)(2,1)}, u32[]{:S(2)}) copy-start(bf16[128,1024]{1,0:T(8,128)(2,1)} %refs_0_.3) | copy-start | bytes 786436
  24.2 34.0 %copy-start.3 = (bf16[128,1024]{1,0:T(8,128)(2,1)S(1)}, bf16[128,1024]{1,0:T(8,128)(2,1)}, u32[]{:S(2)}) copy-start(bf16[128,1024]{1,0:T(8,128)(2,1)} %own.7) | copy-start | bytes 786436
  24.2 34.1 %copy-start.5 = (s32[128]{0:T(128)S(1)}, s32[128]{0:T(128)}, u32[]{:S(2)}) copy-start(s32[128]{0:T(128)} %param.9) | copy-start | bytes 1540
  24.2 67.8 %all-to-all-start = ((bf16[16,128,1024]{2,1,0:T(8,128)(2,1)}), bf16[16,128,1024]{2,1,0:T(8,128)(2,1)}, u32[]{:S(2)}, u32[]{:S(2)}) async-start(bf16[16,128,1024]{2,1,0:T(8,128)(2,1)} %bitcast.14), calls=%async_computation | async-start | bytes 8388608 | tf_op jit(solution)/shard_map/feats/all_to_all | solution.py:236
  31.8 26.4 %collective-permute-start = (bf16[128,1024]{1,0:T(8,128)(2,1)S(1)}, bf16[128,1024]{1,0:T(8,128)(2,1)S(1)}, u32[]{:S(2)}, u32[]{:S(2)}) collective-permute-start(bf16[128,1024]{1,0:T(8,128)(2,1)S(1)} %copy-done.2), channel_id=1, source_target_pairs={{0,1},{1,0},{2,3},{3,2},{4,5},{5,4},{6,7},{7,6},{8,9},{9,8},{10,11... | collective-permute-start | bytes 786440 | tf_op jit(solution)/shard_map/core_swap/ppermute | solution.py:30
  33.8 24.4 %collective-permute-start.4 = (bf16[64,1024]{1,0:T(8,128)(2,1)S(1)}, bf16[64,1024]{1,0:T(8,128)(2,1)S(1)}, u32[]{:S(2)}, u32[]{:S(2)}) collective-permute-start(bf16[64,1024]{1,0:T(8,128)(2,1)S(1)} %slice.9), channel_id=1, source_target_pairs={{0,2},{1,3},{2,4},{3,5},{4,6},{5,7},{6,8},{7,9},{8,10},{9,11},{10,... | collective-permute-start | bytes 393224 | tf_op jit(solution)/shard_map/image_relay_far/ppermute | solution.py:22
  41.0 17.3 %collective-permute-start.2 = (bf16[64,1024]{1,0:T(8,128)(2,1)S(1)}, bf16[64,1024]{1,0:T(8,128)(2,1)S(1)}, u32[]{:S(2)}, u32[]{:S(2)}) collective-permute-start(bf16[64,1024]{1,0:T(8,128)(2,1)S(1)} %slice.8), channel_id=1, source_target_pairs={{0,510},{1,511},{2,0},{3,1},{4,2},{5,3},{6,4},{7,5},{8,6},{9,7},{1... | collective-permute-start | bytes 393224 | tf_op jit(solution)/shard_map/image_relay_near/ppermute | solution.py:22
  52.1 25.8 %collective-permute-start.7 = (bf16[128,1024]{1,0:T(8,128)(2,1)S(1)}, bf16[128,1024]{1,0:T(8,128)(2,1)S(1)}, u32[]{:S(2)}, u32[]{:S(2)}) collective-permute-start(bf16[128,1024]{1,0:T(8,128)(2,1)S(1)} %copy-done.2), channel_id=1, source_target_pairs={{0,6},{1,7},{2,8},{3,9},{4,10},{5,11},{6,12},{7,13},{8,14},{9,15},... | collective-permute-start | bytes 786440 | tf_op jit(solution)/shard_map/report_far/ppermute | solution.py:22
  54.0 26.3 %collective-permute-start.6 = (bf16[128,1024]{1,0:T(8,128)(2,1)S(1)}, bf16[128,1024]{1,0:T(8,128)(2,1)S(1)}, u32[]{:S(2)}, u32[]{:S(2)}) collective-permute-start(bf16[128,1024]{1,0:T(8,128)(2,1)S(1)} %copy-done.2), channel_id=1, source_target_pairs={{0,2},{1,3},{2,4},{3,5},{4,6},{5,7},{6,8},{7,9},{8,10},{9,11},{10,... | collective-permute-start | bytes 786440 | tf_op jit(solution)/shard_map/report_near/ppermute | solution.py:22
  80.3 4.7 %collective-permute-start.8 = (f32[128,1024]{1,0:T(8,128)S(1)}, f32[128,1024]{1,0:T(8,128)S(1)}, u32[]{:S(2)}, u32[]{:S(2)}) collective-permute-start(f32[128,1024]{1,0:T(8,128)S(1)} %get-tuple-element.21), channel_id=1, source_target_pairs={{0,1},{1,0},{2,3},{3,2},{4,5},{5,4},{6,7},{7,6},{8,9},{9,8},{10,11... | collective-permute-start | bytes 1572872 | tf_op jit(solution)/shard_map/caption_swap/ppermute | solution.py:30
  82.2 33.7 %collective-permute-start.10 = (bf16[128,1024]{1,0:T(8,128)(2,1)S(1)}, bf16[128,1024]{1,0:T(8,128)(2,1)S(1)}, u32[]{:S(2)}, u32[]{:S(2)}) collective-permute-start(bf16[128,1024]{1,0:T(8,128)(2,1)S(1)} %collective-permute-done.6.refs_1_), channel_id=1, source_target_pairs={{0,2},{1,3},{2,4},{3,5},{4,6},{5,7},{6,8},{7,9},{8,10},{9,11},{10,... | collective-permute-start | bytes 786440 | tf_op jit(solution)/shard_map/report_relay/ppermute | solution.py:22
  87.0 30.9 %collective-permute-start.11 = (bf16[128,1024]{1,0:T(8,128)(2,1)S(1)}, bf16[128,1024]{1,0:T(8,128)(2,1)S(1)}, u32[]{:S(2)}, u32[]{:S(2)}) collective-permute-start(bf16[128,1024]{1,0:T(8,128)(2,1)S(1)} %copy-done.2), channel_id=1, source_target_pairs={{1,9},{3,11},{5,13},{7,15},{9,17},{11,19},{13,21},{15,23},{17,25},... | collective-permute-start | bytes 786440 | tf_op jit(solution)/shard_map/report_beside/ppermute | solution.py:35
  92.0 36.8 %all-to-all-start.1 = ((bf16[16,128,256]{2,1,0:T(8,128)(2,1)}), bf16[16,128,256]{2,1,0:T(8,128)(2,1)S(1)}, u32[]{:S(2)}, u32[]{:S(2)}) async-start(bf16[16,128,256]{2,1,0:T(8,128)(2,1)} %bitcast.5), calls=%async_computation.1 | async-start | bytes 2097152 | tf_op jit(solution)/shard_map/captions/all_to_all | solution.py:311
  115.9 0.7 copy-start.6
  128.7 0.7 copy-start.4
  129.4 27.8 %copy-start.7 = (bf16[128,1024]{1,0:T(8,128)(2,1)S(1)}, bf16[128,1024]{1,0:T(8,128)(2,1)}, u32[]{:S(2)}) copy-start(bf16[128,1024]{1,0:T(8,128)(2,1)} %copy-done.6) | copy-start | bytes 786436
  133.2 3.8 %collective-permute-start.13 = (f32[512,256]{1,0:T(8,128)S(1)}, f32[512,256]{1,0:T(8,128)S(1)}, u32[]{:S(2)}, u32[]{:S(2)}) collective-permute-start(f32[512,256]{1,0:T(8,128)S(1)} %get-tuple-element.32), channel_id=1, source_target_pairs={{0,1},{1,0},{2,3},{3,2},{4,5},{5,4},{6,7},{7,6},{8,9},{9,8},{10,11... | collective-permute-start | bytes 1572872 | tf_op jit(solution)/shard_map/head_swap/ppermute | solution.py:30
  137.8 38.9 %all-to-all-start.2 = ((bf16[64,8,256]{2,1,0:T(8,128)(2,1)}), bf16[64,8,256]{2,1,0:T(8,128)(2,1)S(1)}, u32[]{:S(2)}, u32[]{:S(2)}) async-start(bf16[64,8,256]{2,1,0:T(8,128)(2,1)} %fusion), calls=%async_computation.2 | async-start | bytes 524288 | tf_op jit(solution)/shard_map/head_sum/all_to_all | solution.py:323
  153.9 3.4 %collective-permute-start.9 = (bf16[128,1024]{1,0:T(8,128)(2,1)S(1)}, bf16[128,1024]{1,0:T(8,128)(2,1)S(1)}, u32[]{:S(2)}, u32[]{:S(2)}) collective-permute-start(bf16[128,1024]{1,0:T(8,128)(2,1)S(1)} %copy-done.3), channel_id=1, source_target_pairs={{0,1},{1,0},{2,3},{3,2},{4,5},{5,4},{6,7},{7,6},{8,9},{9,8},{10,11... | collective-permute-start | bytes 786440 | tf_op jit(solution)/shard_map/image_swap/ppermute | solution.py:30
  159.5 3.8 %collective-permute-start.12 = (f32[128,1024]{1,0:T(8,128)S(1)}, f32[128,1024]{1,0:T(8,128)S(1)}, u32[]{:S(2)}, u32[]{:S(2)}) collective-permute-start(f32[128,1024]{1,0:T(8,128)S(1)} %get-tuple-element.26), channel_id=1, source_target_pairs={{0,1},{1,0},{2,3},{3,2},{4,5},{5,4},{6,7},{7,6},{8,9},{9,8},{10,11... | collective-permute-start | bytes 1572872 | tf_op jit(solution)/shard_map/picture_swap/ppermute | solution.py:30
